TPU v7x, 32 devices: a whole 2x2x4 slice. The times are simulated.
32 devices in a mesh: slab: 8 (over z, x), xy: 4 (over y, core).
Axes of the slice: x: 2, y: 2, z: 4, core: 2. Of those that a mesh axis runs over, the one named last changes fastest.
Arguments:
- atom_feats: bfloat16 [2048, 16, 128], P(('slab', 'xy')), may hold values from -6 to 6
- mix_weight: bfloat16 [4, 128, 128], replicated, may hold values from -0.5 to 0.5
- gate_weight: bfloat16 [128, 384], replicated, may hold values from -0.5 to 0.5
- radial_weight: float32 [8, 512], replicated, may hold values from -2 to 2
- out_weight: float32 [128], replicated, may hold values from -0.5 to 0.5
- pair_vec: float32 [3, 8, 4096], P(None, None, ('slab', 'xy')), may hold values from -1.5 to 1.5
- nbr_atom: int32 [8, 4096], P(None, ('slab', 'xy')), may hold values from 0 to 2047, as said below
- nbr_count: int32 [4096], P(('slab', 'xy')), may hold values from 1 to 8
- target: float32 [4096], P(('slab', 'xy')), may hold values from -6 to 6
Outputs:
- density: float32 [4096], P(('slab', 'xy'))
- feat_grad: float32 [2048, 16, 128], P(('slab', 'xy'))
- mix_grad: float32 [4, 128, 128], replicated
- gate_grad: float32 [128, 384], replicated
Inputs may be any that keep to these rules, and one draw needn't show every extreme that they name: `nbr_atom`: atom numbers run domain by domain, 64 atoms each, domains in the order of the probes' slabs. Every entry of a probe's block, live or padding, names an atom of a domain in the probe's own z slab or in the z slab just below or above it (any in-plane position); one from the slab below is among the last 16 atoms of its domain, one from the slab above among the first 16.
All inputs are finite; a program needn't handle non-finite values.
Results may differ from a plain program's by a relative error of at most 0.003.
Values may be sent and summed in bfloat16 or wider, within the bound.
No kernel may reach another device: no remote copies, remote signals or barrier semaphores. Data moves between devices by JAX's collectives and lax.ppermute only.
A program may use at most 64 MiB of HBM per device.

v0:
```python
import math

import jax
import jax.numpy as jnp
import numpy as np
from jax import lax
from jax.sharding import PartitionSpec as P

DEGREE_SPANS = ((0, 1), (1, 4), (4, 9), (9, 16))
DEGREE_REPEATS = (1, 3, 5, 7)
root_three = math.sqrt(3.0)
cubic_outer = math.sqrt(10.0) / 4.0
cubic_middle = math.sqrt(15.0)
cubic_inner = math.sqrt(6.0) / 4.0


def extended_2(cells, sides, width):
    for axis, dim in sides:
        count = lax.axis_size(axis)
        ends = count - 1
        head = lax.slice_in_dim(cells, 0, width, axis=dim)
        tail = lax.slice_in_dim(cells, cells.shape[dim] - width, cells.shape[dim], axis=dim)
        cells = jnp.concatenate(
            [
                lax.ppermute(tail, axis, [(i, (i + 1) % count) for i in range(ends)]),
                cells,
                lax.ppermute(head, axis, [((i + 1) % count, i) for i in range(ends)]),
            ],
            axis=dim,
        )
    return cells


def from_behind(block, axis, distance):
    devices = range(lax.axis_size(axis))
    route = [(i - distance, i) for i in devices if i - distance in devices]
    return lax.ppermute(block, axis, route)


def harmonics(vectors):
    along_x, along_y, along_z = (vectors[0], vectors[1], vectors[2])
    radius_sq = along_x * along_x + along_y * along_y + along_z * along_z
    terms = [
        jnp.ones_like(along_x),
        along_x,
        along_y,
        along_z,
        root_three * along_x * along_y,
        root_three * along_y * along_z,
        0.5 * (3.0 * along_z * along_z - radius_sq),
        root_three * along_x * along_z,
        0.5 * root_three * (along_x * along_x - along_y * along_y),
        cubic_outer * along_y * (3.0 * along_x * along_x - along_y * along_y),
        cubic_middle * along_x * along_y * along_z,
        cubic_inner * along_y * (5.0 * along_z * along_z - radius_sq),
        0.5 * along_z * (5.0 * along_z * along_z - 3.0 * radius_sq),
        cubic_inner * along_x * (5.0 * along_z * along_z - radius_sq),
        0.5 * cubic_middle * along_z * (along_x * along_x - along_y * along_y),
        cubic_outer * along_x * (along_x * along_x - 3.0 * along_y * along_y),
    ]
    return (jnp.stack(terms, axis=0), radius_sq)


def pair_coefficient(vectors, radial_weight):
    harm_values, radius_sq = harmonics(vectors)
    nbasis = radial_weight.shape[0]
    hidden_widths = radial_weight.shape[1] // 4
    distance = jnp.sqrt(radius_sq)
    envelope = (1.0 - radius_sq / 7.0) ** 2
    centers = 0.35 * jnp.arange(nbasis, dtype=jnp.float32)
    basis = jnp.exp(-(((distance[None, :] - centers[:, None]) / 0.35) ** 2)) * envelope[None, :]
    radial = jnp.dot(basis.T, radial_weight, precision=lax.Precision.HIGHEST)
    radial = radial.reshape(radial.shape[0], 4, hidden_widths)
    expanded = jnp.repeat(radial, np.array(DEGREE_REPEATS), axis=1, total_repeat_length=16)
    return harm_values.T[:, :, None] * expanded


def silu_slope(values):
    sig = jax.nn.sigmoid(values)
    return sig * (1.0 + values * (1.0 - sig))


def atom_layer(features, mix_weight, gate_weight):
    hidden_widths = features.shape[2]
    count_atoms = features.shape[0]
    gate_pre = jnp.dot(features[:, 0, :], gate_weight, preferred_element_type=jnp.float32)
    gates = jax.nn.sigmoid(gate_pre)
    mixed = []
    updates = []
    for degree in range(4):
        start_row, end_row = DEGREE_SPANS[degree]
        block = features[:, start_row:end_row, :].reshape(-1, hidden_widths)
        product = jnp.dot(block, mix_weight[degree], preferred_element_type=jnp.float32)
        product = product.reshape(count_atoms, end_row - start_row, hidden_widths)
        mixed.append(product)
        if degree == 0:
            updates.append(jax.nn.silu(product))
        else:
            gate_block = gates[:, None, (degree - 1) * hidden_widths : degree * hidden_widths]
            updates.append(product * gate_block)
    atom_out = (features.astype(jnp.float32) + jnp.concatenate(updates, axis=1)).astype(
        jnp.bfloat16
    )
    return (atom_out, gates, mixed)


def layer_backward(features, mix_weight, gate_weight, gates, mixed, upstream):
    hidden_widths = features.shape[2]
    count_atoms = features.shape[0]
    wide = features.astype(jnp.float32)
    grad_blocks = []
    mix_grads = []
    gate_parts = []
    for degree in range(4):
        start_row, end_row = DEGREE_SPANS[degree]
        incoming = upstream[:, start_row:end_row, :]
        if degree == 0:
            d_mixed = incoming * silu_slope(mixed[0])
        else:
            gate_block = gates[:, None, (degree - 1) * hidden_widths : degree * hidden_widths]
            d_mixed = incoming * gate_block
            gate_parts.append(jnp.sum(incoming * mixed[degree], axis=1))
        flat_grad = d_mixed.reshape(-1, hidden_widths)
        flat_feat = wide[:, start_row:end_row, :].reshape(-1, hidden_widths)
        mix_grads.append(jnp.dot(flat_feat.T, flat_grad, precision=lax.Precision.HIGHEST))
        back = jnp.dot(
            flat_grad, mix_weight[degree].astype(jnp.float32).T, precision=lax.Precision.HIGHEST
        )
        grad_blocks.append(incoming + back.reshape(count_atoms, end_row - start_row, hidden_widths))
    d_gate_pre = jnp.concatenate(gate_parts, axis=1) * gates * (1.0 - gates)
    gate_grad = jnp.dot(wide[:, 0, :].T, d_gate_pre, precision=lax.Precision.HIGHEST)
    scalar_back = jnp.dot(
        d_gate_pre, gate_weight.astype(jnp.float32).T, precision=lax.Precision.HIGHEST
    )
    grad_blocks[0] = grad_blocks[0] + scalar_back[:, None, :]
    return (jnp.concatenate(grad_blocks, axis=1), jnp.stack(mix_grads, axis=0), gate_grad)


def select_table(row_ids, total_rows, dtype):
    return (row_ids[:, None] == jnp.arange(total_rows, dtype=jnp.int32)[None, :]).astype(dtype)


def probe_forward(source, coordinates, vectors, counts, radial_weight, out_weight):
    capacity_total = coordinates.shape[0]
    sampler_total = coordinates.shape[1]
    total_rows, harm_count, hidden_widths = source.shape
    flat_source = source.reshape(total_rows, harm_count * hidden_widths)

    def proceed_once(neighbor_signal, slot):
        table = select_table(coordinates[slot], total_rows, jnp.bfloat16)
        rows = jnp.dot(table, flat_source, preferred_element_type=jnp.float32)
        rows = rows.reshape(sampler_total, harm_count, hidden_widths)
        coefficient = pair_coefficient(vectors[:, slot, :], radial_weight)
        active = (slot < counts).astype(jnp.float32)
        term = jnp.sum(coefficient * rows, axis=1)
        return (neighbor_signal + active[:, None] * term, None)

    neighbor_signal, discarded_result = lax.scan(
        proceed_once,
        jnp.zeros((sampler_total, hidden_widths), jnp.float32),
        jnp.arange(capacity_total, dtype=jnp.int32),
    )
    density = jnp.dot(jax.nn.silu(neighbor_signal), out_weight, precision=lax.Precision.HIGHEST)
    return (density, neighbor_signal)


def spread_rows(table, contribution):
    flat = contribution.reshape(contribution.shape[0], -1)
    return lax.dot_general(table, flat, (((0,), (0,)), ((), ())), precision=lax.Precision.HIGHEST)


def probe_backward(derivative_input, coordinates, vectors, counts, radial_weight, d_message):
    capacity_total = coordinates.shape[0]
    total_rows = derivative_input.shape[0]
    flat_start = derivative_input.reshape(total_rows, -1)

    def proceed_once(accumulated, slot):
        coefficient = pair_coefficient(vectors[:, slot, :], radial_weight)
        active = (slot < counts).astype(jnp.float32)
        contribution = (active[:, None] * d_message)[:, None, :] * coefficient
        table = select_table(coordinates[slot], total_rows, jnp.float32)
        return (accumulated + spread_rows(table, contribution), None)

    flat_result, discarded_result = lax.scan(
        proceed_once, flat_start, jnp.arange(capacity_total, dtype=jnp.int32)
    )
    return flat_result.reshape(derivative_input.shape)


def body(
    atom_feats,
    mix_weight,
    gate_weight,
    radial_weight,
    out_weight,
    pair_vec,
    nbr_atom,
    nbr_count,
    target,
):
    atom_out, gates, mixed = atom_layer(atom_feats, mix_weight, gate_weight)
    atom_rows = atom_feats.shape[0]
    plane_count = lax.axis_size("xy")
    slab_here = lax.axis_index("slab")
    domain = nbr_atom // atom_rows
    row_in = nbr_atom % atom_rows
    slab_step = domain // plane_count - slab_here
    plane_of = domain % plane_count
    face_rows = atom_rows // 4
    extended = extended_2(atom_out, (("slab", 0),), face_rows)
    source = lax.all_gather(extended, "xy", axis=0, tiled=True)
    coordinates = (
        plane_of * (atom_rows + 2 * face_rows) + face_rows + row_in + slab_step * atom_rows
    )
    density, neighbor_signal = probe_forward(
        source, coordinates, pair_vec, nbr_count, radial_weight, out_weight
    )
    probes_dev = float(target.shape[0])
    d_density = (density - target) / probes_dev
    d_message = d_density[:, None] * out_weight[None, :] * silu_slope(neighbor_signal)
    derivative_input = probe_backward(
        jnp.zeros(source.shape, jnp.float32),
        coordinates,
        pair_vec,
        nbr_count,
        radial_weight,
        d_message,
    )
    plane_grad = lax.psum_scatter(derivative_input, "xy", scatter_dimension=0, tiled=True)
    from_above = from_behind(plane_grad[:face_rows], "slab", -1)
    from_below = from_behind(plane_grad[face_rows + atom_rows :], "slab", 1)
    owned_grad = plane_grad[face_rows : face_rows + atom_rows]
    upstream = jnp.concatenate(
        [
            owned_grad[:face_rows] + from_below,
            owned_grad[face_rows : atom_rows - face_rows],
            owned_grad[atom_rows - face_rows :] + from_above,
        ],
        axis=0,
    )
    feat_grad, mix_local, gate_local = layer_backward(
        atom_feats, mix_weight, gate_weight, gates, mixed, upstream
    )
    mix_total, gate_total = lax.psum((mix_local, gate_local), ("slab", "xy"))
    scale = 1.0 / float(lax.axis_size("slab") * plane_count)
    return (density, feat_grad, mix_total * scale, gate_total * scale)


def solution(mesh):
    in_specs = (
        P(("slab", "xy"), None, None),
        P(),
        P(),
        P(),
        P(),
        P(None, None, ("slab", "xy")),
        P(None, ("slab", "xy")),
        P(("slab", "xy")),
        P(("slab", "xy")),
    )
    out_specs = (P(("slab", "xy")), P(("slab", "xy"), None, None), P(), P())
    return jax.shard_map(body, mesh=mesh, in_specs=in_specs, out_specs=out_specs, check_vma=False)
```

profile of v0, /device:TPU:0, one launch (start us, length us, event | category | flops | bytes accessed | tf_op | source)
XLA Modules:
  0.0 496.5 jit_solution(11693360001133354124)
XLA Ops:
  11.8 1.8 broadcast_multiply_fusion.6
  13.6 1.8 broadcast_multiply_fusion.4
  16.4 4.8 collective-permute-start
  23.2 4.3 collective-permute-done.1
  28.4 20.9 %all-gather.2.cloned.1.call-done = bf16[384,16,128]{2,0,1:T(8,128)(2,1)} async-done(((bf16[96,16,128]{2,0,1:T(8,128)(2,1)}), bf16[384,16,128]{2,0,1:T(8,128)(2,1)}) %all-gather.2.cloned.1.call-update) | async-done | bytes 1572880 | tf_op jit(solution)/shard_map/all_gather | solution.py:211
  49.3 2.6 copy.54
  51.8 2.6 copy.55
  55.0 95.1 %while.30 = (s32[]{:T(128)}, f32[128,128]{1,0:T(8,128)}, s32[8]{0:T(128)}, s32[128]{0:T(128)}, f32[3,8,128]{2,1,0:T(8,128)}, /*index=5*/f32[8,512]{1,0:T(8,128)S...) while((s32[]{:T(128)}, f32[128,128]{1,0:T(8,128)}, ...), condition=%wide.region_5.7_spmd.clone.clone, body=%wide.region_1.6_spmd.clone.clone.sunk | while | flops 208500096 | bytes 12650521 | solution.py:158
  63.8 2.0 convolution_bitcast_fusion.14
  75.7 2.0 convolution_bitcast_fusion.14
  87.6 2.0 convolution_bitcast_fusion.14
  99.4 2.0 convolution_bitcast_fusion.14
  111.3 2.0 convolution_bitcast_fusion.14
  123.2 2.0 convolution_bitcast_fusion.14
  135.1 2.0 convolution_bitcast_fusion.14
  147.0 2.0 convolution_bitcast_fusion.14
  152.6 142.1 %while.31 = (s32[]{:T(128)}, f32[384,2048]{1,0:T(8,128)S(1)}, s32[8]{0:T(128)S(1)}, s32[8,128]{1,0:T(8,128)S(1)}, s32[128]{0:T(128)}, /*index=5*/f32[128,128]{1,...) while((s32[]{:T(128)}, f32[384,2048]{1,0:T(8,128)S(1)}, ...), condition=%wide.region_10.12_spmd.clone.clone, body=%wide.region_7.11_spmd.clone.clone.sunk | while | flops 1216476544 | bytes 15206397 | solution.py:184
  161.5 2.5 fusion.153
  164.1 2.6 copy.89
  166.6 3.7 select_add_fusion.5
  179.3 2.5 fusion.153
  181.8 2.6 copy.89
  184.4 3.7 select_add_fusion.5
  197.1 2.5 fusion.153
  199.6 2.6 copy.89
  202.2 3.7 select_add_fusion.5
  214.8 2.5 fusion.153
  217.4 2.6 copy.89
  219.9 3.7 select_add_fusion.5
  232.6 2.5 fusion.153
  235.1 2.6 copy.89
  237.7 3.7 select_add_fusion.5
  250.4 2.5 fusion.153
  252.9 2.6 copy.89
  255.5 3.7 select_add_fusion.5
  268.1 2.5 fusion.153
  270.7 2.6 copy.89
  273.2 3.7 select_add_fusion.5
  285.9 2.5 fusion.153
  288.4 2.6 copy.89
  291.0 3.7 select_add_fusion.5
  294.7 2.4 copy.56
  297.1 3.5 copy.57
  300.8 38.0 %reduce-scatter.2.cloned.1.call-done = f32[96,16,128]{2,0,1:T(8,128)} async-done(((f32[384,16,128]{2,0,1:T(8,128)}), f32[96,16,128]{2,0,1:T(8,128)}) %reduce-scatter.2.cloned.1.call-update) | async-done | bytes 786448 | tf_op jit(solution)/shard_map/reduce_scatter | solution.py:229
  339.7 3.4 collective-permute-start.2
  343.1 2.7 collective-permute-done.2
  349.1 5.1 %collective-permute-done.3 = f32[16,16,128]{2,0,1:T(8,128)S(1)} collective-permute-done((f32[16,16,128]{2,0,1:T(8,128)S(1)}, f32[16,16,128]{2,0,1:T(8,128)S(1)}, u32[]{:S(2)}, u32[]{:S(2)}) %collective-permute-start.3) | collective-permute-done | bytes 131104 | tf_op jit(solution)/shard_map/ppermute | solution.py:37
  360.8 125.6 %all-reduce.3.cloned.1.call-done = (f32[4,128,128]{1,2,0:T(8,128)}, f32[128,384]{0,1:T(8,128)}) async-done(((f32[4,128,128]{1,2,0:T(8,128)}, f32[128,384]{0,1:T(8,128)}), (f32[4,128,128]{1,2,0:T(8,128)}, f32[128,384]{0,1:T(8,128)})) %all-reduce.3.cloned.1.call-update) | async-done | bytes 458768 | tf_op jit(solution)/shard_map/psum | solution.py:244
  (452 shorter events, 144.3 us)
Async XLA Ops:
  7.2 2.6 copy-start
  7.2 21.2 %copy-start.24 = (s32[8,128]{1,0:T(8,128)S(1)}, s32[8,128]{1,0:T(8,128)}, u32[]{:S(2)}) copy-start(s32[8,128]{1,0:T(8,128)} %param.27) | copy-start | bytes 12292
  7.2 42.1 %all-gather.2.cloned.1.call-start = ((), (), s32[]{:S(2)}) async-start(), calls=%async_computation.1 | async-start | bytes 1966080 | tf_op jit(solution)/shard_map/all_gather | solution.py:211
  8.3 7.1 %copy-start.7 = (bf16[64,16,128]{2,0,1:T(8,128)(2,1)}, bf16[64,16,128]{2,0,1:T(8,128)(2,1)S(1)}, u32[]{:S(2)}) copy-start(bf16[64,16,128]{2,0,1:T(8,128)(2,1)S(1)} %copy.49) | copy-start | bytes 786436
  10.0 3.6 copy-start.10
  10.0 3.6 copy-start.15
  10.0 3.6 copy-start.17
  10.0 18.3 %copy-start.13 = (f32[64,128]{1,0:T(8,128)}, f32[64,128]{1,0:T(8,128)S(1)}, u32[]{:S(2)}) copy-start(f32[64,128]{1,0:T(8,128)S(1)} %get-tuple-element.552) | copy-start | bytes 98308
  16.4 6.7 %collective-permute-start = (bf16[16,16,128]{2,0,1:T(8,128)(2,1)S(1)}, bf16[16,16,128]{2,0,1:T(8,128)(2,1)S(1)}, u32[]{:S(2)}, u32[]{:S(2)}) collective-permute-start(bf16[16,16,128]{2,0,1:T(8,128)(2,1)S(1)} %get-tuple-element.549), channel_id=1, source_target_pairs={{0,4},{4,8},{8,12},{12,16},{16,20},{20,24},{24,28},{1,5},{5,9},{9,... | collective-permute-start | bytes 196616 | tf_op jit(solution)/shard_map/ppermute | solution.py:25
  21.3 6.2 %collective-permute-start.1 = (bf16[16,16,128]{2,0,1:T(8,128)(2,1)S(1)}, bf16[16,16,128]{2,0,1:T(8,128)(2,1)S(1)}, u32[]{:S(2)}, u32[]{:S(2)}) collective-permute-start(bf16[16,16,128]{2,0,1:T(8,128)(2,1)S(1)} %get-tuple-element.550), channel_id=1, source_target_pairs={{4,0},{8,4},{12,8},{16,12},{20,16},{24,20},{28,24},{5,1},{9,5},{13... | collective-permute-start | bytes 196616 | tf_op jit(solution)/shard_map/ppermute | solution.py:27
  28.2 310.5 %reduce-scatter.2.cloned.1.call-start = ((), (), s32[]{:S(2)}) async-start(), calls=%async_computation.2 | async-start | bytes 3932160 | tf_op jit(solution)/shard_map/reduce_scatter | solution.py:229
  28.4 26.6 %copy-start.6 = (f32[8,512]{1,0:T(8,128)S(1)}, f32[8,512]{1,0:T(8,128)}, u32[]{:S(2)}) copy-start(f32[8,512]{1,0:T(8,128)} %param.24) | copy-start | bytes 49156
  28.4 26.6 %copy-start.23 = (s32[16]{0:T(128)S(1)}, s32[16]{0:T(128)}, u32[]{:S(2)}) copy-start(s32[16]{0:T(128)} %constant.579) | copy-start | bytes 196
  55.0 95.1 %copy-start.25 = (f32[128]{0:T(128)S(1)}, f32[128]{0:T(128)}, u32[]{:S(2)}) copy-start(f32[128]{0:T(128)} %param.25) | copy-start | bytes 1540
  63.8 2.3 copy-start.2
  99.4 2.3 copy-start.2
  111.3 2.3 copy-start.2
  135.1 2.3 copy-start.2
  147.0 2.3 copy-start.2
  152.6 6.8 %copy-start.4 = (f32[128,128]{1,0:T(8,128)}, f32[128,128]{1,0:T(8,128)S(1)}, u32[]{:S(2)}) copy-start(f32[128,128]{1,0:T(8,128)S(1)} %get-tuple-element.812) | copy-start | bytes 196612 | tf_op jit(solution)/shard_map/while
  166.6 3.7 copy-start.5
  170.4 6.8 %copy-start.4 = (f32[128,128]{1,0:T(8,128)}, f32[128,128]{1,0:T(8,128)S(1)}, u32[]{:S(2)}) copy-start(f32[128,128]{1,0:T(8,128)S(1)} %get-tuple-element.812) | copy-start | bytes 196612 | tf_op jit(solution)/shard_map/while
  184.4 3.7 copy-start.5
  188.1 6.8 %copy-start.4 = (f32[128,128]{1,0:T(8,128)}, f32[128,128]{1,0:T(8,128)S(1)}, u32[]{:S(2)}) copy-start(f32[128,128]{1,0:T(8,128)S(1)} %get-tuple-element.812) | copy-start | bytes 196612 | tf_op jit(solution)/shard_map/while
  202.2 3.7 copy-start.5
  205.9 6.8 %copy-start.4 = (f32[128,128]{1,0:T(8,128)}, f32[128,128]{1,0:T(8,128)S(1)}, u32[]{:S(2)}) copy-start(f32[128,128]{1,0:T(8,128)S(1)} %get-tuple-element.812) | copy-start | bytes 196612 | tf_op jit(solution)/shard_map/while
  219.9 3.7 copy-start.5
  223.7 6.8 %copy-start.4 = (f32[128,128]{1,0:T(8,128)}, f32[128,128]{1,0:T(8,128)S(1)}, u32[]{:S(2)}) copy-start(f32[128,128]{1,0:T(8,128)S(1)} %get-tuple-element.812) | copy-start | bytes 196612 | tf_op jit(solution)/shard_map/while
  237.7 3.7 copy-start.5
  241.4 6.8 %copy-start.4 = (f32[128,128]{1,0:T(8,128)}, f32[128,128]{1,0:T(8,128)S(1)}, u32[]{:S(2)}) copy-start(f32[128,128]{1,0:T(8,128)S(1)} %get-tuple-element.812) | copy-start | bytes 196612 | tf_op jit(solution)/shard_map/while
  255.5 3.7 copy-start.5
  259.2 6.8 %copy-start.4 = (f32[128,128]{1,0:T(8,128)}, f32[128,128]{1,0:T(8,128)S(1)}, u32[]{:S(2)}) copy-start(f32[128,128]{1,0:T(8,128)S(1)} %get-tuple-element.812) | copy-start | bytes 196612 | tf_op jit(solution)/shard_map/while
  273.2 3.7 copy-start.5
  277.0 6.8 %copy-start.4 = (f32[128,128]{1,0:T(8,128)}, f32[128,128]{1,0:T(8,128)S(1)}, u32[]{:S(2)}) copy-start(f32[128,128]{1,0:T(8,128)S(1)} %get-tuple-element.812) | copy-start | bytes 196612 | tf_op jit(solution)/shard_map/while
  291.0 3.7 copy-start.5
  300.6 54.5 %copy-start.12 = (f32[64,5,128]{2,0,1:T(8,128)S(1)}, f32[64,5,128]{2,0,1:T(8,128)}, u32[]{:S(2)}) copy-start(f32[64,5,128]{2,0,1:T(8,128)} %get-tuple-element.557) | copy-start | bytes 491524
  300.6 54.5 %copy-start.20 = (f32[64,3,128]{2,0,1:T(8,128)S(1)}, f32[64,3,128]{2,0,1:T(8,128)}, u32[]{:S(2)}) copy-start(f32[64,3,128]{2,0,1:T(8,128)} %get-tuple-element.559) | copy-start | bytes 294916
  300.6 54.6 %copy-start.9 = (f32[64,7,128]{2,0,1:T(8,128)S(1)}, f32[64,7,128]{2,0,1:T(8,128)}, u32[]{:S(2)}) copy-start(f32[64,7,128]{2,0,1:T(8,128)} %get-tuple-element.555) | copy-start | bytes 688132
  300.7 54.6 %copy-start.11 = (f32[64,384]{1,0:T(8,128)S(1)}, f32[64,384]{1,0:T(8,128)}, u32[]{:S(2)}) copy-start(f32[64,384]{1,0:T(8,128)} %copy-done.10) | copy-start | bytes 294916
  300.7 54.8 %copy-start.8 = (bf16[64,16,128]{2,0,1:T(8,128)(2,1)S(1)}, bf16[64,16,128]{2,0,1:T(8,128)(2,1)}, u32[]{:S(2)}) copy-start(bf16[64,16,128]{2,0,1:T(8,128)(2,1)} %copy-done.7) | copy-start | bytes 786436
  300.7 55.9 %copy-start.16 = (f32[64,128]{1,0:T(8,128)S(1)}, f32[64,128]{1,0:T(8,128)}, u32[]{:S(2)}) copy-start(f32[64,128]{1,0:T(8,128)} %copy-done.15) | copy-start | bytes 98308
  300.7 56.2 %copy-start.19 = (bf16[4,128,128]{2,1,0:T(8,128)(2,1)S(1)}, bf16[4,128,128]{2,1,0:T(8,128)(2,1)}, u32[]{:S(2)}) copy-start(bf16[4,128,128]{2,1,0:T(8,128)(2,1)} %param.22) | copy-start | bytes 393220
  300.7 56.4 %copy-start.18 = (f32[64,128]{1,0:T(8,128)S(1)}, f32[64,128]{1,0:T(8,128)}, u32[]{:S(2)}) copy-start(f32[64,128]{1,0:T(8,128)} %copy-done.17) | copy-start | bytes 98308
  300.7 185.7 %all-reduce.3.cloned.1.call-start = ((), (), s32[]{:S(2)}) async-start(), calls=%async_computation.3 | async-start | bytes 917504 | tf_op jit(solution)/shard_map/psum | solution.py:244
  339.7 6.1 %collective-permute-start.2 = (f32[16,16,128]{2,0,1:T(8,128)S(1)}, f32[16,16,128]{2,0,1:T(8,128)S(1)}, u32[]{:S(2)}, u32[]{:S(2)}) collective-permute-start(f32[16,16,128]{2,0,1:T(8,128)S(1)} %slice.240), channel_id=1, source_target_pairs={{0,4},{4,8},{8,12},{12,16},{16,20},{20,24},{24,28},{1,5},{5,9},{9,... | collective-permute-start | bytes 393224 | tf_op jit(solution)/shard_map/ppermute | solution.py:37
  346.8 10.9 %copy-start.14 = (f32[64,128]{1,0:T(8,128)S(1)}, f32[64,128]{1,0:T(8,128)}, u32[]{:S(2)}) copy-start(f32[64,128]{1,0:T(8,128)} %copy-done.13) | copy-start | bytes 98308
  346.9 7.3 %collective-permute-start.3 = (f32[16,16,128]{2,0,1:T(8,128)S(1)}, f32[16,16,128]{2,0,1:T(8,128)S(1)}, u32[]{:S(2)}, u32[]{:S(2)}) collective-permute-start(f32[16,16,128]{2,0,1:T(8,128)S(1)} %get-tuple-element.548), channel_id=1, source_target_pairs={{4,0},{8,4},{12,8},{16,12},{20,16},{24,20},{28,24},{5,1},{9,5},{13... | collective-permute-start | bytes 393224 | tf_op jit(solution)/shard_map/ppermute | solution.py:37
  355.1 3.3 copy-start.22
  (20 other events, 28.6 us)
Sparse Core Ops, SparseCore 0:
  28.4 20.8 all-gather.1
  300.8 37.9 reduce-scatter.1
  359.5 126.8 all-reduce.2
where the time goes:
time: 501 us; the launch traced here: 497 us
  waiting for transfers between devices  197 us (39%)
  other arithmetic  92 us (18%)
  local copies, waits for them, and re-layouts  85.1 us (17%)
  matrix products  64.8 us (13%)
  loops' own time  32.3 us (6%)
  between operations  14.2 us (3%)
  starting transfers between devices  10.9 us (2%)
    psum x1, waiting for transfers between devices, body(): mix_total, gate_total = lax.psum((mix_local, gate_local), ('slab', 'xy'))  126 us
    reduce_scatter x1, waiting for transfers between devices, body(): lax.psum_scatter(derivative_input, 'xy', scatter_dimension=0, tiled=True)  38 us
    dot_general x8, matrix products, spread_rows(): lax.dot_general(table, flat, (((0,), (0,)), ((), ())), precision=lax.Prec...  29.6 us
    mul x16, other arithmetic, proceed_once(): contribution = (active[:, None] * d_message)[:, None, :] * coefficient  26.1 us
    gather x16, local copies, waits for them, and re-layouts, pair_coefficient(): jnp.repeat(radial, np.array(DEGREE_REPEATS), axis=1, total_repeat_length=16)  25.4 us
    all_gather x1, waiting for transfers between devices, body(): source = lax.all_gather(extended, 'xy', axis=0, tiled=True)  20.9 us
    convert_element_type x16, other arithmetic, proceed_once(): active = (slot < counts).astype(jnp.float32)  20.8 us
    mul x8, local copies, waits for them, and re-layouts, proceed_once(): contribution = (active[:, None] * d_message)[:, None, :] * coefficient  20.5 us
  transfers between devices with their start and end apart: 7, of which 7 were waited for; matrix products, arithmetic and copies ran while one was open for 0% of the time, Pallas kernels for 0%

commit v1 on v0

v1 whole, which is shorter than its diff:
```python
import functools
import math

import jax
import jax.numpy as jnp
from jax import lax
from jax.experimental import pallas as pl
from jax.experimental.pallas import tpu as pltpu
from jax.sharding import PartitionSpec as P

DEGREE_SPANS = ((0, 1), (1, 4), (4, 9), (9, 16))
DEGREE_OF = (0,) + (1,) * 3 + (2,) * 5 + (3,) * 7
HARM = 16
SPACING = 0.35
root_three = math.sqrt(3.0)
cubic_outer = math.sqrt(10.0) / 4.0
cubic_middle = math.sqrt(15.0)
cubic_inner = math.sqrt(6.0) / 4.0
VMEM_BYTES = 56 * 2**20
F32 = jnp.float32
BF16 = jnp.bfloat16


def harmonics(x, y, z):
    r2 = x * x + y * y + z * z
    terms = [
        None,
        x,
        y,
        z,
        root_three * x * y,
        root_three * y * z,
        0.5 * (3.0 * z * z - r2),
        root_three * x * z,
        0.5 * root_three * (x * x - y * y),
        cubic_outer * y * (3.0 * x * x - y * y),
        cubic_middle * x * y * z,
        cubic_inner * y * (5.0 * z * z - r2),
        0.5 * z * (5.0 * z * z - 3.0 * r2),
        cubic_inner * x * (5.0 * z * z - r2),
        0.5 * cubic_middle * z * (x * x - y * y),
        cubic_outer * x * (x * x - 3.0 * y * y),
    ]
    return terms, r2


def split_high_low(values):
    high = values.astype(BF16)
    return high, (values - high.astype(F32)).astype(BF16)


def dot_lanes(left, right):
    return lax.dot_general(left, right, (((1,), (1,)), ((), ())), preferred_element_type=F32)


def dot(left, right):
    return jnp.dot(left, right, preferred_element_type=F32)


def partner(block, axis, bit):
    count = lax.axis_size(axis)
    return lax.ppermute(block, axis, [(i, i ^ bit) for i in range(count)])


def shifted(block, axis, step):
    count = lax.axis_size(axis)
    return lax.ppermute(block, axis, [(i, i + step) for i in range(count) if 0 <= i + step < count])


class Pairs:
    def __init__(self, info, slots, atoms, face_rows, plane, me):
        def rows(first):
            return jnp.concatenate([ref[first * slots : (first + 1) * slots, :] for ref in info], axis=1)

        self.slots = slots
        self.harm, r2 = harmonics(rows(0), rows(1), rows(2))
        code = rows(3).astype(jnp.int32)
        tail = rows(4)
        slot = lax.broadcasted_iota(jnp.int32, code.shape, 0).astype(F32)
        active = (slot < tail[0:1, :]).astype(F32)
        self.target = tail[1:2, :]
        relative = (code & (plane - 1)) ^ me
        offset = code >> (plane.bit_length() - 1)
        width = jnp.where(offset < plane * atoms, atoms, 2 * face_rows)
        self.column = offset + relative * width
        envelope = (1.0 - r2 / 7.0) ** 2 * active
        self.basis_parts = (jnp.sqrt(r2), envelope)

    def radial(self, lhs_ref, out_ref, nbasis):
        distance, envelope = self.basis_parts
        values = [
            jnp.exp(-(((distance - SPACING * b) / SPACING) ** 2)) * envelope for b in range(nbasis)
        ]
        basis = jnp.concatenate(values, axis=0)
        high, low = split_high_low(basis)
        stack = jnp.concatenate([high, low, high], axis=0)
        out_ref[...] = dot(lhs_ref[...], stack)

    def table(self, k, total):
        column = self.column[k : k + 1, :]
        rows = lax.broadcasted_iota(jnp.int32, (total, column.shape[1]), 0)
        return jnp.where(rows == column, 1.0, 0.0).astype(BF16)

    def weight(self, lm, k):
        return self.harm[lm][k : k + 1, :]


def forward_kernel(slots, plane, me_ref, *refs):
    wide = refs[:plane]
    faces = refs[plane : 2 * plane]
    info = refs[2 * plane : 3 * plane]
    mix_ref, gate_ref, radial_ref, out_w_ref = refs[3 * plane : 3 * plane + 4]
    feats_ref, mixed_ref, gates_ref, msg_ref, dens_ref = refs[3 * plane + 4 : 3 * plane + 9]
    table_ref, coef_ref = refs[3 * plane + 9 :]
    atoms = wide[0].shape[1]
    edge = faces[0].shape[1]
    total = plane * (atoms + edge)
    part = mix_ref.shape[1] // 2
    for j in range(plane):
        feats_ref[:, j * atoms : (j + 1) * atoms, :] = wide[j][...]
        feats_ref[:, plane * atoms + j * edge : plane * atoms + (j + 1) * edge, :] = faces[j][...]
    gates_ref[...] = jax.nn.sigmoid(dot_lanes(gate_ref[...], feats_ref[0]))
    for lm in range(HARM):
        degree = DEGREE_OF[lm]
        both = dot_lanes(mix_ref[degree], feats_ref[lm])
        mixed, plain = both[:part], both[part:]
        mixed_ref[lm * part : (lm + 1) * part, :] = mixed
        if degree == 0:
            update = mixed * jax.nn.sigmoid(mixed)
        else:
            update = mixed * gates_ref[(degree - 1) * part : degree * part, :]
        table_ref[lm * part : (lm + 1) * part, :] = (plain + update).astype(BF16)
    pairs = Pairs(info, slots, atoms, edge // 2, plane, me_ref[0])
    nbasis = radial_ref.shape[1] // (3 * slots)
    pairs.radial(radial_ref, coef_ref, nbasis)
    message = jnp.zeros(msg_ref.shape, F32)
    for k in range(slots):
        rows = dot(table_ref[...], pairs.table(k, total))
        for degree, (start, end) in enumerate(DEGREE_SPANS):
            inner = None
            for lm in range(start, end):
                term = rows[lm * part : (lm + 1) * part]
                if lm > 0:
                    term = term * pairs.weight(lm, k)
                inner = term if inner is None else inner + term
            at = (k * 4 + degree) * part
            message = message + inner * coef_ref[at : at + part, :]
    msg_ref[...] = message
    partial = jnp.sum(message * jax.nn.sigmoid(message) * out_w_ref[...], axis=0, keepdims=True)
    dens_ref[...] = jnp.broadcast_to(partial, dens_ref.shape)


def backward_kernel(slots, plane, scale, probes_dev, me_ref, *refs):
    info = refs[:plane]
    dens = refs[plane : 2 * plane]
    feats_ref, mixed_ref, gates_ref, msg_ref, radial_ref, out_w_ref = refs[2 * plane : 2 * plane + 6]
    weight_ref, density_ref = refs[2 * plane + 6 : 2 * plane + 8]
    send_refs = refs[2 * plane + 8 : 3 * plane + 8]
    coef_ref, grad_ref = refs[3 * plane + 8 :]
    part = msg_ref.shape[0]
    total = feats_ref.shape[1]
    rows_out = send_refs[0].shape[0]
    atoms = 2 * rows_out // 3
    edge = rows_out - atoms
    probes = msg_ref.shape[1] // plane
    pairs = Pairs(info, slots, atoms, edge // 2, plane, me_ref[0])
    pairs.radial(radial_ref, coef_ref, radial_ref.shape[1] // (3 * slots))
    density = dens[0][0:1, :]
    for j in range(1, plane):
        other = dens[j][0:1, :]
        density = density + jnp.concatenate(
            [other[:, (b ^ j) * probes : ((b ^ j) + 1) * probes] for b in range(plane)], axis=1
        )
    density_ref[...] = jnp.broadcast_to(density[:, :probes], density_ref.shape)
    d_density = (density - pairs.target) * (1.0 / probes_dev)
    message = msg_ref[...]
    sig = jax.nn.sigmoid(message)
    d_message = d_density * out_w_ref[...] * (sig * (1.0 + message * (1.0 - sig)))
    for k in range(slots):
        pieces = []
        for degree, (start, end) in enumerate(DEGREE_SPANS):
            at = (k * 4 + degree) * part
            base = coef_ref[at : at + part, :] * d_message
            for lm in range(start, end):
                piece = base if lm == 0 else base * pairs.weight(lm, k)
                pieces.append(piece.astype(BF16))
        contribution = jnp.concatenate(pieces, axis=0)
        product = dot_lanes(contribution, pairs.table(k, total))
        if k == 0:
            grad_ref[...] = product
        else:
            grad_ref[...] += product
    for degree, (start, end) in enumerate(DEGREE_SPANS):
        sums = None
        gate_sum = None
        for lm in range(start, end):
            grad = grad_ref[lm * part : (lm + 1) * part, :]
            mixed = mixed_ref[lm * part : (lm + 1) * part, :]
            if degree == 0:
                s = jax.nn.sigmoid(mixed)
                d_mixed = grad * (s * (1.0 + mixed * (1.0 - s)))
            else:
                d_mixed = grad * gates_ref[(degree - 1) * part : degree * part, :]
                gate_sum = grad * mixed if gate_sum is None else gate_sum + grad * mixed
            high, low = split_high_low(d_mixed)
            product = dot(jnp.concatenate([high, low], axis=0), feats_ref[lm])
            sums = product if sums is None else sums + product
        weight_ref[degree * part : (degree + 1) * part, :] = (sums[:part] + sums[part:]) * scale
        if degree > 0:
            gates = gates_ref[(degree - 1) * part : degree * part, :]
            high, low = split_high_low(gate_sum * gates * (1.0 - gates))
            product = dot(jnp.concatenate([high, low], axis=0), feats_ref[0])
            at = (3 + degree) * part
            weight_ref[at : at + part, :] = (product[:part] + product[part:]) * scale
    turned = grad_ref[...].T
    for j in range(plane):
        send_refs[j][:atoms, :] = turned[j * atoms : (j + 1) * atoms].astype(BF16)
        at = plane * atoms + j * edge
        send_refs[j][atoms:, :] = turned[at : at + edge].astype(BF16)


def finish_kernel(plane, me_ref, *refs):
    slices = refs[:plane]
    below_ref, above_ref, feats_ref, mix_ref, gate_ref, out_ref = refs[plane:]
    atoms = feats_ref.shape[1]
    channels = feats_ref.shape[2]
    part = channels // plane
    face = below_ref.shape[1]
    per = channels // part
    me = me_ref[0]
    lane = lax.broadcasted_iota(jnp.int32, (atoms, channels), 1)
    gates = jax.nn.sigmoid(dot(feats_ref[0], gate_ref[...]))

    def slab(j, group):
        columns = slice(group * channels, (group + 1) * channels)
        own = slices[j][:atoms, columns].astype(F32)
        low = own[:face] + below_ref[j, :, columns].astype(F32)
        high = own[atoms - face :] + above_ref[j, :, columns].astype(F32)
        return jnp.concatenate([low, own[face : atoms - face], high], axis=0)

    upstream = []
    for group in range(HARM // per):
        blocks = [slab(j, group) for j in range(plane)]
        for place in range(per):
            total = None
            for j in range(plane):
                home = (me ^ j) * part
                shift = (home - place * part + channels) % channels
                moved = pltpu.roll(blocks[j], shift, 1)
                keep = jnp.where((lane >= home) & (lane < home + part), moved, 0.0)
                total = keep if total is None else total + keep
            upstream.append(total)
    gate_parts = []
    zero_row = None
    for degree, (start, end) in enumerate(DEGREE_SPANS):
        weight = mix_ref[degree]
        gate_sum = None
        for lm in range(start, end):
            mixed = dot(feats_ref[lm], weight)
            if degree == 0:
                s = jax.nn.sigmoid(mixed)
                d_mixed = upstream[lm] * (s * (1.0 + mixed * (1.0 - s)))
            else:
                d_mixed = upstream[lm] * gates[:, (degree - 1) * channels : degree * channels]
                product = upstream[lm] * mixed
                gate_sum = product if gate_sum is None else gate_sum + product
            high, low = split_high_low(d_mixed)
            back = dot_lanes(jnp.concatenate([high, low], axis=0), weight)
            result = upstream[lm] + back[:atoms] + back[atoms:]
            if degree == 0:
                zero_row = result
            else:
                out_ref[:, lm, :] = result
        if degree > 0:
            gate_parts.append(gate_sum)
    d_gate = jnp.concatenate(gate_parts, axis=1) * gates * (1.0 - gates)
    high, low = split_high_low(d_gate)
    back = dot_lanes(jnp.concatenate([high, low], axis=0), gate_ref[...])
    out_ref[:, 0, :] = zero_row + back[:atoms] + back[atoms:]


def assemble_kernel(plane, me_ref, *refs):
    pieces = refs[:plane]
    mix_ref, gate_ref = refs[plane : plane + 2]
    (joined_ref,) = refs[plane + 2 :]
    part = pieces[0].shape[0] // 7
    channels = plane * part
    for j in range(plane):
        home = pl.multiple_of((me_ref[0] ^ j) * part, part)
        for block in range(7):
            joined_ref[block, pl.ds(home, part), :] = pieces[j][block * part : (block + 1) * part, :]
    for block in range(4):
        mix_ref[block] = joined_ref[block].T
    for block in range(3):
        gate_ref[:, block * channels : (block + 1) * channels] = joined_ref[4 + block].T


def call(kernel, outs, scratch, scalars, *arrays):
    vmem = pl.BlockSpec(memory_space=pltpu.VMEM)
    return pl.pallas_call(
        kernel,
        out_shape=outs,
        in_specs=[pl.BlockSpec(memory_space=pltpu.SMEM)] + [vmem] * len(arrays),
        out_specs=jax.tree.map(lambda _: vmem, outs),
        scratch_shapes=scratch,
        compiler_params=pltpu.CompilerParams(vmem_limit_bytes=VMEM_BYTES),
    )(scalars, *arrays)


def body(
    atom_feats,
    mix_weight,
    gate_weight,
    radial_weight,
    out_weight,
    pair_vec,
    nbr_atom,
    nbr_count,
    target,
):
    atoms, harm_count, channels = atom_feats.shape
    slots, probes = nbr_atom.shape
    nbasis = radial_weight.shape[0]
    plane = lax.axis_size("xy")
    slabs = lax.axis_size("slab")
    part = channels // plane
    face = atoms // 4
    edge = 2 * face
    total = plane * (atoms + edge)
    lanes = plane * probes
    me = lax.axis_index("xy").astype(jnp.int32)
    me_arr = me[None]

    domain = nbr_atom // atoms
    row = nbr_atom % atoms
    step = domain // plane - lax.axis_index("slab")
    wide = plane * atoms
    offset = jnp.where(step == 0, row, jnp.where(step < 0, wide + row - (atoms - face), wide + face + row))
    code = offset * plane + domain % plane
    tail = jnp.concatenate(
        [nbr_count.astype(F32)[None], target[None], jnp.zeros((slots - 2, probes), F32)], axis=0
    )
    info = jnp.concatenate([pair_vec.reshape(3 * slots, probes), code.astype(F32), tail], axis=0)

    own = jnp.transpose(atom_feats, (1, 0, 2))
    from_below = shifted(own[:, atoms - face :, :], "slab", 1)
    from_above = shifted(own[:, :face, :], "slab", -1)
    faces = jnp.concatenate([from_below, from_above], axis=1)
    gathered = [(own, faces, info)]
    bits = [1 << b for b in reversed(range((plane - 1).bit_length()))]
    held = {0: (own, faces, info)}
    for bit in bits:
        for j in list(held):
            held[j ^ bit] = tuple(partner(x, "xy", bit) for x in held[j])
    pieces = [held[j] for j in range(plane)]

    first = me * part
    mix_part = lax.dynamic_slice_in_dim(mix_weight, first, part, axis=2)
    mix_part = jnp.transpose(mix_part, (0, 2, 1))
    pick = lax.broadcasted_iota(jnp.int32, (4, part, channels), 1) + first
    pick = (pick == lax.broadcasted_iota(jnp.int32, (4, part, channels), 2)).astype(BF16)
    mix_part = jnp.concatenate([mix_part, pick], axis=1)
    gate_part = lax.dynamic_slice_in_dim(gate_weight.reshape(channels, 3, channels), first, part, axis=2)
    gate_part = jnp.transpose(gate_part, (1, 2, 0)).reshape(3 * part, channels)
    radial_part = lax.dynamic_slice_in_dim(radial_weight.reshape(nbasis, 4, channels), first, part, axis=2)
    radial_part = jnp.transpose(radial_part, (1, 2, 0)).reshape(4 * part, nbasis)
    high = lax.reduce_precision(radial_part, 8, 7)
    three = jnp.stack([high, high, radial_part - high], axis=1)
    same = jnp.eye(slots, dtype=F32)
    radial_lhs = three[None, :, :, :, None] * same[:, None, None, None, :]
    radial_lhs = radial_lhs.reshape(slots * 4 * part, 3 * nbasis * slots).astype(BF16)
    out_part = lax.dynamic_slice_in_dim(out_weight, first, part)[:, None]

    infos = [p[2] for p in pieces]
    feats, mixed, gates, message, dens = call(
        functools.partial(forward_kernel, slots, plane),
        (
            jax.ShapeDtypeStruct((harm_count, total, channels), BF16),
            jax.ShapeDtypeStruct((harm_count * part, total), F32),
            jax.ShapeDtypeStruct((3 * part, total), F32),
            jax.ShapeDtypeStruct((part, lanes), F32),
            jax.ShapeDtypeStruct((8, lanes), F32),
        ),
        [
            pltpu.VMEM((harm_count * part, total), BF16),
            pltpu.VMEM((slots * 4 * part, lanes), F32),
        ],
        me_arr,
        *[p[0] for p in pieces],
        *[p[1] for p in pieces],
        *infos,
        mix_part,
        gate_part,
        radial_lhs,
        out_part,
    )
    dens_all = [dens] + [partner(dens, "xy", j) for j in range(1, plane)]

    outs = call(
        functools.partial(backward_kernel, slots, plane, 1.0 / float(slabs * plane), float(probes)),
        (
            jax.ShapeDtypeStruct((7 * part, channels), F32),
            jax.ShapeDtypeStruct((8, probes), F32),
        )
        + tuple(jax.ShapeDtypeStruct((atoms + edge, harm_count * part), BF16) for _ in range(plane)),
        [
            pltpu.VMEM((slots * 4 * part, lanes), F32),
            pltpu.VMEM((harm_count * part, total), F32),
        ],
        me_arr,
        *infos,
        *dens_all,
        feats,
        mixed,
        gates,
        message,
        radial_lhs,
        out_part,
    )
    weight, density, sends = outs[0], outs[1], list(outs[2:])

    have = {0: {j: sends[j] for j in range(plane)}}
    for bit in bits:
        fresh = {}
        for source, parts in have.items():
            fresh[source ^ bit] = {j ^ bit: partner(x, "xy", bit) for j, x in parts.items() if j & bit}
            have[source] = {j: x for j, x in parts.items() if not j & bit}
        have.update(fresh)
    slices = [have[j][0] for j in range(plane)]
    to_below = jnp.stack([s[atoms : atoms + face] for s in slices], axis=0)
    to_above = jnp.stack([s[atoms + face :] for s in slices], axis=0)
    grad_above = shifted(to_below, "slab", -1)
    grad_below = shifted(to_above, "slab", 1)
    feat_grad = call(
        functools.partial(finish_kernel, plane),
        jax.ShapeDtypeStruct((atoms, harm_count, channels), F32),
        [],
        me_arr,
        *slices,
        grad_below,
        grad_above,
        own,
        mix_weight,
        gate_weight,
    )

    for b in range((slabs - 1).bit_length()):
        weight = weight + partner(weight, "slab", 1 << b)
    columns = {0: weight}
    for bit in bits:
        for j in list(columns):
            columns[j ^ bit] = partner(columns[j], "xy", bit)
    mix_grad, gate_grad = call(
        functools.partial(assemble_kernel, plane),
        (
            jax.ShapeDtypeStruct((4, channels, channels), F32),
            jax.ShapeDtypeStruct((channels, 3 * channels), F32),
        ),
        [pltpu.VMEM((7, channels, channels), F32)],
        me_arr,
        *[columns[j] for j in range(plane)],
    )
    return (density[0], feat_grad, mix_grad, gate_grad)


def solution(mesh):
    in_specs = (
        P(("slab", "xy"), None, None),
        P(),
        P(),
        P(),
        P(),
        P(None, None, ("slab", "xy")),
        P(None, ("slab", "xy")),
        P(("slab", "xy")),
        P(("slab", "xy")),
    )
    out_specs = (P(("slab", "xy")), P(("slab", "xy"), None, None), P(), P())
    return jax.shard_map(body, mesh=mesh, in_specs=in_specs, out_specs=out_specs, check_vma=False)
```

time: 501 us -> 88.4 us (0.18)
  waiting for transfers between devices: 197 us -> 27.6 us
  other arithmetic: 92 us -> 3.26 us
  local copies, waits for them, and re-layouts: 85.1 us -> 10.6 us
  matrix products: 64.8 us -> 0 us
  loops' own time: 32.3 us -> 0 us
  starting transfers between devices: 10.9 us -> 28.9 us
  Pallas kernels: 0 us -> 16.4 us
  between operations: 14.2 us -> 1.1 us
    psum x1 -> x0, waiting for transfers between devices: 126 us -> none  [body(): mix_total, gate_total = lax.psum((mix_local, gate_local), ('slab', 'xy'))]
    dot_general x48 -> x0, matrix products: 64.8 us -> none  [the longest x8 29.6 us: spread_rows(): lax.dot_general(table, flat, (((0,), (0,)), ((), ())), precision=lax.Prec...]
    mul x100 -> x0, other arithmetic: 52 us -> none  [the longest x16 26.1 us: proceed_once(): contribution = (active[:, None] * d_message)[:, None, :] * coefficient]
    reduce_scatter x1 -> x0, waiting for transfers between devices: 38 us -> none  [body(): lax.psum_scatter(derivative_input, 'xy', scatter_dimension=0, tiled=True)]
    another operation x2 -> x0, loops' own time: 32.3 us -> none  [the longest x1 16.3 us: probe_backward(): lax.scan(proceed_once, flat_start, jnp.arange(capacity_total, dtype=jnp.i...]
    gather x16 -> x0, local copies, waits for them, and re-layouts: 25.4 us -> none  [pair_coefficient(): jnp.repeat(radial, np.array(DEGREE_REPEATS), axis=1, total_repeat_length=16)]
    all_gather x1 -> x0, waiting for transfers between devices: 20.9 us -> none  [body(): source = lax.all_gather(extended, 'xy', axis=0, tiled=True)]
    convert_element_type x17 -> x4, other arithmetic: 21.8 us -> 0.94 us  [the longest x1 0.71 us: body(): code.astype(F32)]
  transfers between devices with their start and end apart: 7 -> 26, of which waited for: 7 -> 10; matrix products, arithmetic and copies ran while one was open for 0% -> 9% of each run, Pallas kernels for 0% -> 3%
where the time goes in v1:
time: 88.4 us; the launch traced here: 87.9 us
  starting transfers between devices  28.9 us (33%)
  waiting for transfers between devices  27.6 us (31%)
  Pallas kernels  16.4 us (19%)
  local copies, waits for them, and re-layouts  10.6 us (12%)
  other arithmetic  3.26 us (4%)
  between operations  1.1 us (1%)
    ppermute x22, starting transfers between devices, partner(): return lax.ppermute(block, axis, [(i, i ^ bit) for i in range(count)])  19.4 us
    ppermute x22, waiting for transfers between devices, partner(): return lax.ppermute(block, axis, [(i, i ^ bit) for i in range(count)])  17.9 us
    pallas_call x4, Pallas kernels, call(): pl.pallas_call(kernel, out_shape=outs, in_specs=[pl.BlockSpec(memory_spac...  16.4 us
    ppermute x4, waiting for transfers between devices, shifted(): lax.ppermute(block, axis, [(i, i + step) for i in range(count) if 0 <= i...  9.72 us
    ppermute x4, starting transfers between devices, shifted(): lax.ppermute(block, axis, [(i, i + step) for i in range(count) if 0 <= i...  9.47 us
    unnamed x62, local copies, waits for them, and re-layouts  4.64 us
  transfers between devices with their start and end apart: 26, of which 10 were waited for; matrix products, arithmetic and copies ran while one was open for 9% of the time, Pallas kernels for 3%

profile of v1, /device:TPU:0, one launch (start us, length us, event | category | flops | bytes accessed | tf_op | source)
XLA Modules:
  0.0 87.9 jit_solution(17831523063618859887)
XLA Ops:
  0.7 0.7 convert_bitcast_fusion
  1.4 0.7 fusion.3
  2.1 1.4 %concatenate.9.refs_8_.refs_0_ = f32[40,128]{1,0:T(8,128)S(1)} concatenate(f32[24,128]{1,0:T(8,128)} %bitcast.58, f32[8,128]{1,0:T(8,128)S(1)} %fusion.3, f32[1,128]{1,0:T(1,128)S(1)} %convert_bitcast_fusion, f32[1,128]{1,0:T(1,128)} %bitcast.59, f32[6,128]{1,0:T(8,128)S(1)} %broadcast_in_dim.20), dimensions={0} | concatenate | bytes 40960 | tf_op jit(solution)/shard_map/concatenate | solution.py:343
  3.5 3.0 %collective-permute-start.1 = (f32[40,128]{1,0:T(8,128)S(1)}, f32[40,128]{1,0:T(8,128)S(1)}, u32[]{:S(2)}, u32[]{:S(2)}) collective-permute-start(f32[40,128]{1,0:T(8,128)S(1)} %concatenate.9.refs_8_.refs_0_), channel_id=1, source_target_pairs={{0,2},{1,3},{2,0},{3,1},{4,6},{5,7},{6,4},{7,5},{8,10},{9,11},{10,... | collective-permute-start | bytes 61448 | tf_op jit(solution)/shard_map/ppermute | solution.py:62
  6.5 1.0 %copy.33 = bf16[64,16,128]{2,0,1:T(8,128)(2,1)S(1)} copy(bf16[64,16,128]{2,1,0:T(8,128)(2,1)} %param.9) | data formatting | bytes 524288 | tf_op args[0]
  7.7 0.5 collective-permute-start.3
  8.2 3.5 %collective-permute-start.6 = (bf16[16,16,128]{2,1,0:T(8,128)(2,1)S(1)}, bf16[16,16,128]{2,1,0:T(8,128)(2,1)S(1)}, u32[]{:S(2)}, u32[]{:S(2)}) collective-permute-start(bf16[16,16,128]{2,1,0:T(8,128)(2,1)S(1)} %get-tuple-element.31), channel_id=1, source_target_pairs={{0,4},{4,8},{8,12},{12,16},{16,20},{20,24},{24,28},{1,5},{5,9},{9,... | collective-permute-start | bytes 196616 | tf_op jit(solution)/shard_map/ppermute | solution.py:67
  12.2 1.4 %collective-permute-done.6 = bf16[16,16,128]{2,1,0:T(8,128)(2,1)S(1)} collective-permute-done((bf16[16,16,128]{2,1,0:T(8,128)(2,1)S(1)}, bf16[16,16,128]{2,1,0:T(8,128)(2,1)S(1)}, u32[]{:S(2)}, u32[]{:S(2)}) %collective-permute-start.6) | collective-permute-done | bytes 65568 | tf_op jit(solution)/shard_map/ppermute | solution.py:67
  13.7 1.3 %collective-permute-start.7 = (bf16[16,16,128]{2,1,0:T(8,128)(2,1)S(1)}, bf16[16,16,128]{2,1,0:T(8,128)(2,1)S(1)}, u32[]{:S(2)}, u32[]{:S(2)}) collective-permute-start(bf16[16,16,128]{2,1,0:T(8,128)(2,1)S(1)} %get-tuple-element.30), channel_id=1, source_target_pairs={{4,0},{8,4},{12,8},{16,12},{20,16},{24,20},{28,24},{5,1},{9,5},{13... | collective-permute-start | bytes 196616 | tf_op jit(solution)/shard_map/ppermute | solution.py:67
  15.0 5.2 %collective-permute-done.7 = bf16[16,16,128]{2,1,0:T(8,128)(2,1)S(1)} collective-permute-done((bf16[16,16,128]{2,1,0:T(8,128)(2,1)S(1)}, bf16[16,16,128]{2,1,0:T(8,128)(2,1)S(1)}, u32[]{:S(2)}, u32[]{:S(2)}) %collective-permute-start.7) | collective-permute-done | bytes 65568 | tf_op jit(solution)/shard_map/ppermute | solution.py:67
  20.2 1.6 %collective-permute-start.9 = (bf16[16,32,128]{2,1,0:T(8,128)(2,1)S(1)}, bf16[16,32,128]{2,1,0:T(8,128)(2,1)S(1)}, u32[]{:S(2)}, u32[]{:S(2)}) collective-permute-start(bf16[16,32,128]{2,1,0:T(8,128)(2,1)S(1)} %constant_dynamic-update-slice_fusion.refs_4_), channel_id=1, source_target_pairs={{0,2},{1,3},{2,0},{3,1},{4,6},{5,7},{6,4},{7,5},{8,10},{9,11},{10,... | collective-permute-start | bytes 393224 | tf_op jit(solution)/shard_map/ppermute | solution.py:62
  22.1 0.6 pad_maximum_fusion.refs_12_
  22.9 0.6 collective-permute-start.8
  23.4 1.8 %collective-permute-done.9.refs_6_ = bf16[16,32,128]{2,1,0:T(8,128)(2,1)S(1)} collective-permute-done((bf16[16,32,128]{2,1,0:T(8,128)(2,1)S(1)}, bf16[16,32,128]{2,1,0:T(8,128)(2,1)S(1)}, u32[]{:S(2)}, u32[]{:S(2)}) %collective-permute-start.9) | collective-permute-done | bytes 131104 | tf_op jit(solution)/shard_map/ppermute | solution.py:62
  25.2 0.6 constant_dynamic-slice_fusion.1
  25.9 0.5 collective-permute-start.2
  26.4 0.7 copy.23.refs_15_.refs_13_
  27.2 1.0 %copy.22.refs_14_.refs_12_ = bf16[1024,192]{1,0:T(8,128)(2,1)} copy(bf16[1024,192]{0,1:T(8,128)(2,1)S(1)} %bitcast.53) | data formatting | bytes 786432 | tf_op jit(solution)/shard_map/convert_element_type | solution.py:371
  28.3 0.5 copy-done.21
  29.1 5.7 %shard_map.120 = (bf16[16,384,128]{2,1,0:T(8,128)(2,1)}, f32[512,384]{1,0:T(8,128)}, f32[96,384]{1,0:T(8,128)}, f32[32,512]{1,0:T(8,128)}, f32[8,512]{1,0:T(8,128)}) custom-call(s32[1]{0:T(128)} %bitcast.me_ref, bf16[16,64,128]{2,1,0:T(8,128)(2,1)} %bitcast.50, bf16[16,64,128]{2,1,0:T(8,128)(2,1)} %copy-done.7, bf16[16,64,128]{2,1,0:T(8,128)(2,1)} %copy-done.6, ...), custom_call_target="tpu_custom_call" | custom-call | tf_op jit(solution)/shard_map/pallas_call | solution.py:300
  34.8 1.1 %collective-permute-start.13 = (f32[8,512]{1,0:T(8,128)}, f32[8,512]{1,0:T(8,128)S(1)}, u32[]{:S(2)}, u32[]{:S(2)}) collective-permute-start(f32[8,512]{1,0:T(8,128)} %get-tuple-element.17.refs_4_), channel_id=1, source_target_pairs={{0,3},{1,2},{2,1},{3,0},{4,7},{5,6},{6,5},{7,4},{8,11},{9,10},{10,... | collective-permute-start | bytes 49160 | tf_op jit(solution)/shard_map/ppermute | solution.py:62
  35.9 0.5 collective-permute-start.12
  36.7 1.5 %collective-permute-done.13.refs_7_ = f32[8,512]{1,0:T(8,128)S(1)} collective-permute-done((f32[8,512]{1,0:T(8,128)}, f32[8,512]{1,0:T(8,128)S(1)}, u32[]{:S(2)}, u32[]{:S(2)}) %collective-permute-start.13) | collective-permute-done | bytes 16416 | tf_op jit(solution)/shard_map/ppermute | solution.py:62
  38.2 1.7 %collective-permute-done.12.refs_6_ = f32[8,512]{1,0:T(8,128)S(1)} collective-permute-done((f32[8,512]{1,0:T(8,128)}, f32[8,512]{1,0:T(8,128)S(1)}, u32[]{:S(2)}, u32[]{:S(2)}) %collective-permute-start.12) | collective-permute-done | bytes 16416 | tf_op jit(solution)/shard_map/ppermute | solution.py:62
  39.9 0.6 copy-done.25
  40.5 5.8 %shard_map.121 = (f32[224,128]{1,0:T(8,128)}, f32[8,128]{1,0:T(8,128)}, bf16[96,512]{1,0:T(8,128)(2,1)}, bf16[96,512]{1,0:T(8,128)(2,1)}, bf16[96,512]{1,0:T(8,128)(2,1)}, /*index=5*/bf16[96,512]{1,0:T(8,128)(2,1)}) custom-call(s32[1]{0:T(128)} %bitcast.me_ref, f32[40,128]{1,0:T(8,128)} %copy-done.9, f32[40,128]{1,0:T(8,128)} %copy-done.20, ...), custom_call_target="tpu_custom_call" | custom-call | tf_op jit(solution)/shard_map/pallas_call | solution.py:300
  46.3 0.7 slice_bitcast_fusion.6
  47.1 0.5 collective-permute-start.15
  47.6 1.5 %collective-permute-start.16 = (bf16[96,512]{1,0:T(8,128)(2,1)}, bf16[96,512]{1,0:T(8,128)(2,1)S(1)}, u32[]{:S(2)}, u32[]{:S(2)}) collective-permute-start(bf16[96,512]{1,0:T(8,128)(2,1)} %get-tuple-element.26), channel_id=1, source_target_pairs={{0,2},{1,3},{2,0},{3,1},{4,6},{5,7},{6,4},{7,5},{8,10},{9,11},{10,... | collective-permute-start | bytes 294920 | tf_op jit(solution)/shard_map/ppermute | solution.py:62
  49.1 2.9 %collective-permute-start.20 = (f32[224,128]{1,0:T(8,128)}, f32[224,128]{1,0:T(8,128)S(1)}, u32[]{:S(2)}, u32[]{:S(2)}) collective-permute-start(f32[224,128]{1,0:T(8,128)} %get-tuple-element.27), channel_id=1, source_target_pairs={{0,4},{4,0},{8,12},{12,8},{16,20},{20,16},{24,28},{28,24},{1,5},{5... | collective-permute-start | bytes 344072 | tf_op jit(solution)/shard_map/ppermute | solution.py:62
  52.0 2.6 %collective-permute-done.16 = bf16[96,512]{1,0:T(8,128)(2,1)S(1)} collective-permute-done((bf16[96,512]{1,0:T(8,128)(2,1)}, bf16[96,512]{1,0:T(8,128)(2,1)S(1)}, u32[]{:S(2)}, u32[]{:S(2)}) %collective-permute-start.16) | collective-permute-done | bytes 98336 | tf_op jit(solution)/shard_map/ppermute | solution.py:62
  54.6 0.9 collective-permute-done.20
  55.5 0.9 %add.56 = f32[224,128]{1,0:T(8,128)S(1)} add(f32[224,128]{1,0:T(8,128)} %get-tuple-element.27, f32[224,128]{1,0:T(8,128)S(1)} %collective-permute-done.20) | non-fusion elementwise | flops 28672 | bytes 344064 | tf_op jit(solution)/shard_map/add | solution.py:448
  56.4 2.2 %collective-permute-start.21 = (f32[224,128]{1,0:T(8,128)S(1)}, f32[224,128]{1,0:T(8,128)S(1)}, u32[]{:S(2)}, u32[]{:S(2)}) collective-permute-start(f32[224,128]{1,0:T(8,128)S(1)} %add.56), channel_id=1, source_target_pairs={{0,8},{4,12},{8,0},{12,4},{16,24},{20,28},{24,16},{28,20},{1,9},{5... | collective-permute-start | bytes 344072 | tf_op jit(solution)/shard_map/ppermute | solution.py:62
  58.6 3.8 %collective-permute-done.21 = f32[224,128]{1,0:T(8,128)S(1)} collective-permute-done((f32[224,128]{1,0:T(8,128)S(1)}, f32[224,128]{1,0:T(8,128)S(1)}, u32[]{:S(2)}, u32[]{:S(2)}) %collective-permute-start.21) | collective-permute-done | bytes 114720 | tf_op jit(solution)/shard_map/ppermute | solution.py:62
  62.4 2.8 %collective-permute-start.22 = (f32[224,128]{1,0:T(8,128)S(1)}, f32[224,128]{1,0:T(8,128)S(1)}, u32[]{:S(2)}, u32[]{:S(2)}) collective-permute-start(f32[224,128]{1,0:T(8,128)S(1)} %add.57), channel_id=1, source_target_pairs={{0,16},{4,20},{8,24},{12,28},{16,0},{20,4},{24,8},{28,12},{1,17},{... | collective-permute-start | bytes 344072 | tf_op jit(solution)/shard_map/ppermute | solution.py:62
  65.2 5.6 %collective-permute-done.22 = f32[224,128]{1,0:T(8,128)S(1)} collective-permute-done((f32[224,128]{1,0:T(8,128)S(1)}, f32[224,128]{1,0:T(8,128)S(1)}, u32[]{:S(2)}, u32[]{:S(2)}) %collective-permute-start.22) | collective-permute-done | bytes 114720 | tf_op jit(solution)/shard_map/ppermute | solution.py:62
  70.8 0.6 collective-permute-start.24
  71.4 3.4 %collective-permute-start.18 = (bf16[4,16,512]{2,1,0:T(8,128)(2,1)S(1)}, bf16[4,16,512]{2,1,0:T(8,128)(2,1)S(1)}, u32[]{:S(2)}, u32[]{:S(2)}) collective-permute-start(bf16[4,16,512]{2,1,0:T(8,128)(2,1)S(1)} %pad_maximum_fusion.1), channel_id=1, source_target_pairs={{0,4},{4,8},{8,12},{12,16},{16,20},{20,24},{24,28},{1,5},{5,9},{9,... | collective-permute-start | bytes 196616 | tf_op jit(solution)/shard_map/ppermute | solution.py:67
  74.8 1.3 %collective-permute-start.19 = (bf16[4,16,512]{2,1,0:T(8,128)(2,1)S(1)}, bf16[4,16,512]{2,1,0:T(8,128)(2,1)S(1)}, u32[]{:S(2)}, u32[]{:S(2)}) collective-permute-start(bf16[4,16,512]{2,1,0:T(8,128)(2,1)S(1)} %pad_maximum_fusion.2), channel_id=1, source_target_pairs={{4,0},{8,4},{12,8},{16,12},{20,16},{24,20},{28,24},{5,1},{9,5},{13... | collective-permute-start | bytes 196616 | tf_op jit(solution)/shard_map/ppermute | solution.py:67
  76.2 0.5 collective-permute-start.25
  76.7 1.2 %slice_bitcast_fusion.8 = f32[128]{0:T(128)} fusion(f32[8,128]{1,0:T(8,128)} %get-tuple-element.22), kind=kLoop, calls=%fused_computation.43 | loop fusion | bytes 1024 | tf_op jit(solution)/shard_map/squeeze | solution.py:463
  77.9 3.1 %collective-permute-done.19.refs_5_ = bf16[4,16,512]{2,1,0:T(8,128)(2,1)S(1)} collective-permute-done((bf16[4,16,512]{2,1,0:T(8,128)(2,1)S(1)}, bf16[4,16,512]{2,1,0:T(8,128)(2,1)S(1)}, u32[]{:S(2)}, u32[]{:S(2)}) %collective-permute-start.19) | collective-permute-done | bytes 65568 | tf_op jit(solution)/shard_map/ppermute | solution.py:67
  81.0 0.6 copy-done.23
  81.6 3.0 %shard_map.122 = f32[64,16,128]{2,1,0:T(8,128)} custom-call(s32[1]{0:T(128)} %bitcast.me_ref, bf16[96,512]{1,0:T(8,128)(2,1)} %get-tuple-element.23.refs_0_, bf16[96,512]{1,0:T(8,128)(2,1)} %copy-done.10, bf16[96,512]{1,0:T(8,128)(2,1)} %copy-done.11, bf16[96,512]{1,0:T(8,128)(2,1)} %copy-done.12, bf16[4,16,512]{2,1,0:T(8,128)(2,1)} %copy-done.22, ...), custom_call_target="tpu_custom_call" | custom-call | tf_op jit(solution)/shard_map/pallas_call | solution.py:300
  84.7 0.6 copy-done.17
  85.3 0.6 copy-done.18
  85.9 2.0 %shard_map.123 = (f32[4,128,128]{2,1,0:T(8,128)}, f32[128,384]{1,0:T(8,128)}) custom-call(s32[1]{0:T(128)} %bitcast.me_ref, f32[224,128]{1,0:T(8,128)} %copy-done.3, f32[224,128]{1,0:T(8,128)} %copy-done.17, f32[224,128]{1,0:T(8,128)} %copy-done.16, f32[224,128]{1,0:T(8,128)} %copy-done.18), custom_call_target="tpu_custom_call" | custom-call | tf_op jit(solution)/shard_map/pallas_call | solution.py:300
  (100 shorter events, 2.0 us)
Async XLA Ops:
  0.6 11.2 %copy-start = (f32[8,512]{1,0:T(8,128)S(1)}, f32[8,512]{1,0:T(8,128)}, u32[]{:S(2)}) copy-start(f32[8,512]{1,0:T(8,128)} %param.12) | copy-start | bytes 49156
  0.6 21.1 %copy-start.2 = (bf16[4,128,128]{2,1,0:T(8,128)(2,1)S(1)}, bf16[4,128,128]{2,1,0:T(8,128)(2,1)}, u32[]{:S(2)}) copy-start(bf16[4,128,128]{2,1,0:T(8,128)(2,1)} %refs_7_.1) | copy-start | bytes 393220
  0.7 22.1 %copy-start.4 = (bf16[128,384]{1,0:T(8,128)(2,1)S(1)}, bf16[128,384]{1,0:T(8,128)(2,1)}, u32[]{:S(2)}) copy-start(bf16[128,384]{1,0:T(8,128)(2,1)} %refs_8_.1) | copy-start | bytes 294916
  0.7 25.7 %copy-start.27 = (f32[128]{0:T(128)S(1)}, f32[128]{0:T(128)}, u32[]{:S(2)}) copy-start(f32[128]{0:T(128)} %param.13) | copy-start | bytes 1540
  3.5 23.7 %copy-start.9 = (f32[40,128]{1,0:T(8,128)}, f32[40,128]{1,0:T(8,128)S(1)}, u32[]{:S(2)}) copy-start(f32[40,128]{1,0:T(8,128)S(1)} %concatenate.9.refs_8_.refs_0_) | copy-start | bytes 61444
  3.5 19.3 %collective-permute-start.1 = (f32[40,128]{1,0:T(8,128)S(1)}, f32[40,128]{1,0:T(8,128)S(1)}, u32[]{:S(2)}, u32[]{:S(2)}) collective-permute-start(f32[40,128]{1,0:T(8,128)S(1)} %concatenate.9.refs_8_.refs_0_), channel_id=1, source_target_pairs={{0,2},{1,3},{2,0},{3,1},{4,6},{5,7},{6,4},{7,5},{8,10},{9,11},{10,... | collective-permute-start | bytes 61448 | tf_op jit(solution)/shard_map/ppermute | solution.py:62
  6.5 19.4 %collective-permute-start = (f32[40,128]{1,0:T(8,128)S(1)}, f32[40,128]{1,0:T(8,128)S(1)}, u32[]{:S(2)}, u32[]{:S(2)}) collective-permute-start(f32[40,128]{1,0:T(8,128)S(1)} %concatenate.9.refs_8_.refs_0_), channel_id=1, source_target_pairs={{0,1},{1,0},{2,3},{3,2},{4,5},{5,4},{6,7},{7,6},{8,9},{9,8},{10,11... | collective-permute-start | bytes 61448 | tf_op jit(solution)/shard_map/ppermute | solution.py:62
  7.5 20.7 %copy-start.1 = (bf16[64,16,128]{2,0,1:T(8,128)(2,1)}, bf16[64,16,128]{2,0,1:T(8,128)(2,1)S(1)}, u32[]{:S(2)}) copy-start(bf16[64,16,128]{2,0,1:T(8,128)(2,1)S(1)} %copy.33) | copy-start | bytes 786436
  7.6 14.4 %collective-permute-start.4 = (bf16[16,64,128]{2,1,0:T(8,128)(2,1)S(1)}, bf16[16,64,128]{2,1,0:T(8,128)(2,1)S(1)}, u32[]{:S(2)}, u32[]{:S(2)}) collective-permute-start(bf16[16,64,128]{2,1,0:T(8,128)(2,1)S(1)} %bitcast.47), channel_id=1, source_target_pairs={{0,2},{1,3},{2,0},{3,1},{4,6},{5,7},{6,4},{7,5},{8,10},{9,11},{10,... | collective-permute-start | bytes 786440 | tf_op jit(solution)/shard_map/ppermute | solution.py:62
  7.7 20.5 %collective-permute-start.3 = (bf16[16,64,128]{2,1,0:T(8,128)(2,1)S(1)}, bf16[16,64,128]{2,1,0:T(8,128)(2,1)S(1)}, u32[]{:S(2)}, u32[]{:S(2)}) collective-permute-start(bf16[16,64,128]{2,1,0:T(8,128)(2,1)S(1)} %bitcast.48), channel_id=1, source_target_pairs={{0,1},{1,0},{2,3},{3,2},{4,5},{5,4},{6,7},{7,6},{8,9},{9,8},{10,11... | collective-permute-start | bytes 786440 | tf_op jit(solution)/shard_map/ppermute | solution.py:62
  8.2 5.4 %collective-permute-start.6 = (bf16[16,16,128]{2,1,0:T(8,128)(2,1)S(1)}, bf16[16,16,128]{2,1,0:T(8,128)(2,1)S(1)}, u32[]{:S(2)}, u32[]{:S(2)}) collective-permute-start(bf16[16,16,128]{2,1,0:T(8,128)(2,1)S(1)} %get-tuple-element.31), channel_id=1, source_target_pairs={{0,4},{4,8},{8,12},{12,16},{16,20},{20,24},{24,28},{1,5},{5,9},{9,... | collective-permute-start | bytes 196616 | tf_op jit(solution)/shard_map/ppermute | solution.py:67
  13.7 6.5 %collective-permute-start.7 = (bf16[16,16,128]{2,1,0:T(8,128)(2,1)S(1)}, bf16[16,16,128]{2,1,0:T(8,128)(2,1)S(1)}, u32[]{:S(2)}, u32[]{:S(2)}) collective-permute-start(bf16[16,16,128]{2,1,0:T(8,128)(2,1)S(1)} %get-tuple-element.30), channel_id=1, source_target_pairs={{4,0},{8,4},{12,8},{16,12},{20,16},{24,20},{28,24},{5,1},{9,5},{13... | collective-permute-start | bytes 196616 | tf_op jit(solution)/shard_map/ppermute | solution.py:67
  20.2 8.1 %copy-start.5 = (bf16[16,32,128]{2,1,0:T(8,128)(2,1)}, bf16[16,32,128]{2,1,0:T(8,128)(2,1)S(1)}, u32[]{:S(2)}) copy-start(bf16[16,32,128]{2,1,0:T(8,128)(2,1)S(1)} %constant_dynamic-update-slice_fusion.refs_4_) | copy-start | bytes 393220
  20.2 5.0 %collective-permute-start.9 = (bf16[16,32,128]{2,1,0:T(8,128)(2,1)S(1)}, bf16[16,32,128]{2,1,0:T(8,128)(2,1)S(1)}, u32[]{:S(2)}, u32[]{:S(2)}) collective-permute-start(bf16[16,32,128]{2,1,0:T(8,128)(2,1)S(1)} %constant_dynamic-update-slice_fusion.refs_4_), channel_id=1, source_target_pairs={{0,2},{1,3},{2,0},{3,1},{4,6},{5,7},{6,4},{7,5},{8,10},{9,11},{10,... | collective-permute-start | bytes 393224 | tf_op jit(solution)/shard_map/ppermute | solution.py:62
  22.0 6.3 %copy-start.6 = (bf16[16,64,128]{2,1,0:T(8,128)(2,1)}, bf16[16,64,128]{2,1,0:T(8,128)(2,1)S(1)}, u32[]{:S(2)}) copy-start(bf16[16,64,128]{2,1,0:T(8,128)(2,1)S(1)} %collective-permute-done.4.refs_2_) | copy-start | bytes 786436
  22.0 6.3 %collective-permute-start.5 = (bf16[16,64,128]{2,1,0:T(8,128)(2,1)S(1)}, bf16[16,64,128]{2,1,0:T(8,128)(2,1)S(1)}, u32[]{:S(2)}, u32[]{:S(2)}) collective-permute-start(bf16[16,64,128]{2,1,0:T(8,128)(2,1)S(1)} %collective-permute-done.4.refs_2_), channel_id=1, source_target_pairs={{0,1},{1,0},{2,3},{3,2},{4,5},{5,4},{6,7},{7,6},{8,9},{9,8},{10,11... | collective-permute-start | bytes 786440 | tf_op jit(solution)/shard_map/ppermute | solution.py:62
  22.9 5.5 %copy-start.19 = (f32[40,128]{1,0:T(8,128)}, f32[40,128]{1,0:T(8,128)S(1)}, u32[]{:S(2)}) copy-start(f32[40,128]{1,0:T(8,128)S(1)} %collective-permute-done.1.refs_10_.refs_2_) | copy-start | bytes 61444
  22.9 5.4 %collective-permute-start.8 = (bf16[16,32,128]{2,1,0:T(8,128)(2,1)S(1)}, bf16[16,32,128]{2,1,0:T(8,128)(2,1)S(1)}, u32[]{:S(2)}, u32[]{:S(2)}) collective-permute-start(bf16[16,32,128]{2,1,0:T(8,128)(2,1)S(1)} %constant_dynamic-update-slice_fusion.refs_4_), channel_id=1, source_target_pairs={{0,1},{1,0},{2,3},{3,2},{4,5},{5,4},{6,7},{7,6},{8,9},{9,8},{10,11... | collective-permute-start | bytes 393224 | tf_op jit(solution)/shard_map/ppermute | solution.py:62
  25.2 3.1 %copy-start.13 = (bf16[16,32,128]{2,1,0:T(8,128)(2,1)}, bf16[16,32,128]{2,1,0:T(8,128)(2,1)S(1)}, u32[]{:S(2)}) copy-start(bf16[16,32,128]{2,1,0:T(8,128)(2,1)S(1)} %collective-permute-done.9.refs_6_) | copy-start | bytes 393220
  25.2 3.0 %collective-permute-start.10 = (bf16[16,32,128]{2,1,0:T(8,128)(2,1)S(1)}, bf16[16,32,128]{2,1,0:T(8,128)(2,1)S(1)}, u32[]{:S(2)}, u32[]{:S(2)}) collective-permute-start(bf16[16,32,128]{2,1,0:T(8,128)(2,1)S(1)} %collective-permute-done.9.refs_6_), channel_id=1, source_target_pairs={{0,1},{1,0},{2,3},{3,2},{4,5},{5,4},{6,7},{7,6},{8,9},{9,8},{10,11... | collective-permute-start | bytes 393224 | tf_op jit(solution)/shard_map/ppermute | solution.py:62
  25.9 2.5 %copy-start.20 = (f32[40,128]{1,0:T(8,128)}, f32[40,128]{1,0:T(8,128)S(1)}, u32[]{:S(2)}) copy-start(f32[40,128]{1,0:T(8,128)S(1)} %collective-permute-done.refs_9_.refs_1_) | copy-start | bytes 61444
  25.9 2.3 %collective-permute-start.2 = (f32[40,128]{1,0:T(8,128)S(1)}, f32[40,128]{1,0:T(8,128)S(1)}, u32[]{:S(2)}, u32[]{:S(2)}) collective-permute-start(f32[40,128]{1,0:T(8,128)S(1)} %collective-permute-done.1.refs_10_.refs_2_), channel_id=1, source_target_pairs={{0,1},{1,0},{2,3},{3,2},{4,5},{5,4},{6,7},{7,6},{8,9},{9,8},{10,11... | collective-permute-start | bytes 61448 | tf_op jit(solution)/shard_map/ppermute | solution.py:62
  28.2 0.7 copy-start.14
  28.2 0.8 copy-start.7
  28.3 0.8 copy-start.15
  28.3 0.8 copy-start.8
  34.8 3.4 %collective-permute-start.13 = (f32[8,512]{1,0:T(8,128)}, f32[8,512]{1,0:T(8,128)S(1)}, u32[]{:S(2)}, u32[]{:S(2)}) collective-permute-start(f32[8,512]{1,0:T(8,128)} %get-tuple-element.17.refs_4_), channel_id=1, source_target_pairs={{0,3},{1,2},{2,1},{3,0},{4,7},{5,6},{6,5},{7,4},{8,11},{9,10},{10,... | collective-permute-start | bytes 49160 | tf_op jit(solution)/shard_map/ppermute | solution.py:62
  35.9 3.9 %collective-permute-start.12 = (f32[8,512]{1,0:T(8,128)}, f32[8,512]{1,0:T(8,128)S(1)}, u32[]{:S(2)}, u32[]{:S(2)}) collective-permute-start(f32[8,512]{1,0:T(8,128)} %get-tuple-element.17.refs_4_), channel_id=1, source_target_pairs={{0,2},{1,3},{2,0},{3,1},{4,6},{5,7},{6,4},{7,5},{8,10},{9,11},{10,... | collective-permute-start | bytes 49160 | tf_op jit(solution)/shard_map/ppermute | solution.py:62
  36.5 3.4 %collective-permute-start.11 = (f32[8,512]{1,0:T(8,128)}, f32[8,512]{1,0:T(8,128)S(1)}, u32[]{:S(2)}, u32[]{:S(2)}) collective-permute-start(f32[8,512]{1,0:T(8,128)} %get-tuple-element.17.refs_4_), channel_id=1, source_target_pairs={{0,1},{1,0},{2,3},{3,2},{4,5},{5,4},{6,7},{7,6},{8,9},{9,8},{10,11... | collective-permute-start | bytes 49160 | tf_op jit(solution)/shard_map/ppermute | solution.py:62
  38.2 1.7 %copy-start.24 = (f32[8,512]{1,0:T(8,128)}, f32[8,512]{1,0:T(8,128)S(1)}, u32[]{:S(2)}) copy-start(f32[8,512]{1,0:T(8,128)S(1)} %collective-permute-done.13.refs_7_) | copy-start | bytes 49156
  46.3 5.8 %collective-permute-start.14 = (bf16[96,512]{1,0:T(8,128)(2,1)}, bf16[96,512]{1,0:T(8,128)(2,1)S(1)}, u32[]{:S(2)}, u32[]{:S(2)}) collective-permute-start(bf16[96,512]{1,0:T(8,128)(2,1)} %get-tuple-element.24), channel_id=1, source_target_pairs={{0,1},{1,0},{2,3},{3,2},{4,5},{5,4},{6,7},{7,6},{8,9},{9,8},{10,11... | collective-permute-start | bytes 294920 | tf_op jit(solution)/shard_map/ppermute | solution.py:62
  47.1 11.5 %collective-permute-start.15 = (bf16[96,512]{1,0:T(8,128)(2,1)}, bf16[96,512]{1,0:T(8,128)(2,1)S(1)}, u32[]{:S(2)}, u32[]{:S(2)}) collective-permute-start(bf16[96,512]{1,0:T(8,128)(2,1)} %get-tuple-element.25), channel_id=1, source_target_pairs={{0,2},{1,3},{2,0},{3,1},{4,6},{5,7},{6,4},{7,5},{8,10},{9,11},{10,... | collective-permute-start | bytes 294920 | tf_op jit(solution)/shard_map/ppermute | solution.py:62
  47.6 7.0 %collective-permute-start.16 = (bf16[96,512]{1,0:T(8,128)(2,1)}, bf16[96,512]{1,0:T(8,128)(2,1)S(1)}, u32[]{:S(2)}, u32[]{:S(2)}) collective-permute-start(bf16[96,512]{1,0:T(8,128)(2,1)} %get-tuple-element.26), channel_id=1, source_target_pairs={{0,2},{1,3},{2,0},{3,1},{4,6},{5,7},{6,4},{7,5},{8,10},{9,11},{10,... | collective-permute-start | bytes 294920 | tf_op jit(solution)/shard_map/ppermute | solution.py:62
  49.1 6.4 %collective-permute-start.20 = (f32[224,128]{1,0:T(8,128)}, f32[224,128]{1,0:T(8,128)S(1)}, u32[]{:S(2)}, u32[]{:S(2)}) collective-permute-start(f32[224,128]{1,0:T(8,128)} %get-tuple-element.27), channel_id=1, source_target_pairs={{0,4},{4,0},{8,12},{12,8},{16,20},{20,16},{24,28},{28,24},{1,5},{5... | collective-permute-start | bytes 344072 | tf_op jit(solution)/shard_map/ppermute | solution.py:62
  52.0 29.0 %copy-start.10 = (bf16[96,512]{1,0:T(8,128)(2,1)}, bf16[96,512]{1,0:T(8,128)(2,1)S(1)}, u32[]{:S(2)}) copy-start(bf16[96,512]{1,0:T(8,128)(2,1)S(1)} %collective-permute-done.14.refs_1_) | copy-start | bytes 294916
  54.6 10.6 %collective-permute-start.17 = (bf16[96,512]{1,0:T(8,128)(2,1)S(1)}, bf16[96,512]{1,0:T(8,128)(2,1)S(1)}, u32[]{:S(2)}, u32[]{:S(2)}) collective-permute-start(bf16[96,512]{1,0:T(8,128)(2,1)S(1)} %collective-permute-done.16), channel_id=1, source_target_pairs={{0,1},{1,0},{2,3},{3,2},{4,5},{5,4},{6,7},{7,6},{8,9},{9,8},{10,11... | collective-permute-start | bytes 294920 | tf_op jit(solution)/shard_map/ppermute | solution.py:62
  56.4 6.0 %collective-permute-start.21 = (f32[224,128]{1,0:T(8,128)S(1)}, f32[224,128]{1,0:T(8,128)S(1)}, u32[]{:S(2)}, u32[]{:S(2)}) collective-permute-start(f32[224,128]{1,0:T(8,128)S(1)} %add.56), channel_id=1, source_target_pairs={{0,8},{4,12},{8,0},{12,4},{16,24},{20,28},{24,16},{28,20},{1,9},{5... | collective-permute-start | bytes 344072 | tf_op jit(solution)/shard_map/ppermute | solution.py:62
  58.6 22.4 %copy-start.11 = (bf16[96,512]{1,0:T(8,128)(2,1)}, bf16[96,512]{1,0:T(8,128)(2,1)S(1)}, u32[]{:S(2)}) copy-start(bf16[96,512]{1,0:T(8,128)(2,1)S(1)} %collective-permute-done.15.refs_2_) | copy-start | bytes 294916
  62.4 8.4 %collective-permute-start.22 = (f32[224,128]{1,0:T(8,128)S(1)}, f32[224,128]{1,0:T(8,128)S(1)}, u32[]{:S(2)}, u32[]{:S(2)}) collective-permute-start(f32[224,128]{1,0:T(8,128)S(1)} %add.57), channel_id=1, source_target_pairs={{0,16},{4,20},{8,24},{12,28},{16,0},{20,4},{24,8},{28,12},{1,17},{... | collective-permute-start | bytes 344072 | tf_op jit(solution)/shard_map/ppermute | solution.py:62
  65.2 15.7 %copy-start.12 = (bf16[96,512]{1,0:T(8,128)(2,1)}, bf16[96,512]{1,0:T(8,128)(2,1)S(1)}, u32[]{:S(2)}) copy-start(bf16[96,512]{1,0:T(8,128)(2,1)S(1)} %collective-permute-done.17.refs_3_) | copy-start | bytes 294916
  70.8 13.8 %copy-start.3 = (f32[224,128]{1,0:T(8,128)}, f32[224,128]{1,0:T(8,128)S(1)}, u32[]{:S(2)}) copy-start(f32[224,128]{1,0:T(8,128)S(1)} %add.58.refs_0_) | copy-start | bytes 344068
  70.8 5.4 %collective-permute-start.24 = (f32[224,128]{1,0:T(8,128)S(1)}, f32[224,128]{1,0:T(8,128)S(1)}, u32[]{:S(2)}, u32[]{:S(2)}) collective-permute-start(f32[224,128]{1,0:T(8,128)S(1)} %add.58.refs_0_), channel_id=1, source_target_pairs={{0,2},{1,3},{2,0},{3,1},{4,6},{5,7},{6,4},{7,5},{8,10},{9,11},{10,... | collective-permute-start | bytes 344072 | tf_op jit(solution)/shard_map/ppermute | solution.py:62
  71.4 6.5 %collective-permute-start.18 = (bf16[4,16,512]{2,1,0:T(8,128)(2,1)S(1)}, bf16[4,16,512]{2,1,0:T(8,128)(2,1)S(1)}, u32[]{:S(2)}, u32[]{:S(2)}) collective-permute-start(bf16[4,16,512]{2,1,0:T(8,128)(2,1)S(1)} %pad_maximum_fusion.1), channel_id=1, source_target_pairs={{0,4},{4,8},{8,12},{12,16},{16,20},{20,24},{24,28},{1,5},{5,9},{9,... | collective-permute-start | bytes 196616 | tf_op jit(solution)/shard_map/ppermute | solution.py:67
  74.8 6.2 %collective-permute-start.19 = (bf16[4,16,512]{2,1,0:T(8,128)(2,1)S(1)}, bf16[4,16,512]{2,1,0:T(8,128)(2,1)S(1)}, u32[]{:S(2)}, u32[]{:S(2)}) collective-permute-start(bf16[4,16,512]{2,1,0:T(8,128)(2,1)S(1)} %pad_maximum_fusion.2), channel_id=1, source_target_pairs={{4,0},{8,4},{12,8},{16,12},{20,16},{24,20},{28,24},{5,1},{9,5},{13... | collective-permute-start | bytes 196616 | tf_op jit(solution)/shard_map/ppermute | solution.py:67
  76.1 8.5 %collective-permute-start.23 = (f32[224,128]{1,0:T(8,128)S(1)}, f32[224,128]{1,0:T(8,128)S(1)}, u32[]{:S(2)}, u32[]{:S(2)}) collective-permute-start(f32[224,128]{1,0:T(8,128)S(1)} %add.58.refs_0_), channel_id=1, source_target_pairs={{0,1},{1,0},{2,3},{3,2},{4,5},{5,4},{6,7},{7,6},{8,9},{9,8},{10,11... | collective-permute-start | bytes 344072 | tf_op jit(solution)/shard_map/ppermute | solution.py:62
  76.2 8.4 %copy-start.16 = (f32[224,128]{1,0:T(8,128)}, f32[224,128]{1,0:T(8,128)S(1)}, u32[]{:S(2)}) copy-start(f32[224,128]{1,0:T(8,128)S(1)} %collective-permute-done.24.refs_2_) | copy-start | bytes 344068
  76.2 8.4 %collective-permute-start.25 = (f32[224,128]{1,0:T(8,128)S(1)}, f32[224,128]{1,0:T(8,128)S(1)}, u32[]{:S(2)}, u32[]{:S(2)}) collective-permute-start(f32[224,128]{1,0:T(8,128)S(1)} %collective-permute-done.24.refs_2_), channel_id=1, source_target_pairs={{0,1},{1,0},{2,3},{3,2},{4,5},{5,4},{6,7},{7,6},{8,9},{9,8},{10,11... | collective-permute-start | bytes 344072 | tf_op jit(solution)/shard_map/ppermute | solution.py:62
  77.9 3.1 %copy-start.22 = (bf16[4,16,512]{2,1,0:T(8,128)(2,1)}, bf16[4,16,512]{2,1,0:T(8,128)(2,1)S(1)}, u32[]{:S(2)}) copy-start(bf16[4,16,512]{2,1,0:T(8,128)(2,1)S(1)} %collective-permute-done.18.refs_4_) | copy-start | bytes 196612
  (6 other events, 3.7 us)

commit v2 on v1

--- a/solution.py
+++ b/solution.py
@@ -16,7 +16,7 @@
 cubic_outer = math.sqrt(10.0) / 4.0
 cubic_middle = math.sqrt(15.0)
 cubic_inner = math.sqrt(6.0) / 4.0
-VMEM_BYTES = 56 * 2**20
+VMEM_BYTES = 20 * 2**20
 F32 = jnp.float32
 BF16 = jnp.bfloat16
 
@@ -346,7 +346,7 @@
     from_below = shifted(own[:, atoms - face :, :], "slab", 1)
     from_above = shifted(own[:, :face, :], "slab", -1)
     faces = jnp.concatenate([from_below, from_above], axis=1)
-    gathered = [(own, faces, info)]
+    info, _ = lax.optimization_barrier((info, from_above))
     bits = [1 << b for b in reversed(range((plane - 1).bit_length()))]
     held = {0: (own, faces, info)}
     for bit in bits:
@@ -419,14 +419,11 @@
     )
     weight, density, sends = outs[0], outs[1], list(outs[2:])
 
-    have = {0: {j: sends[j] for j in range(plane)}}
-    for bit in bits:
-        fresh = {}
-        for source, parts in have.items():
-            fresh[source ^ bit] = {j ^ bit: partner(x, "xy", bit) for j, x in parts.items() if j & bit}
-            have[source] = {j: x for j, x in parts.items() if not j & bit}
-        have.update(fresh)
-    slices = [have[j][0] for j in range(plane)]
+    steps = [1 << b for b in range((slabs - 1).bit_length())]
+    weight = weight + partner(weight, "slab", steps[0])
+
+    weight, *sends = lax.optimization_barrier((weight, *sends))
+    slices = [sends[0]] + [partner(sends[j], "xy", j) for j in range(1, plane)]
     to_below = jnp.stack([s[atoms : atoms + face] for s in slices], axis=0)
     to_above = jnp.stack([s[atoms + face :] for s in slices], axis=0)
     grad_above = shifted(to_below, "slab", -1)
@@ -444,8 +441,8 @@
         gate_weight,
     )
 
-    for b in range((slabs - 1).bit_length()):
-        weight = weight + partner(weight, "slab", 1 << b)
+    for bit in steps[1:]:
+        weight = weight + partner(weight, "slab", bit)
     columns = {0: weight}
     for bit in bits:
         for j in list(columns):

time: 88.4 us -> 67.6 us (0.76)
  local copies, waits for them, and re-layouts: 10.6 us -> 2.66 us
  Pallas kernels: 16.4 us -> 9.33 us
  waiting for transfers between devices: 27.6 us -> 24.2 us
  other arithmetic: 3.26 us -> 1.69 us
    pallas_call x4, Pallas kernels: 16.4 us -> 9.33 us  [call(): pl.pallas_call(kernel, out_shape=outs, in_specs=[pl.BlockSpec(memory_spac...]
    unnamed x62 -> x18, local copies, waits for them, and re-layouts: 4.64 us -> 1.45 us
    ppermute x4, waiting for transfers between devices: 9.72 us -> 6.78 us  [shifted(): lax.ppermute(block, axis, [(i, i + step) for i in range(count) if 0 <= i...]
    concatenate x1, local copies, waits for them, and re-layouts: 1.38 us -> 0.02 us  [body(): jnp.concatenate([pair_vec.reshape(3 * slots, probes), code.astype(F32), t...]
    add x3, other arithmetic: 0.94 us -> 0.04 us  [the longest x2 0.03 us: body(): weight = weight + partner(weight, 'slab', bit)]
    ppermute x22 -> x21, starting transfers between devices: 19.4 us -> 18.6 us  [partner(): return lax.ppermute(block, axis, [(i, i ^ bit) for i in range(count)])]
    ppermute x22 -> x21, waiting for transfers between devices: 17.9 us -> 17.4 us  [partner(): return lax.ppermute(block, axis, [(i, i ^ bit) for i in range(count)])]
  transfers between devices with their start and end apart: 26 -> 25, of which waited for: 10 -> 10; matrix products, arithmetic and copies ran while one was open for 9% -> 5% of each run, Pallas kernels for 3% -> 3%
where the time goes in v2:
time: 67.6 us; the launch traced here: 67.3 us
  starting transfers between devices  28.6 us (42%)
  waiting for transfers between devices  24.2 us (36%)
  Pallas kernels  9.33 us (14%)
  local copies, waits for them, and re-layouts  2.66 us (4%)
  other arithmetic  1.69 us (2%)
  between operations  0.95 us (1%)
    ppermute x21, starting transfers between devices, partner(): return lax.ppermute(block, axis, [(i, i ^ bit) for i in range(count)])  18.6 us
    ppermute x21, waiting for transfers between devices, partner(): return lax.ppermute(block, axis, [(i, i ^ bit) for i in range(count)])  17.4 us
    ppermute x4, starting transfers between devices, shifted(): lax.ppermute(block, axis, [(i, i + step) for i in range(count) if 0 <= i...  9.91 us
    pallas_call x4, Pallas kernels, call(): pl.pallas_call(kernel, out_shape=outs, in_specs=[pl.BlockSpec(memory_spac...  9.33 us
    ppermute x4, waiting for transfers between devices, shifted(): lax.ppermute(block, axis, [(i, i + step) for i in range(count) if 0 <= i...  6.78 us
    unnamed x18, local copies, waits for them, and re-layouts  1.45 us
  transfers between devices with their start and end apart: 25, of which 10 were waited for; matrix products, arithmetic and copies ran while one was open for 5% of the time, Pallas kernels for 3%

profile of v2, /device:TPU:0, one launch (start us, length us, event | category | flops | bytes accessed | tf_op | source)
XLA Modules:
  0.0 67.3 jit_solution(4219918213033513619)
XLA Ops:
  0.7 1.1 %copy.33 = bf16[64,16,128]{2,0,1:T(8,128)(2,1)S(1)} copy(bf16[64,16,128]{2,1,0:T(8,128)(2,1)} %param.9) | data formatting | bytes 524288 | tf_op args[0]
  1.8 3.0 %collective-permute-start.5 = (bf16[16,64,128]{2,1,0:T(8,128)(2,1)S(1)}, bf16[16,64,128]{2,1,0:T(8,128)(2,1)S(1)}, u32[]{:S(2)}, u32[]{:S(2)}) collective-permute-start(bf16[16,64,128]{2,1,0:T(8,128)(2,1)S(1)} %bitcast.47), channel_id=1, source_target_pairs={{0,2},{1,3},{2,0},{3,1},{4,6},{5,7},{6,4},{7,5},{8,10},{9,11},{10,... | collective-permute-start | bytes 786440 | tf_op jit(solution)/shard_map/ppermute | solution.py:62
  4.9 3.4 %collective-permute-start.7 = (bf16[16,16,128]{2,1,0:T(8,128)(2,1)S(1)}, bf16[16,16,128]{2,1,0:T(8,128)(2,1)S(1)}, u32[]{:S(2)}, u32[]{:S(2)}) collective-permute-start(bf16[16,16,128]{2,1,0:T(8,128)(2,1)S(1)} %get-tuple-element.42), channel_id=1, source_target_pairs={{0,4},{4,8},{8,12},{12,16},{16,20},{20,24},{24,28},{1,5},{5,9},{9,... | collective-permute-start | bytes 196616 | tf_op jit(solution)/shard_map/ppermute | solution.py:67
  8.3 1.3 %collective-permute-start = (bf16[16,16,128]{2,1,0:T(8,128)(2,1)S(1)}, bf16[16,16,128]{2,1,0:T(8,128)(2,1)S(1)}, u32[]{:S(2)}, u32[]{:S(2)}) collective-permute-start(bf16[16,16,128]{2,1,0:T(8,128)(2,1)S(1)} %get-tuple-element.43), channel_id=1, source_target_pairs={{4,0},{8,4},{12,8},{16,12},{20,16},{24,20},{28,24},{5,1},{9,5},{13... | collective-permute-start | bytes 196616 | tf_op jit(solution)/shard_map/ppermute | solution.py:67
  9.6 0.1 constant_dynamic-slice_fusion
  9.7 0.1 reshape.64
  9.8 0.1 fusion
  9.9 0.7 %fusion.3 = f32[8,128]{1,0:T(8,128)S(1)} fusion(s32[8,128]{1,0:T(8,128)} %param.15, s32[]{:T(128)S(6)} %axis_index.25), kind=kLoop, calls=%fused_computation.32 | loop fusion | flops 49152 | bytes 8196 | tf_op jit(solution)/shard_map/convert_element_type | solution.py:343
  10.6 0.2 multiply_convert_fusion
  10.8 0.7 convert_bitcast_fusion
  11.4 3.0 %collective-permute-done = bf16[16,16,128]{2,1,0:T(8,128)(2,1)S(1)} collective-permute-done((bf16[16,16,128]{2,1,0:T(8,128)(2,1)S(1)}, bf16[16,16,128]{2,1,0:T(8,128)(2,1)S(1)}, u32[]{:S(2)}, u32[]{:S(2)}) %collective-permute-start) | collective-permute-done | bytes 65568 | tf_op jit(solution)/shard_map/ppermute | solution.py:67
  14.5 0.6 collective-permute-start.9
  15.0 0.1 constant_dynamic-slice_fusion.2
  15.1 0.1 copy.26
  15.3 1.6 %collective-permute-start.2 = (f32[40,128]{1,0:T(8,128)S(1)}, f32[40,128]{1,0:T(8,128)S(1)}, u32[]{:S(2)}, u32[]{:S(2)}) collective-permute-start(f32[40,128]{1,0:T(8,128)S(1)} %concatenate.9.refs_8_.refs_0_), channel_id=1, source_target_pairs={{0,2},{1,3},{2,0},{3,1},{4,6},{5,7},{6,4},{7,5},{8,10},{9,11},{10,... | collective-permute-start | bytes 61448 | tf_op jit(solution)/shard_map/ppermute | solution.py:62
  16.9 0.1 copy.20
  17.0 0.6 collective-permute-start.1
  17.6 2.1 %collective-permute-done.2.refs_10_.refs_2_ = f32[40,128]{1,0:T(8,128)S(1)} collective-permute-done((f32[40,128]{1,0:T(8,128)S(1)}, f32[40,128]{1,0:T(8,128)S(1)}, u32[]{:S(2)}, u32[]{:S(2)}) %collective-permute-start.2) | collective-permute-done | bytes 20512 | tf_op jit(solution)/shard_map/ppermute | solution.py:62
  19.7 0.5 collective-permute-start.10
  20.2 0.1 collective-permute-start.3
  20.3 0.1 dynamic-slice_bitcast_fusion
  20.4 0.1 copy.23.refs_15_.refs_13_
  20.6 0.2 copy.22.refs_14_.refs_12_
  20.8 0.7 collective-permute-done.3.refs_11_.refs_3_
  21.4 3.5 %shard_map.120 = (bf16[16,384,128]{2,1,0:T(8,128)(2,1)S(1)}, f32[512,384]{1,0:T(8,128)S(1)}, f32[96,384]{1,0:T(8,128)S(1)}, f32[32,512]{1,0:T(8,128)S(1)}, f32[8,512]{1,0:T(8,128)S(1)}) custom-call(s32[1]{0:T(128)} %bitcast.me_ref, bf16[16,64,128]{2,1,0:T(8,128)(2,1)S(1)} %bitcast.50, bf16[16,64,128]{2,1,0:T(8,128)(2,1)S(1)} %collective-permute-done.4.refs_1_, ...), custom_call_target="tpu_custom_call" | custom-call | tf_op jit(solution)/shard_map/pallas_call | solution.py:300
  24.9 0.8 %collective-permute-start.13 = (f32[8,512]{1,0:T(8,128)S(1)}, f32[8,512]{1,0:T(8,128)S(1)}, u32[]{:S(2)}, u32[]{:S(2)}) collective-permute-start(f32[8,512]{1,0:T(8,128)S(1)} %get-tuple-element.24.refs_4_), channel_id=1, source_target_pairs={{0,3},{1,2},{2,1},{3,0},{4,7},{5,6},{6,5},{7,4},{8,11},{9,10},{10,... | collective-permute-start | bytes 49160 | tf_op jit(solution)/shard_map/ppermute | solution.py:62
  25.7 1.1 %collective-permute-start.12 = (f32[8,512]{1,0:T(8,128)S(1)}, f32[8,512]{1,0:T(8,128)S(1)}, u32[]{:S(2)}, u32[]{:S(2)}) collective-permute-start(f32[8,512]{1,0:T(8,128)S(1)} %get-tuple-element.24.refs_4_), channel_id=1, source_target_pairs={{0,2},{1,3},{2,0},{3,1},{4,6},{5,7},{6,4},{7,5},{8,10},{9,11},{10,... | collective-permute-start | bytes 49160 | tf_op jit(solution)/shard_map/ppermute | solution.py:62
  26.9 1.3 %collective-permute-done.13.refs_7_ = f32[8,512]{1,0:T(8,128)S(1)} collective-permute-done((f32[8,512]{1,0:T(8,128)S(1)}, f32[8,512]{1,0:T(8,128)S(1)}, u32[]{:S(2)}, u32[]{:S(2)}) %collective-permute-start.13) | collective-permute-done | bytes 16416 | tf_op jit(solution)/shard_map/ppermute | solution.py:62
  28.2 1.3 %collective-permute-done.12.refs_6_ = f32[8,512]{1,0:T(8,128)S(1)} collective-permute-done((f32[8,512]{1,0:T(8,128)S(1)}, f32[8,512]{1,0:T(8,128)S(1)}, u32[]{:S(2)}, u32[]{:S(2)}) %collective-permute-start.12) | collective-permute-done | bytes 16416 | tf_op jit(solution)/shard_map/ppermute | solution.py:62
  29.5 3.2 %shard_map.121 = (f32[224,128]{1,0:T(8,128)S(1)}, f32[8,128]{1,0:T(8,128)S(1)}, bf16[96,512]{1,0:T(8,128)(2,1)S(1)}, bf16[96,512]{1,0:T(8,128)(2,1)S(1)}, bf16[9...) custom-call(s32[1]{0:T(128)} %bitcast.me_ref, f32[40,128]{1,0:T(8,128)S(1)} %concatenate.9.refs_8_.refs_0_, ...), custom_call_target="tpu_custom_call" | custom-call | tf_op jit(solution)/shard_map/pallas_call | solution.py:300
  32.7 2.5 %collective-permute-start.14 = (f32[224,128]{1,0:T(8,128)S(1)}, f32[224,128]{1,0:T(8,128)S(1)}, u32[]{:S(2)}, u32[]{:S(2)}) collective-permute-start(f32[224,128]{1,0:T(8,128)S(1)} %get-tuple-element.30), channel_id=1, source_target_pairs={{0,4},{4,0},{8,12},{12,8},{16,20},{20,16},{24,28},{28,24},{1,5},{5... | collective-permute-start | bytes 344072 | tf_op jit(solution)/shard_map/ppermute | solution.py:62
  35.2 2.8 %collective-permute-done.14 = f32[224,128]{1,0:T(8,128)S(1)} collective-permute-done((f32[224,128]{1,0:T(8,128)S(1)}, f32[224,128]{1,0:T(8,128)S(1)}, u32[]{:S(2)}, u32[]{:S(2)}) %collective-permute-start.14) | collective-permute-done | bytes 114720 | tf_op jit(solution)/shard_map/ppermute | solution.py:62
  38.0 0.1 collective-permute-start.15
  38.1 1.1 %collective-permute-start.16 = (bf16[96,512]{1,0:T(8,128)(2,1)S(1)}, bf16[96,512]{1,0:T(8,128)(2,1)S(1)}, u32[]{:S(2)}, u32[]{:S(2)}) collective-permute-start(bf16[96,512]{1,0:T(8,128)(2,1)S(1)} %get-tuple-element.37), channel_id=1, source_target_pairs={{0,2},{1,3},{2,0},{3,1},{4,6},{5,7},{6,4},{7,5},{8,10},{9,11},{10,... | collective-permute-start | bytes 294920 | tf_op jit(solution)/shard_map/ppermute | solution.py:62
  39.2 0.7 %collective-permute-start.17 = (bf16[96,512]{1,0:T(8,128)(2,1)S(1)}, bf16[96,512]{1,0:T(8,128)(2,1)S(1)}, u32[]{:S(2)}, u32[]{:S(2)}) collective-permute-start(bf16[96,512]{1,0:T(8,128)(2,1)S(1)} %get-tuple-element.38), channel_id=1, source_target_pairs={{0,3},{1,2},{2,1},{3,0},{4,7},{5,6},{6,5},{7,4},{8,11},{9,10},{10,... | collective-permute-start | bytes 294920 | tf_op jit(solution)/shard_map/ppermute | solution.py:62
  39.9 1.6 %collective-permute-start.20 = (f32[224,128]{1,0:T(8,128)S(1)}, f32[224,128]{1,0:T(8,128)S(1)}, u32[]{:S(2)}, u32[]{:S(2)}) collective-permute-start(f32[224,128]{1,0:T(8,128)S(1)} %add.56), channel_id=1, source_target_pairs={{0,8},{4,12},{8,0},{12,4},{16,24},{20,28},{24,16},{28,20},{1,9},{5... | collective-permute-start | bytes 344072 | tf_op jit(solution)/shard_map/ppermute | solution.py:62
  41.5 2.2 %collective-permute-done.16.refs_2_ = bf16[96,512]{1,0:T(8,128)(2,1)S(1)} collective-permute-done((bf16[96,512]{1,0:T(8,128)(2,1)S(1)}, bf16[96,512]{1,0:T(8,128)(2,1)S(1)}, u32[]{:S(2)}, u32[]{:S(2)}) %collective-permute-start.16) | collective-permute-done | bytes 98336 | tf_op jit(solution)/shard_map/ppermute | solution.py:62
  43.7 1.6 %collective-permute-done.20 = f32[224,128]{1,0:T(8,128)S(1)} collective-permute-done((f32[224,128]{1,0:T(8,128)S(1)}, f32[224,128]{1,0:T(8,128)S(1)}, u32[]{:S(2)}, u32[]{:S(2)}) %collective-permute-start.20) | collective-permute-done | bytes 114720 | tf_op jit(solution)/shard_map/ppermute | solution.py:62
  45.3 2.7 %collective-permute-start.21 = (f32[224,128]{1,0:T(8,128)S(1)}, f32[224,128]{1,0:T(8,128)S(1)}, u32[]{:S(2)}, u32[]{:S(2)}) collective-permute-start(f32[224,128]{1,0:T(8,128)S(1)} %add.57), channel_id=1, source_target_pairs={{0,16},{4,20},{8,24},{12,28},{16,0},{20,4},{24,8},{28,12},{1,17},{... | collective-permute-start | bytes 344072 | tf_op jit(solution)/shard_map/ppermute | solution.py:62
  48.0 5.4 %collective-permute-done.21 = f32[224,128]{1,0:T(8,128)S(1)} collective-permute-done((f32[224,128]{1,0:T(8,128)S(1)}, f32[224,128]{1,0:T(8,128)S(1)}, u32[]{:S(2)}, u32[]{:S(2)}) %collective-permute-start.21) | collective-permute-done | bytes 114720 | tf_op jit(solution)/shard_map/ppermute | solution.py:62
  53.4 1.1 %collective-permute-start.23 = (f32[224,128]{1,0:T(8,128)S(1)}, f32[224,128]{1,0:T(8,128)S(1)}, u32[]{:S(2)}, u32[]{:S(2)}) collective-permute-start(f32[224,128]{1,0:T(8,128)S(1)} %add.58.refs_0_), channel_id=1, source_target_pairs={{0,2},{1,3},{2,0},{3,1},{4,6},{5,7},{6,4},{7,5},{8,10},{9,11},{10,... | collective-permute-start | bytes 344072 | tf_op jit(solution)/shard_map/ppermute | solution.py:62
  54.5 3.9 %collective-permute-start.18 = (bf16[4,16,512]{2,1,0:T(8,128)(2,1)S(1)}, bf16[4,16,512]{2,1,0:T(8,128)(2,1)S(1)}, u32[]{:S(2)}, u32[]{:S(2)}) collective-permute-start(bf16[4,16,512]{2,1,0:T(8,128)(2,1)S(1)} %pad_maximum_fusion.1), channel_id=1, source_target_pairs={{0,4},{4,8},{8,12},{12,16},{16,20},{20,24},{24,28},{1,5},{5,9},{9,... | collective-permute-start | bytes 196616 | tf_op jit(solution)/shard_map/ppermute | solution.py:67
  58.5 1.3 %collective-permute-start.19 = (bf16[4,16,512]{2,1,0:T(8,128)(2,1)S(1)}, bf16[4,16,512]{2,1,0:T(8,128)(2,1)S(1)}, u32[]{:S(2)}, u32[]{:S(2)}) collective-permute-start(bf16[4,16,512]{2,1,0:T(8,128)(2,1)S(1)} %pad_maximum_fusion.2), channel_id=1, source_target_pairs={{4,0},{8,4},{12,8},{16,12},{20,16},{24,20},{28,24},{5,1},{9,5},{13... | collective-permute-start | bytes 196616 | tf_op jit(solution)/shard_map/ppermute | solution.py:67
  59.9 0.5 collective-permute-start.24
  60.4 0.5 slice_bitcast_fusion.8
  60.9 3.8 %collective-permute-done.19.refs_5_ = bf16[4,16,512]{2,1,0:T(8,128)(2,1)S(1)} collective-permute-done((bf16[4,16,512]{2,1,0:T(8,128)(2,1)S(1)}, bf16[4,16,512]{2,1,0:T(8,128)(2,1)S(1)}, u32[]{:S(2)}, u32[]{:S(2)}) %collective-permute-start.19) | collective-permute-done | bytes 65568 | tf_op jit(solution)/shard_map/ppermute | solution.py:67
  64.6 1.7 %shard_map.122 = f32[64,16,128]{2,1,0:T(8,128)} custom-call(s32[1]{0:T(128)} %bitcast.me_ref, bf16[96,512]{1,0:T(8,128)(2,1)S(1)} %get-tuple-element.35.refs_0_, bf16[96,512]{1,0:T(8,128)(2,1)S(1)} %collective-permute-done.15.refs_1_, bf16[96,512]{1,0:T(8,128)(2,1)S(1)} %collective-permute-done.16.refs_2_, ...), custom_call_target="tpu_custom_call" | custom-call | tf_op jit(solution)/shard_map/pallas_call | solution.py:300
  66.4 0.9 %shard_map.123 = (f32[4,128,128]{2,1,0:T(8,128)}, f32[128,384]{1,0:T(8,128)}) custom-call(s32[1]{0:T(128)} %bitcast.me_ref, f32[224,128]{1,0:T(8,128)S(1)} %add.58.refs_0_, f32[224,128]{1,0:T(8,128)S(1)} %collective-permute-done.22.refs_1_, f32[224,128]{1,0:T(8,128)S(1)} %collective-permute-done.23.refs_2_, f32[224,128]{1,0:T(8,128)S(1)} %collective-permute-done.24.refs_3_), custom_call_target="tpu_custom_call" | custom-call | tf_op jit(solution)/shard_map/pallas_call | solution.py:300
  (54 shorter events, 0.4 us)
Async XLA Ops:
  0.6 9.0 %copy-start = (f32[8,512]{1,0:T(8,128)S(1)}, f32[8,512]{1,0:T(8,128)}, u32[]{:S(2)}) copy-start(f32[8,512]{1,0:T(8,128)} %param.12) | copy-start | bytes 49156
  0.6 14.4 %copy-start.1 = (bf16[4,128,128]{2,1,0:T(8,128)(2,1)S(1)}, bf16[4,128,128]{2,1,0:T(8,128)(2,1)}, u32[]{:S(2)}) copy-start(bf16[4,128,128]{2,1,0:T(8,128)(2,1)} %refs_7_.1) | copy-start | bytes 393220
  0.7 14.6 %copy-start.4 = (f32[128]{0:T(128)S(1)}, f32[128]{0:T(128)}, u32[]{:S(2)}) copy-start(f32[128]{0:T(128)} %param.17) | copy-start | bytes 1540
  0.7 14.6 %copy-start.3 = (f32[3,8,128]{2,1,0:T(8,128)S(1)}, f32[3,8,128]{2,1,0:T(8,128)}, u32[]{:S(2)}) copy-start(f32[3,8,128]{2,1,0:T(8,128)} %param.14) | copy-start | bytes 36868
  0.7 16.2 %copy-start.2 = (bf16[128,384]{1,0:T(8,128)(2,1)S(1)}, bf16[128,384]{1,0:T(8,128)(2,1)}, u32[]{:S(2)}) copy-start(bf16[128,384]{1,0:T(8,128)(2,1)} %refs_8_.1) | copy-start | bytes 294916
  0.7 19.6 %copy-start.5 = (f32[128]{0:T(128)S(1)}, f32[128]{0:T(128)}, u32[]{:S(2)}) copy-start(f32[128]{0:T(128)} %param.13) | copy-start | bytes 1540
  1.8 15.0 %collective-permute-start.5 = (bf16[16,64,128]{2,1,0:T(8,128)(2,1)S(1)}, bf16[16,64,128]{2,1,0:T(8,128)(2,1)S(1)}, u32[]{:S(2)}, u32[]{:S(2)}) collective-permute-start(bf16[16,64,128]{2,1,0:T(8,128)(2,1)S(1)} %bitcast.47), channel_id=1, source_target_pairs={{0,2},{1,3},{2,0},{3,1},{4,6},{5,7},{6,4},{7,5},{8,10},{9,11},{10,... | collective-permute-start | bytes 786440 | tf_op jit(solution)/shard_map/ppermute | solution.py:62
  4.9 16.6 %collective-permute-start.4 = (bf16[16,64,128]{2,1,0:T(8,128)(2,1)S(1)}, bf16[16,64,128]{2,1,0:T(8,128)(2,1)S(1)}, u32[]{:S(2)}, u32[]{:S(2)}) collective-permute-start(bf16[16,64,128]{2,1,0:T(8,128)(2,1)S(1)} %bitcast.48), channel_id=1, source_target_pairs={{0,1},{1,0},{2,3},{3,2},{4,5},{5,4},{6,7},{7,6},{8,9},{9,8},{10,11... | collective-permute-start | bytes 786440 | tf_op jit(solution)/shard_map/ppermute | solution.py:62
  4.9 6.5 %collective-permute-start.7 = (bf16[16,16,128]{2,1,0:T(8,128)(2,1)S(1)}, bf16[16,16,128]{2,1,0:T(8,128)(2,1)S(1)}, u32[]{:S(2)}, u32[]{:S(2)}) collective-permute-start(bf16[16,16,128]{2,1,0:T(8,128)(2,1)S(1)} %get-tuple-element.42), channel_id=1, source_target_pairs={{0,4},{4,8},{8,12},{12,16},{16,20},{20,24},{24,28},{1,5},{5,9},{9,... | collective-permute-start | bytes 196616 | tf_op jit(solution)/shard_map/ppermute | solution.py:67
  8.3 6.2 %collective-permute-start = (bf16[16,16,128]{2,1,0:T(8,128)(2,1)S(1)}, bf16[16,16,128]{2,1,0:T(8,128)(2,1)S(1)}, u32[]{:S(2)}, u32[]{:S(2)}) collective-permute-start(bf16[16,16,128]{2,1,0:T(8,128)(2,1)S(1)} %get-tuple-element.43), channel_id=1, source_target_pairs={{4,0},{8,4},{12,8},{16,12},{20,16},{24,20},{28,24},{5,1},{9,5},{13... | collective-permute-start | bytes 196616 | tf_op jit(solution)/shard_map/ppermute | solution.py:67
  14.5 5.3 %collective-permute-start.9 = (bf16[16,32,128]{2,1,0:T(8,128)(2,1)S(1)}, bf16[16,32,128]{2,1,0:T(8,128)(2,1)S(1)}, u32[]{:S(2)}, u32[]{:S(2)}) collective-permute-start(bf16[16,32,128]{2,1,0:T(8,128)(2,1)S(1)} %constant_dynamic-update-slice_fusion.refs_4_), channel_id=1, source_target_pairs={{0,2},{1,3},{2,0},{3,1},{4,6},{5,7},{6,4},{7,5},{8,10},{9,11},{10,... | collective-permute-start | bytes 393224 | tf_op jit(solution)/shard_map/ppermute | solution.py:62
  15.3 4.4 %collective-permute-start.2 = (f32[40,128]{1,0:T(8,128)S(1)}, f32[40,128]{1,0:T(8,128)S(1)}, u32[]{:S(2)}, u32[]{:S(2)}) collective-permute-start(f32[40,128]{1,0:T(8,128)S(1)} %concatenate.9.refs_8_.refs_0_), channel_id=1, source_target_pairs={{0,2},{1,3},{2,0},{3,1},{4,6},{5,7},{6,4},{7,5},{8,10},{9,11},{10,... | collective-permute-start | bytes 61448 | tf_op jit(solution)/shard_map/ppermute | solution.py:62
  16.9 4.6 %collective-permute-start.6 = (bf16[16,64,128]{2,1,0:T(8,128)(2,1)S(1)}, bf16[16,64,128]{2,1,0:T(8,128)(2,1)S(1)}, u32[]{:S(2)}, u32[]{:S(2)}) collective-permute-start(bf16[16,64,128]{2,1,0:T(8,128)(2,1)S(1)} %collective-permute-done.5.refs_2_), channel_id=1, source_target_pairs={{0,1},{1,0},{2,3},{3,2},{4,5},{5,4},{6,7},{7,6},{8,9},{9,8},{10,11... | collective-permute-start | bytes 786440 | tf_op jit(solution)/shard_map/ppermute | solution.py:62
  17.0 3.2 %collective-permute-start.1 = (f32[40,128]{1,0:T(8,128)S(1)}, f32[40,128]{1,0:T(8,128)S(1)}, u32[]{:S(2)}, u32[]{:S(2)}) collective-permute-start(f32[40,128]{1,0:T(8,128)S(1)} %concatenate.9.refs_8_.refs_0_), channel_id=1, source_target_pairs={{0,1},{1,0},{2,3},{3,2},{4,5},{5,4},{6,7},{7,6},{8,9},{9,8},{10,11... | collective-permute-start | bytes 61448 | tf_op jit(solution)/shard_map/ppermute | solution.py:62
  19.7 1.7 %collective-permute-start.8 = (bf16[16,32,128]{2,1,0:T(8,128)(2,1)S(1)}, bf16[16,32,128]{2,1,0:T(8,128)(2,1)S(1)}, u32[]{:S(2)}, u32[]{:S(2)}) collective-permute-start(bf16[16,32,128]{2,1,0:T(8,128)(2,1)S(1)} %constant_dynamic-update-slice_fusion.refs_4_), channel_id=1, source_target_pairs={{0,1},{1,0},{2,3},{3,2},{4,5},{5,4},{6,7},{7,6},{8,9},{9,8},{10,11... | collective-permute-start | bytes 393224 | tf_op jit(solution)/shard_map/ppermute | solution.py:62
  19.7 1.7 %collective-permute-start.10 = (bf16[16,32,128]{2,1,0:T(8,128)(2,1)S(1)}, bf16[16,32,128]{2,1,0:T(8,128)(2,1)S(1)}, u32[]{:S(2)}, u32[]{:S(2)}) collective-permute-start(bf16[16,32,128]{2,1,0:T(8,128)(2,1)S(1)} %collective-permute-done.9.refs_6_), channel_id=1, source_target_pairs={{0,1},{1,0},{2,3},{3,2},{4,5},{5,4},{6,7},{7,6},{8,9},{9,8},{10,11... | collective-permute-start | bytes 393224 | tf_op jit(solution)/shard_map/ppermute | solution.py:62
  20.2 1.2 %collective-permute-start.3 = (f32[40,128]{1,0:T(8,128)S(1)}, f32[40,128]{1,0:T(8,128)S(1)}, u32[]{:S(2)}, u32[]{:S(2)}) collective-permute-start(f32[40,128]{1,0:T(8,128)S(1)} %collective-permute-done.2.refs_10_.refs_2_), channel_id=1, source_target_pairs={{0,1},{1,0},{2,3},{3,2},{4,5},{5,4},{6,7},{7,6},{8,9},{9,8},{10,11... | collective-permute-start | bytes 61448 | tf_op jit(solution)/shard_map/ppermute | solution.py:62
  24.9 3.2 %collective-permute-start.13 = (f32[8,512]{1,0:T(8,128)S(1)}, f32[8,512]{1,0:T(8,128)S(1)}, u32[]{:S(2)}, u32[]{:S(2)}) collective-permute-start(f32[8,512]{1,0:T(8,128)S(1)} %get-tuple-element.24.refs_4_), channel_id=1, source_target_pairs={{0,3},{1,2},{2,1},{3,0},{4,7},{5,6},{6,5},{7,4},{8,11},{9,10},{10,... | collective-permute-start | bytes 49160 | tf_op jit(solution)/shard_map/ppermute | solution.py:62
  25.7 3.7 %collective-permute-start.12 = (f32[8,512]{1,0:T(8,128)S(1)}, f32[8,512]{1,0:T(8,128)S(1)}, u32[]{:S(2)}, u32[]{:S(2)}) collective-permute-start(f32[8,512]{1,0:T(8,128)S(1)} %get-tuple-element.24.refs_4_), channel_id=1, source_target_pairs={{0,2},{1,3},{2,0},{3,1},{4,6},{5,7},{6,4},{7,5},{8,10},{9,11},{10,... | collective-permute-start | bytes 49160 | tf_op jit(solution)/shard_map/ppermute | solution.py:62
  26.8 2.7 %collective-permute-start.11 = (f32[8,512]{1,0:T(8,128)S(1)}, f32[8,512]{1,0:T(8,128)S(1)}, u32[]{:S(2)}, u32[]{:S(2)}) collective-permute-start(f32[8,512]{1,0:T(8,128)S(1)} %get-tuple-element.24.refs_4_), channel_id=1, source_target_pairs={{0,1},{1,0},{2,3},{3,2},{4,5},{5,4},{6,7},{7,6},{8,9},{9,8},{10,11... | collective-permute-start | bytes 49160 | tf_op jit(solution)/shard_map/ppermute | solution.py:62
  32.7 5.3 %collective-permute-start.14 = (f32[224,128]{1,0:T(8,128)S(1)}, f32[224,128]{1,0:T(8,128)S(1)}, u32[]{:S(2)}, u32[]{:S(2)}) collective-permute-start(f32[224,128]{1,0:T(8,128)S(1)} %get-tuple-element.30), channel_id=1, source_target_pairs={{0,4},{4,0},{8,12},{12,8},{16,20},{20,16},{24,28},{28,24},{1,5},{5... | collective-permute-start | bytes 344072 | tf_op jit(solution)/shard_map/ppermute | solution.py:62
  38.0 3.5 %collective-permute-start.15 = (bf16[96,512]{1,0:T(8,128)(2,1)S(1)}, bf16[96,512]{1,0:T(8,128)(2,1)S(1)}, u32[]{:S(2)}, u32[]{:S(2)}) collective-permute-start(bf16[96,512]{1,0:T(8,128)(2,1)S(1)} %get-tuple-element.36), channel_id=1, source_target_pairs={{0,1},{1,0},{2,3},{3,2},{4,5},{5,4},{6,7},{7,6},{8,9},{9,8},{10,11... | collective-permute-start | bytes 294920 | tf_op jit(solution)/shard_map/ppermute | solution.py:62
  38.1 5.7 %collective-permute-start.16 = (bf16[96,512]{1,0:T(8,128)(2,1)S(1)}, bf16[96,512]{1,0:T(8,128)(2,1)S(1)}, u32[]{:S(2)}, u32[]{:S(2)}) collective-permute-start(bf16[96,512]{1,0:T(8,128)(2,1)S(1)} %get-tuple-element.37), channel_id=1, source_target_pairs={{0,2},{1,3},{2,0},{3,1},{4,6},{5,7},{6,4},{7,5},{8,10},{9,11},{10,... | collective-permute-start | bytes 294920 | tf_op jit(solution)/shard_map/ppermute | solution.py:62
  39.2 8.8 %collective-permute-start.17 = (bf16[96,512]{1,0:T(8,128)(2,1)S(1)}, bf16[96,512]{1,0:T(8,128)(2,1)S(1)}, u32[]{:S(2)}, u32[]{:S(2)}) collective-permute-start(bf16[96,512]{1,0:T(8,128)(2,1)S(1)} %get-tuple-element.38), channel_id=1, source_target_pairs={{0,3},{1,2},{2,1},{3,0},{4,7},{5,6},{6,5},{7,4},{8,11},{9,10},{10,... | collective-permute-start | bytes 294920 | tf_op jit(solution)/shard_map/ppermute | solution.py:62
  39.9 5.4 %collective-permute-start.20 = (f32[224,128]{1,0:T(8,128)S(1)}, f32[224,128]{1,0:T(8,128)S(1)}, u32[]{:S(2)}, u32[]{:S(2)}) collective-permute-start(f32[224,128]{1,0:T(8,128)S(1)} %add.56), channel_id=1, source_target_pairs={{0,8},{4,12},{8,0},{12,4},{16,24},{20,28},{24,16},{28,20},{1,9},{5... | collective-permute-start | bytes 344072 | tf_op jit(solution)/shard_map/ppermute | solution.py:62
  45.3 8.0 %collective-permute-start.21 = (f32[224,128]{1,0:T(8,128)S(1)}, f32[224,128]{1,0:T(8,128)S(1)}, u32[]{:S(2)}, u32[]{:S(2)}) collective-permute-start(f32[224,128]{1,0:T(8,128)S(1)} %add.57), channel_id=1, source_target_pairs={{0,16},{4,20},{8,24},{12,28},{16,0},{20,4},{24,8},{28,12},{1,17},{... | collective-permute-start | bytes 344072 | tf_op jit(solution)/shard_map/ppermute | solution.py:62
  53.4 6.5 %collective-permute-start.23 = (f32[224,128]{1,0:T(8,128)S(1)}, f32[224,128]{1,0:T(8,128)S(1)}, u32[]{:S(2)}, u32[]{:S(2)}) collective-permute-start(f32[224,128]{1,0:T(8,128)S(1)} %add.58.refs_0_), channel_id=1, source_target_pairs={{0,2},{1,3},{2,0},{3,1},{4,6},{5,7},{6,4},{7,5},{8,10},{9,11},{10,... | collective-permute-start | bytes 344072 | tf_op jit(solution)/shard_map/ppermute | solution.py:62
  54.5 6.3 %collective-permute-start.18 = (bf16[4,16,512]{2,1,0:T(8,128)(2,1)S(1)}, bf16[4,16,512]{2,1,0:T(8,128)(2,1)S(1)}, u32[]{:S(2)}, u32[]{:S(2)}) collective-permute-start(bf16[4,16,512]{2,1,0:T(8,128)(2,1)S(1)} %pad_maximum_fusion.1), channel_id=1, source_target_pairs={{0,4},{4,8},{8,12},{12,16},{16,20},{20,24},{24,28},{1,5},{5,9},{9,... | collective-permute-start | bytes 196616 | tf_op jit(solution)/shard_map/ppermute | solution.py:67
  58.5 6.2 %collective-permute-start.19 = (bf16[4,16,512]{2,1,0:T(8,128)(2,1)S(1)}, bf16[4,16,512]{2,1,0:T(8,128)(2,1)S(1)}, u32[]{:S(2)}, u32[]{:S(2)}) collective-permute-start(bf16[4,16,512]{2,1,0:T(8,128)(2,1)S(1)} %pad_maximum_fusion.2), channel_id=1, source_target_pairs={{4,0},{8,4},{12,8},{16,12},{20,16},{24,20},{28,24},{5,1},{9,5},{13... | collective-permute-start | bytes 196616 | tf_op jit(solution)/shard_map/ppermute | solution.py:67
  59.8 6.6 %collective-permute-start.22 = (f32[224,128]{1,0:T(8,128)S(1)}, f32[224,128]{1,0:T(8,128)S(1)}, u32[]{:S(2)}, u32[]{:S(2)}) collective-permute-start(f32[224,128]{1,0:T(8,128)S(1)} %add.58.refs_0_), channel_id=1, source_target_pairs={{0,1},{1,0},{2,3},{3,2},{4,5},{5,4},{6,7},{7,6},{8,9},{9,8},{10,11... | collective-permute-start | bytes 344072 | tf_op jit(solution)/shard_map/ppermute | solution.py:62
  59.9 6.5 %collective-permute-start.24 = (f32[224,128]{1,0:T(8,128)S(1)}, f32[224,128]{1,0:T(8,128)S(1)}, u32[]{:S(2)}, u32[]{:S(2)}) collective-permute-start(f32[224,128]{1,0:T(8,128)S(1)} %collective-permute-done.23.refs_2_), channel_id=1, source_target_pairs={{0,1},{1,0},{2,3},{3,2},{4,5},{5,4},{6,7},{7,6},{8,9},{9,8},{10,11... | collective-permute-start | bytes 344072 | tf_op jit(solution)/shard_map/ppermute | solution.py:62

commit v3 on v2

--- a/solution.py
+++ b/solution.py
@@ -19,6 +19,7 @@
 VMEM_BYTES = 20 * 2**20
 F32 = jnp.float32
 BF16 = jnp.bfloat16
+LAST_STEP = F32
 
 
 def harmonics(x, y, z):
@@ -62,56 +63,51 @@
     return lax.ppermute(block, axis, [(i, i ^ bit) for i in range(count)])
 
 
-def shifted(block, axis, step):
+def beside(block, axis, first):
     count = lax.axis_size(axis)
-    return lax.ppermute(block, axis, [(i, i + step) for i in range(count) if 0 <= i + step < count])
-
-
-class Pairs:
-    def __init__(self, info, slots, atoms, face_rows, plane, me):
-        def rows(first):
-            return jnp.concatenate([ref[first * slots : (first + 1) * slots, :] for ref in info], axis=1)
-
-        self.slots = slots
-        self.harm, r2 = harmonics(rows(0), rows(1), rows(2))
-        code = rows(3).astype(jnp.int32)
-        tail = rows(4)
-        slot = lax.broadcasted_iota(jnp.int32, code.shape, 0).astype(F32)
-        active = (slot < tail[0:1, :]).astype(F32)
-        self.target = tail[1:2, :]
-        relative = (code & (plane - 1)) ^ me
-        offset = code >> (plane.bit_length() - 1)
-        width = jnp.where(offset < plane * atoms, atoms, 2 * face_rows)
-        self.column = offset + relative * width
-        envelope = (1.0 - r2 / 7.0) ** 2 * active
-        self.basis_parts = (jnp.sqrt(r2), envelope)
-
-    def radial(self, lhs_ref, out_ref, nbasis):
-        distance, envelope = self.basis_parts
-        values = [
-            jnp.exp(-(((distance - SPACING * b) / SPACING) ** 2)) * envelope for b in range(nbasis)
-        ]
-        basis = jnp.concatenate(values, axis=0)
-        high, low = split_high_low(basis)
-        stack = jnp.concatenate([high, low, high], axis=0)
-        out_ref[...] = dot(lhs_ref[...], stack)
-
-    def table(self, k, total):
-        column = self.column[k : k + 1, :]
-        rows = lax.broadcasted_iota(jnp.int32, (total, column.shape[1]), 0)
-        return jnp.where(rows == column, 1.0, 0.0).astype(BF16)
-
-    def weight(self, lm, k):
-        return self.harm[lm][k : k + 1, :]
-
-
-def forward_kernel(slots, plane, me_ref, *refs):
+    start = 0 if first else 1
+    pairs = [(i, i + 1) for i in range(start, count - 1, 2)]
+    return lax.ppermute(block, axis, pairs + [(j, i) for i, j in pairs])
+
+
+def table(column_ref, k, total):
+    column = column_ref[k : k + 1, :]
+    rows = lax.broadcasted_iota(jnp.int32, (total, column.shape[1]), 0)
+    return jnp.where(rows == column, 1.0, 0.0).astype(BF16)
+
+
+def geometry_kernel(slots, atoms, edge, plane, place_ref, *refs):
+    info = refs[:plane]
+    lhs_ref, coef_ref, harm_ref, column_ref, target_ref = refs[plane:]
+
+    def rows(first):
+        return jnp.concatenate([ref[first * slots : (first + 1) * slots, :] for ref in info], axis=1)
+
+    harm, r2 = harmonics(rows(0), rows(1), rows(2))
+    for lm in range(1, HARM):
+        harm_ref[lm * slots : (lm + 1) * slots, :] = harm[lm]
+    harm_ref[:slots, :] = jnp.ones_like(r2)
+    code = rows(3).astype(jnp.int32)
+    tail = rows(4)
+    target_ref[...] = tail
+    slot = lax.broadcasted_iota(jnp.int32, code.shape, 0).astype(F32)
+    active = (slot < tail[0:1, :]).astype(F32)
+    relative = (code & (plane - 1)) ^ (place_ref[0] >> 1)
+    offset = code >> (plane.bit_length() - 1)
+    column_ref[...] = offset + relative * jnp.where(offset < plane * atoms, atoms, edge)
+    envelope = (1.0 - r2 / 7.0) ** 2 * active
+    distance = jnp.sqrt(r2)
+    nbasis = lhs_ref.shape[1] // (3 * slots)
+    values = [jnp.exp(-(((distance - SPACING * b) / SPACING) ** 2)) * envelope for b in range(nbasis)]
+    high, low = split_high_low(jnp.concatenate(values, axis=0))
+    coef_ref[...] = dot(lhs_ref[...], jnp.concatenate([high, low, high], axis=0))
+
+
+def forward_kernel(slots, plane, *refs):
     wide = refs[:plane]
     faces = refs[plane : 2 * plane]
-    info = refs[2 * plane : 3 * plane]
-    mix_ref, gate_ref, radial_ref, out_w_ref = refs[3 * plane : 3 * plane + 4]
-    feats_ref, mixed_ref, gates_ref, msg_ref, dens_ref = refs[3 * plane + 4 : 3 * plane + 9]
-    table_ref, coef_ref = refs[3 * plane + 9 :]
+    coef_ref, harm_ref, column_ref, mix_ref, gate_ref, out_w_ref = refs[2 * plane : 2 * plane + 6]
+    feats_ref, mixed_ref, gates_ref, msg_ref, dens_ref, source_ref = refs[2 * plane + 6 :]
     atoms = wide[0].shape[1]
     edge = faces[0].shape[1]
     total = plane * (atoms + edge)
@@ -129,19 +125,16 @@
             update = mixed * jax.nn.sigmoid(mixed)
         else:
             update = mixed * gates_ref[(degree - 1) * part : degree * part, :]
-        table_ref[lm * part : (lm + 1) * part, :] = (plain + update).astype(BF16)
-    pairs = Pairs(info, slots, atoms, edge // 2, plane, me_ref[0])
-    nbasis = radial_ref.shape[1] // (3 * slots)
-    pairs.radial(radial_ref, coef_ref, nbasis)
+        source_ref[lm * part : (lm + 1) * part, :] = (plain + update).astype(BF16)
     message = jnp.zeros(msg_ref.shape, F32)
     for k in range(slots):
-        rows = dot(table_ref[...], pairs.table(k, total))
+        rows = dot(source_ref[...], table(column_ref, k, total))
         for degree, (start, end) in enumerate(DEGREE_SPANS):
             inner = None
             for lm in range(start, end):
                 term = rows[lm * part : (lm + 1) * part]
                 if lm > 0:
-                    term = term * pairs.weight(lm, k)
+                    term = term * harm_ref[lm * slots + k : lm * slots + k + 1, :]
                 inner = term if inner is None else inner + term
             at = (k * 4 + degree) * part
             message = message + inner * coef_ref[at : at + part, :]
@@ -150,21 +143,19 @@
     dens_ref[...] = jnp.broadcast_to(partial, dens_ref.shape)
 
 
-def backward_kernel(slots, plane, scale, probes_dev, me_ref, *refs):
-    info = refs[:plane]
-    dens = refs[plane : 2 * plane]
-    feats_ref, mixed_ref, gates_ref, msg_ref, radial_ref, out_w_ref = refs[2 * plane : 2 * plane + 6]
-    weight_ref, density_ref = refs[2 * plane + 6 : 2 * plane + 8]
-    send_refs = refs[2 * plane + 8 : 3 * plane + 8]
-    coef_ref, grad_ref = refs[3 * plane + 8 :]
+def backward_kernel(slots, plane, scale, probes_dev, *refs):
+    dens = refs[:plane]
+    coef_ref, harm_ref, column_ref, target_ref, feats_ref = refs[plane : plane + 5]
+    mixed_ref, gates_ref, msg_ref, out_w_ref = refs[plane + 5 : plane + 9]
+    weight_ref, density_ref = refs[plane + 9 : plane + 11]
+    send_refs = refs[plane + 11 : -1]
+    grad_ref = refs[-1]
     part = msg_ref.shape[0]
     total = feats_ref.shape[1]
     rows_out = send_refs[0].shape[0]
     atoms = 2 * rows_out // 3
     edge = rows_out - atoms
     probes = msg_ref.shape[1] // plane
-    pairs = Pairs(info, slots, atoms, edge // 2, plane, me_ref[0])
-    pairs.radial(radial_ref, coef_ref, radial_ref.shape[1] // (3 * slots))
     density = dens[0][0:1, :]
     for j in range(1, plane):
         other = dens[j][0:1, :]
@@ -172,7 +163,7 @@
             [other[:, (b ^ j) * probes : ((b ^ j) + 1) * probes] for b in range(plane)], axis=1
         )
     density_ref[...] = jnp.broadcast_to(density[:, :probes], density_ref.shape)
-    d_density = (density - pairs.target) * (1.0 / probes_dev)
+    d_density = (density - target_ref[1:2, :]) * (1.0 / probes_dev)
     message = msg_ref[...]
     sig = jax.nn.sigmoid(message)
     d_message = d_density * out_w_ref[...] * (sig * (1.0 + message * (1.0 - sig)))
@@ -182,10 +173,10 @@
             at = (k * 4 + degree) * part
             base = coef_ref[at : at + part, :] * d_message
             for lm in range(start, end):
-                piece = base if lm == 0 else base * pairs.weight(lm, k)
+                piece = base if lm == 0 else base * harm_ref[lm * slots + k : lm * slots + k + 1, :]
                 pieces.append(piece.astype(BF16))
         contribution = jnp.concatenate(pieces, axis=0)
-        product = dot_lanes(contribution, pairs.table(k, total))
+        product = dot_lanes(contribution, table(column_ref, k, total))
         if k == 0:
             grad_ref[...] = product
         else:
@@ -214,28 +205,32 @@
             weight_ref[at : at + part, :] = (product[:part] + product[part:]) * scale
     turned = grad_ref[...].T
     for j in range(plane):
-        send_refs[j][:atoms, :] = turned[j * atoms : (j + 1) * atoms].astype(BF16)
+        send_ref = send_refs[j.bit_length()]
+        first = (j - (1 << j.bit_length() >> 1)) * rows_out
+        send_ref[first : first + atoms, :] = turned[j * atoms : (j + 1) * atoms].astype(BF16)
         at = plane * atoms + j * edge
-        send_refs[j][atoms:, :] = turned[at : at + edge].astype(BF16)
-
-
-def finish_kernel(plane, me_ref, *refs):
+        send_ref[first + atoms : first + rows_out, :] = turned[at : at + edge].astype(BF16)
+
+
+def finish_kernel(plane, firsts, place_ref, *refs):
     slices = refs[:plane]
-    below_ref, above_ref, feats_ref, mix_ref, gate_ref, out_ref = refs[plane:]
+    near_ref, far_ref, feats_ref, mix_ref, gate_ref, out_ref = refs[plane:]
     atoms = feats_ref.shape[1]
     channels = feats_ref.shape[2]
     part = channels // plane
-    face = below_ref.shape[1]
+    face = near_ref.shape[1]
+    odd = (jnp.zeros((face, channels), jnp.int32) + place_ref[0]) % 2 > 0
     per = channels // part
-    me = me_ref[0]
+    me = place_ref[0] >> 1
     lane = lax.broadcasted_iota(jnp.int32, (atoms, channels), 1)
     gates = jax.nn.sigmoid(dot(feats_ref[0], gate_ref[...]))
 
     def slab(j, group):
         columns = slice(group * channels, (group + 1) * channels)
-        own = slices[j][:atoms, columns].astype(F32)
-        low = own[:face] + below_ref[j, :, columns].astype(F32)
-        high = own[atoms - face :] + above_ref[j, :, columns].astype(F32)
+        own = slices[j][firsts[j] : firsts[j] + atoms, columns].astype(F32)
+        near, far = near_ref[j, :, columns].astype(F32), far_ref[j, :, columns].astype(F32)
+        low = own[:face] + jnp.where(odd, near, far)
+        high = own[atoms - face :] + jnp.where(odd, far, near)
         return jnp.concatenate([low, own[face : atoms - face], high], axis=0)
 
     upstream = []
@@ -279,14 +274,14 @@
     out_ref[:, 0, :] = zero_row + back[:atoms] + back[atoms:]
 
 
-def assemble_kernel(plane, me_ref, *refs):
+def assemble_kernel(plane, place_ref, *refs):
     pieces = refs[:plane]
     mix_ref, gate_ref = refs[plane : plane + 2]
     (joined_ref,) = refs[plane + 2 :]
     part = pieces[0].shape[0] // 7
     channels = plane * part
     for j in range(plane):
-        home = pl.multiple_of((me_ref[0] ^ j) * part, part)
+        home = pl.multiple_of(((place_ref[0] >> 1) ^ j) * part, part)
         for block in range(7):
             joined_ref[block, pl.ds(home, part), :] = pieces[j][block * part : (block + 1) * part, :]
     for block in range(4):
@@ -295,16 +290,17 @@
         gate_ref[:, block * channels : (block + 1) * channels] = joined_ref[4 + block].T
 
 
-def call(kernel, outs, scratch, scalars, *arrays):
+def call(kernel, outs, scratch, *arrays):
     vmem = pl.BlockSpec(memory_space=pltpu.VMEM)
+    smem = pl.BlockSpec(memory_space=pltpu.SMEM)
     return pl.pallas_call(
         kernel,
         out_shape=outs,
-        in_specs=[pl.BlockSpec(memory_space=pltpu.SMEM)] + [vmem] * len(arrays),
+        in_specs=[smem if x.shape == (1,) else vmem for x in arrays],
         out_specs=jax.tree.map(lambda _: vmem, outs),
         scratch_shapes=scratch,
         compiler_params=pltpu.CompilerParams(vmem_limit_bytes=VMEM_BYTES),
-    )(scalars, *arrays)
+    )(*arrays)
 
 
 def body(
@@ -329,13 +325,17 @@
     total = plane * (atoms + edge)
     lanes = plane * probes
     me = lax.axis_index("xy").astype(jnp.int32)
-    me_arr = me[None]
+    slab = lax.axis_index("slab").astype(jnp.int32)
+    odd = slab % 2
+    place = (me * 2 + odd)[None]
 
     domain = nbr_atom // atoms
     row = nbr_atom % atoms
-    step = domain // plane - lax.axis_index("slab")
+    step = domain // plane - slab
     wide = plane * atoms
-    offset = jnp.where(step == 0, row, jnp.where(step < 0, wide + row - (atoms - face), wide + face + row))
+    below = wide + (1 - odd) * face + row - (atoms - face)
+    above = wide + odd * face + row
+    offset = jnp.where(step == 0, row, jnp.where(step < 0, below, above))
     code = offset * plane + domain % plane
     tail = jnp.concatenate(
         [nbr_count.astype(F32)[None], target[None], jnp.zeros((slots - 2, probes), F32)], axis=0
@@ -343,12 +343,14 @@
     info = jnp.concatenate([pair_vec.reshape(3 * slots, probes), code.astype(F32), tail], axis=0)
 
     own = jnp.transpose(atom_feats, (1, 0, 2))
-    from_below = shifted(own[:, atoms - face :, :], "slab", 1)
-    from_above = shifted(own[:, :face, :], "slab", -1)
-    faces = jnp.concatenate([from_below, from_above], axis=1)
-    info, _ = lax.optimization_barrier((info, from_above))
+    last = atoms - face
+    near = beside(lax.dynamic_slice_in_dim(own, (1 - odd) * last, face, 1), "slab", True)
+    far = beside(lax.dynamic_slice_in_dim(own, odd * last, face, 1), "slab", False)
+    faces = jnp.concatenate([near, far], axis=1)
+    info, near = lax.optimization_barrier((info, near))
     bits = [1 << b for b in reversed(range((plane - 1).bit_length()))]
-    held = {0: (own, faces, info)}
+    infos = [info] + [partner(info, "xy", j) for j in range(1, plane)]
+    held = {0: (own, faces)}
     for bit in bits:
         for j in list(held):
             held[j ^ bit] = tuple(partner(x, "xy", bit) for x in held[j])
@@ -371,7 +373,19 @@
     radial_lhs = radial_lhs.reshape(slots * 4 * part, 3 * nbasis * slots).astype(BF16)
     out_part = lax.dynamic_slice_in_dim(out_weight, first, part)[:, None]
 
-    infos = [p[2] for p in pieces]
+    coef, harm, column, goals = call(
+        functools.partial(geometry_kernel, slots, atoms, edge, plane),
+        (
+            jax.ShapeDtypeStruct((slots * 4 * part, lanes), F32),
+            jax.ShapeDtypeStruct((harm_count * slots, lanes), F32),
+            jax.ShapeDtypeStruct((slots, lanes), jnp.int32),
+            jax.ShapeDtypeStruct((slots, lanes), F32),
+        ),
+        [],
+        place,
+        *infos,
+        radial_lhs,
+    )
     feats, mixed, gates, message, dens = call(
         functools.partial(forward_kernel, slots, plane),
         (
@@ -381,72 +395,83 @@
             jax.ShapeDtypeStruct((part, lanes), F32),
             jax.ShapeDtypeStruct((8, lanes), F32),
         ),
-        [
-            pltpu.VMEM((harm_count * part, total), BF16),
-            pltpu.VMEM((slots * 4 * part, lanes), F32),
-        ],
-        me_arr,
+        [pltpu.VMEM((harm_count * part, total), BF16)],
         *[p[0] for p in pieces],
         *[p[1] for p in pieces],
-        *infos,
+        coef,
+        harm,
+        column,
         mix_part,
         gate_part,
-        radial_lhs,
         out_part,
     )
     dens_all = [dens] + [partner(dens, "xy", j) for j in range(1, plane)]
 
+    groups = [1] + [1 << b for b in range((plane - 1).bit_length())]
     outs = call(
         functools.partial(backward_kernel, slots, plane, 1.0 / float(slabs * plane), float(probes)),
         (
             jax.ShapeDtypeStruct((7 * part, channels), F32),
             jax.ShapeDtypeStruct((8, probes), F32),
         )
-        + tuple(jax.ShapeDtypeStruct((atoms + edge, harm_count * part), BF16) for _ in range(plane)),
-        [
-            pltpu.VMEM((slots * 4 * part, lanes), F32),
-            pltpu.VMEM((harm_count * part, total), F32),
-        ],
-        me_arr,
-        *infos,
+        + tuple(jax.ShapeDtypeStruct((rows * (atoms + edge), harm_count * part), BF16) for rows in groups),
+        [pltpu.VMEM((harm_count * part, total), F32)],
         *dens_all,
+        coef,
+        harm,
+        column,
+        goals,
         feats,
         mixed,
         gates,
         message,
-        radial_lhs,
         out_part,
     )
     weight, density, sends = outs[0], outs[1], list(outs[2:])
 
     steps = [1 << b for b in range((slabs - 1).bit_length())]
-    weight = weight + partner(weight, "slab", steps[0])
-
-    weight, *sends = lax.optimization_barrier((weight, *sends))
-    slices = [sends[0]] + [partner(sends[j], "xy", j) for j in range(1, plane)]
-    to_below = jnp.stack([s[atoms : atoms + face] for s in slices], axis=0)
-    to_above = jnp.stack([s[atoms + face :] for s in slices], axis=0)
-    grad_above = shifted(to_below, "slab", -1)
-    grad_below = shifted(to_above, "slab", 1)
+    size = atoms + edge
+    entries = [(0, sends[0], {0: 0})]
+    for b, block in enumerate(sends[1:]):
+        entries.append((0, block, {j: (j - (1 << b)) * size for j in range(1 << b, 2 << b)}))
+    for bit in bits:
+        due = [e for e in entries if any(bit <= j < 2 * bit for j in e[2])]
+        for source, block, places in due:
+            moved = {j ^ bit: at for j, at in places.items()}
+            entries.append((source ^ bit, partner(block, "xy", bit), moved))
+    mine = {source: (block, places[0]) for source, block, places in entries if 0 in places}
+    slices = [mine[j][0] for j in range(plane)]
+    firsts = tuple(mine[j][1] for j in range(plane))
+    for bit in steps[:-1]:
+        weight = weight + partner(weight, "slab", bit)
+    weight = weight.astype(LAST_STEP)
+    weight, *slices = lax.optimization_barrier((weight, *slices))
+    weight = (weight, partner(weight, "slab", steps[-1]))
+    edges = [s[f + atoms : f + size] for s, f in zip(slices, firsts)]
+    near_grad = beside(jnp.stack([e[:face] for e in edges], axis=0), "slab", True)
+    far_grad = beside(jnp.stack([e[face:] for e in edges], axis=0), "slab", False)
+    *weight, near_grad, far_grad = lax.optimization_barrier((*weight, near_grad, far_grad))
+    weight = weight[0].astype(F32) + weight[1].astype(F32)
     feat_grad = call(
-        functools.partial(finish_kernel, plane),
+        functools.partial(finish_kernel, plane, firsts),
         jax.ShapeDtypeStruct((atoms, harm_count, channels), F32),
         [],
-        me_arr,
+        place,
         *slices,
-        grad_below,
-        grad_above,
+        near_grad,
+        far_grad,
         own,
         mix_weight,
         gate_weight,
     )
 
-    for bit in steps[1:]:
-        weight = weight + partner(weight, "slab", bit)
     columns = {0: weight}
     for bit in bits:
-        for j in list(columns):
-            columns[j ^ bit] = partner(columns[j], "xy", bit)
+        arrived = {j ^ bit: partner(columns[j], "xy", bit) for j in columns}
+        if bit == bits[0]:
+            *values, feat_grad = lax.optimization_barrier((*arrived.values(), feat_grad))
+            arrived = dict(zip(arrived, values))
+        columns.update(arrived)
     mix_grad, gate_grad = call(
         functools.partial(assemble_kernel, plane),
         (
@@ -454,7 +479,7 @@
             jax.ShapeDtypeStruct((channels, 3 * channels), F32),
         ),
         [pltpu.VMEM((7, channels, channels), F32)],
-        me_arr,
+        place,
         *[columns[j] for j in range(plane)],
     )
     return (density[0], feat_grad, mix_grad, gate_grad)

time: 67.6 us -> 61.9 us (0.916)
  waiting for transfers between devices: 24.2 us -> 20.2 us
  starting transfers between devices: 28.6 us -> 26.2 us
  local copies, waits for them, and re-layouts: 2.66 us -> 3.52 us
    ppermute x4, waiting for transfers between devices: 6.78 us -> 0.89 us  [beside(): return lax.ppermute(block, axis, pairs + [(j, i) for i, j in pairs])]
    ppermute x4, starting transfers between devices: 9.91 us -> 7.43 us  [beside(): return lax.ppermute(block, axis, pairs + [(j, i) for i, j in pairs])]
    ppermute x21, waiting for transfers between devices: 17.4 us -> 19.3 us  [partner(): return lax.ppermute(block, axis, [(i, i ^ bit) for i in range(count)])]
    dynamic_slice x1, local copies, waits for them, and re-layouts: 0.1 us -> 1 us  [body(): mix_part = lax.dynamic_slice_in_dim(mix_weight, first, part, axis=2)]
    pallas_call x4 -> x5, Pallas kernels: 9.33 us -> 9.16 us  [call(): pl.pallas_call(kernel, out_shape=outs, in_specs=[smem if x.shape == (1,)...]
  transfers between devices with their start and end apart: 25 -> 25, of which waited for: 10 -> 12; matrix products, arithmetic and copies ran while one was open for 5% -> 7% of each run, Pallas kernels for 3% -> 4%
where the time goes in v3:
time: 61.9 us; the launch traced here: 61.7 us
  starting transfers between devices  26.2 us (42%)
  waiting for transfers between devices  20.2 us (33%)
  Pallas kernels  9.16 us (15%)
  local copies, waits for them, and re-layouts  3.52 us (6%)
  other arithmetic  1.69 us (3%)
  between operations  0.91 us (1%)
    ppermute x21, waiting for transfers between devices, partner(): return lax.ppermute(block, axis, [(i, i ^ bit) for i in range(count)])  19.3 us
    ppermute x21, starting transfers between devices, partner(): return lax.ppermute(block, axis, [(i, i ^ bit) for i in range(count)])  18.8 us
    pallas_call x5, Pallas kernels, call(): pl.pallas_call(kernel, out_shape=outs, in_specs=[smem if x.shape == (1,)...  9.16 us
    ppermute x4, starting transfers between devices, beside(): return lax.ppermute(block, axis, pairs + [(j, i) for i, j in pairs])  7.43 us
    unnamed x18, local copies, waits for them, and re-layouts  1.4 us
  transfers between devices with their start and end apart: 25, of which 12 were waited for; matrix products, arithmetic and copies ran while one was open for 7% of the time, Pallas kernels for 4%

profile of v3, /device:TPU:0, one launch (start us, length us, event | category | flops | bytes accessed | tf_op | source)
XLA Modules:
  0.0 61.7 jit_solution(14308849930118860339)
XLA Ops:
  0.7 1.1 %copy.38 = bf16[64,16,128]{2,0,1:T(8,128)(2,1)S(1)} copy(bf16[64,16,128]{2,1,0:T(8,128)(2,1)} %param.9) | data formatting | bytes 524288 | tf_op args[0]
  1.8 3.0 %collective-permute-start.1 = (bf16[16,64,128]{2,1,0:T(8,128)(2,1)S(1)}, bf16[16,64,128]{2,1,0:T(8,128)(2,1)S(1)}, u32[]{:S(2)}, u32[]{:S(2)}) collective-permute-start(bf16[16,64,128]{2,1,0:T(8,128)(2,1)S(1)} %bitcast.50), channel_id=1, source_target_pairs={{0,2},{1,3},{2,0},{3,1},{4,6},{5,7},{6,4},{7,5},{8,10},{9,11},{10,... | collective-permute-start | bytes 786440 | tf_op jit(solution)/shard_map/ppermute | solution.py:63
  4.8 0.7 %collective-permute-start.4 = (bf16[16,16,128]{2,1,0:T(8,128)(2,1)S(1)}, bf16[16,16,128]{2,1,0:T(8,128)(2,1)S(1)}, u32[]{:S(2)}, u32[]{:S(2)}) collective-permute-start(bf16[16,16,128]{2,1,0:T(8,128)(2,1)S(1)} %get-tuple-element.60), channel_id=1, source_target_pairs={{4,8},{12,16},{20,24},{8,4},{16,12},{24,20},{5,9},{13,17},{21,25},... | collective-permute-start | bytes 196616 | tf_op jit(solution)/shard_map/ppermute | solution.py:70
  5.5 4.3 %collective-permute-start.3 = (bf16[16,16,128]{2,1,0:T(8,128)(2,1)S(1)}, bf16[16,16,128]{2,1,0:T(8,128)(2,1)S(1)}, u32[]{:S(2)}, u32[]{:S(2)}) collective-permute-start(bf16[16,16,128]{2,1,0:T(8,128)(2,1)S(1)} %get-tuple-element.61), channel_id=1, source_target_pairs={{0,4},{8,12},{16,20},{24,28},{4,0},{12,8},{20,16},{28,24},{1,5},{9... | collective-permute-start | bytes 196616 | tf_op jit(solution)/shard_map/ppermute | solution.py:70
  9.9 0.1 constant_dynamic-slice_fusion.2
  9.9 0.1 reshape.62
  10.0 0.1 fusion
  10.1 0.2 multiply_convert_fusion
  10.3 0.7 %fusion.3 = f32[8,128]{1,0:T(8,128)S(1)} fusion(s32[8,128]{1,0:T(8,128)} %param.15, s32[]{:T(128)S(6)} %add.77, s32[]{:T(128)S(6)} %add.74, s32[]{:T(128)S(6)} %axis_index.23), kind=kLoop, calls=%fused_computation.33 | loop fusion | flops 50176 | bytes 8204 | tf_op jit(solution)/shard_map/convert_element_type | solution.py:343
  11.0 0.7 %convert_bitcast_fusion = f32[1,128]{1,0:T(1,128)S(1)} fusion(s32[128]{0:T(128)} %param.16), kind=kLoop, calls=%fused_computation.47 | loop fusion | flops 128 | bytes 1024 | tf_op jit(solution)/shard_map/broadcast_in_dim | solution.py:341
  11.7 0.9 %collective-permute-done.3 = bf16[16,16,128]{2,1,0:T(8,128)(2,1)S(1)} collective-permute-done((bf16[16,16,128]{2,1,0:T(8,128)(2,1)S(1)}, bf16[16,16,128]{2,1,0:T(8,128)(2,1)S(1)}, u32[]{:S(2)}, u32[]{:S(2)}) %collective-permute-start.3) | collective-permute-done | bytes 65568 | tf_op jit(solution)/shard_map/ppermute | solution.py:70
  12.6 0.6 collective-permute-start.6
  13.1 1.0 %constant_dynamic-slice_fusion.1 = bf16[4,128,32]{2,1,0:T(8,128)(2,1)S(1)} fusion(bf16[4,128,128]{2,1,0:T(8,128)(2,1)} %refs_7_.1, s32[]{:T(128)S(6)} %select_n.52), kind=kLoop, calls=%fused_computation.42 | loop fusion | bytes 65540 | tf_op jit(solution)/shard_map/dynamic_slice | solution.py:360
  14.2 0.1 copy.30
  14.3 0.9 %collective-permute-start.10 = (f32[40,128]{1,0:T(8,128)S(1)}, f32[40,128]{1,0:T(8,128)S(1)}, u32[]{:S(2)}, u32[]{:S(2)}) collective-permute-start(f32[40,128]{1,0:T(8,128)S(1)} %concatenate.10.refs_0_), channel_id=1, source_target_pairs={{0,3},{1,2},{2,1},{3,0},{4,7},{5,6},{6,5},{7,4},{8,11},{9,10},{10,... | collective-permute-start | bytes 61448 | tf_op jit(solution)/shard_map/ppermute | solution.py:63
  15.3 0.7 %collective-permute-start.2 = (bf16[16,64,128]{2,1,0:T(8,128)(2,1)S(1)}, bf16[16,64,128]{2,1,0:T(8,128)(2,1)S(1)}, u32[]{:S(2)}, u32[]{:S(2)}) collective-permute-start(bf16[16,64,128]{2,1,0:T(8,128)(2,1)S(1)} %collective-permute-done.1.refs_2_), channel_id=1, source_target_pairs={{0,1},{1,0},{2,3},{3,2},{4,5},{5,4},{6,7},{7,6},{8,9},{9,8},{10,11... | collective-permute-start | bytes 786440 | tf_op jit(solution)/shard_map/ppermute | solution.py:63
  16.0 0.1 copy.26
  16.1 0.6 collective-permute-start.9
  16.7 1.1 %collective-permute-done.10.refs_3_ = f32[40,128]{1,0:T(8,128)S(1)} collective-permute-done((f32[40,128]{1,0:T(8,128)S(1)}, f32[40,128]{1,0:T(8,128)S(1)}, u32[]{:S(2)}, u32[]{:S(2)}) %collective-permute-start.10) | collective-permute-done | bytes 20512 | tf_op jit(solution)/shard_map/ppermute | solution.py:63
  17.8 0.6 collective-permute-start.5
  18.4 1.6 %collective-permute-done.9.refs_2_ = f32[40,128]{1,0:T(8,128)S(1)} collective-permute-done((f32[40,128]{1,0:T(8,128)S(1)}, f32[40,128]{1,0:T(8,128)S(1)}, u32[]{:S(2)}, u32[]{:S(2)}) %collective-permute-start.9) | collective-permute-done | bytes 20512 | tf_op jit(solution)/shard_map/ppermute | solution.py:63
  20.1 0.1 copy.27.refs_13_.refs_12_
  20.2 0.2 copy.24.refs_4_
  20.4 0.7 %collective-permute-done.8.refs_1_ = f32[40,128]{1,0:T(8,128)S(1)} collective-permute-done((f32[40,128]{1,0:T(8,128)S(1)}, f32[40,128]{1,0:T(8,128)S(1)}, u32[]{:S(2)}, u32[]{:S(2)}) %collective-permute-start.8) | collective-permute-done | bytes 20512 | tf_op jit(solution)/shard_map/ppermute | solution.py:63
  21.2 0.5 shard_map.120
  21.7 3.2 %shard_map.121 = (bf16[16,384,128]{2,1,0:T(8,128)(2,1)S(1)}, f32[512,384]{1,0:T(8,128)S(1)}, f32[96,384]{1,0:T(8,128)S(1)}, f32[32,512]{1,0:T(8,128)S(1)}, f32[8,512]{1,0:T(8,128)S(1)}) custom-call(bf16[16,64,128]{2,1,0:T(8,128)(2,1)S(1)} %bitcast.52, bf16[16,64,128]{2,1,0:T(8,128)(2,1)S(1)} %collective-permute-done.refs_1_, ...), custom_call_target="tpu_custom_call" | custom-call | tf_op jit(solution)/shard_map/pallas_call | solution.py:296
  24.9 0.3 collective-permute-start.13
  25.3 1.5 %collective-permute-start.12 = (f32[8,512]{1,0:T(8,128)S(1)}, f32[8,512]{1,0:T(8,128)S(1)}, u32[]{:S(2)}, u32[]{:S(2)}) collective-permute-start(f32[8,512]{1,0:T(8,128)S(1)} %get-tuple-element.36.refs_0_), channel_id=1, source_target_pairs={{0,2},{1,3},{2,0},{3,1},{4,6},{5,7},{6,4},{7,5},{8,10},{9,11},{10,... | collective-permute-start | bytes 49160 | tf_op jit(solution)/shard_map/ppermute | solution.py:63
  26.9 1.3 %collective-permute-done.13.refs_3_ = f32[8,512]{1,0:T(8,128)S(1)} collective-permute-done((f32[8,512]{1,0:T(8,128)S(1)}, f32[8,512]{1,0:T(8,128)S(1)}, u32[]{:S(2)}, u32[]{:S(2)}) %collective-permute-start.13) | collective-permute-done | bytes 16416 | tf_op jit(solution)/shard_map/ppermute | solution.py:63
  28.2 0.9 %collective-permute-done.12.refs_2_ = f32[8,512]{1,0:T(8,128)S(1)} collective-permute-done((f32[8,512]{1,0:T(8,128)S(1)}, f32[8,512]{1,0:T(8,128)S(1)}, u32[]{:S(2)}, u32[]{:S(2)}) %collective-permute-start.12) | collective-permute-done | bytes 16416 | tf_op jit(solution)/shard_map/ppermute | solution.py:63
  29.0 2.8 %shard_map.122 = (f32[224,128]{1,0:T(8,128)S(1)}, f32[8,128]{1,0:T(8,128)S(1)}, bf16[96,512]{1,0:T(8,128)(2,1)S(1)}, bf16[96,512]{1,0:T(8,128)(2,1)S(1)}, bf16[192,512]{1,0:T(8,128)(2,1)S(1)}) custom-call(f32[8,512]{1,0:T(8,128)S(1)} %get-tuple-element.36.refs_0_, f32[8,512]{1,0:T(8,128)S(1)} %collective-permute-done.11.refs_1_, ...), custom_call_target="tpu_custom_call" | custom-call | tf_op jit(solution)/shard_map/pallas_call | solution.py:296
  31.8 1.6 %collective-permute-start.17 = (bf16[192,512]{1,0:T(8,128)(2,1)S(1)}, bf16[192,512]{1,0:T(8,128)(2,1)S(1)}, u32[]{:S(2)}, u32[]{:S(2)}) collective-permute-start(bf16[192,512]{1,0:T(8,128)(2,1)S(1)} %get-tuple-element.46), channel_id=1, source_target_pairs={{0,2},{1,3},{2,0},{3,1},{4,6},{5,7},{6,4},{7,5},{8,10},{9,11},{10,... | collective-permute-start | bytes 589832 | tf_op jit(solution)/shard_map/ppermute | solution.py:63
  33.4 2.5 %collective-permute-start.14 = (f32[224,128]{1,0:T(8,128)S(1)}, f32[224,128]{1,0:T(8,128)S(1)}, u32[]{:S(2)}, u32[]{:S(2)}) collective-permute-start(f32[224,128]{1,0:T(8,128)S(1)} %get-tuple-element.43), channel_id=1, source_target_pairs={{0,4},{4,0},{8,12},{12,8},{16,20},{20,16},{24,28},{28,24},{1,5},{5... | collective-permute-start | bytes 344072 | tf_op jit(solution)/shard_map/ppermute | solution.py:63
  35.9 2.2 %collective-permute-done.17.refs_2_ = bf16[192,512]{1,0:T(8,128)(2,1)S(1)} collective-permute-done((bf16[192,512]{1,0:T(8,128)(2,1)S(1)}, bf16[192,512]{1,0:T(8,128)(2,1)S(1)}, u32[]{:S(2)}, u32[]{:S(2)}) %collective-permute-start.17) | collective-permute-done | bytes 196640 | tf_op jit(solution)/shard_map/ppermute | solution.py:63
  38.1 0.6 collective-permute-done.14
  38.6 2.2 %collective-permute-start.15 = (f32[224,128]{1,0:T(8,128)S(1)}, f32[224,128]{1,0:T(8,128)S(1)}, u32[]{:S(2)}, u32[]{:S(2)}) collective-permute-start(f32[224,128]{1,0:T(8,128)S(1)} %add.85), channel_id=1, source_target_pairs={{0,8},{4,12},{8,0},{12,4},{16,24},{20,28},{24,16},{28,20},{1,9},{5... | collective-permute-start | bytes 344072 | tf_op jit(solution)/shard_map/ppermute | solution.py:63
  40.9 0.1 collective-permute-start.16
  40.9 3.6 %collective-permute-done.15 = f32[224,128]{1,0:T(8,128)S(1)} collective-permute-done((f32[224,128]{1,0:T(8,128)S(1)}, f32[224,128]{1,0:T(8,128)S(1)}, u32[]{:S(2)}, u32[]{:S(2)}) %collective-permute-start.15) | collective-permute-done | bytes 114720 | tf_op jit(solution)/shard_map/ppermute | solution.py:63
  44.6 1.7 %collective-permute-start.20 = (bf16[4,16,512]{2,1,0:T(8,128)(2,1)S(1)}, bf16[4,16,512]{2,1,0:T(8,128)(2,1)S(1)}, u32[]{:S(2)}, u32[]{:S(2)}) collective-permute-start(bf16[4,16,512]{2,1,0:T(8,128)(2,1)S(1)} %pad_maximum_fusion.1), channel_id=1, source_target_pairs={{0,4},{8,12},{16,20},{24,28},{4,0},{12,8},{20,16},{28,24},{1,5},{9... | collective-permute-start | bytes 196616 | tf_op jit(solution)/shard_map/ppermute | solution.py:70
  46.4 2.6 %collective-permute-start.19 = (f32[224,128]{1,0:T(8,128)S(1)}, f32[224,128]{1,0:T(8,128)S(1)}, u32[]{:S(2)}, u32[]{:S(2)}) collective-permute-start(f32[224,128]{1,0:T(8,128)S(1)} %add.86), channel_id=1, source_target_pairs={{0,16},{4,20},{8,24},{12,28},{16,0},{20,4},{24,8},{28,12},{1,17},{... | collective-permute-start | bytes 344072 | tf_op jit(solution)/shard_map/ppermute | solution.py:63
  48.9 0.7 %collective-permute-start.21 = (bf16[4,16,512]{2,1,0:T(8,128)(2,1)S(1)}, bf16[4,16,512]{2,1,0:T(8,128)(2,1)S(1)}, u32[]{:S(2)}, u32[]{:S(2)}) collective-permute-start(bf16[4,16,512]{2,1,0:T(8,128)(2,1)S(1)} %pad_maximum_fusion.2), channel_id=1, source_target_pairs={{4,8},{12,16},{20,24},{8,4},{16,12},{24,20},{5,9},{13,17},{21,25},... | collective-permute-start | bytes 196616 | tf_op jit(solution)/shard_map/ppermute | solution.py:70
  49.6 4.9 %collective-permute-done.19 = f32[224,128]{1,0:T(8,128)S(1)} collective-permute-done((f32[224,128]{1,0:T(8,128)S(1)}, f32[224,128]{1,0:T(8,128)S(1)}, u32[]{:S(2)}, u32[]{:S(2)}) %collective-permute-start.19) | collective-permute-done | bytes 114720 | tf_op jit(solution)/shard_map/ppermute | solution.py:63
  54.6 1.5 %collective-permute-start.22 = (f32[224,128]{1,0:T(8,128)S(1)}, f32[224,128]{1,0:T(8,128)S(1)}, u32[]{:S(2)}, u32[]{:S(2)}) collective-permute-start(f32[224,128]{1,0:T(8,128)S(1)} %add.87.refs_0_), channel_id=1, source_target_pairs={{0,2},{1,3},{2,0},{3,1},{4,6},{5,7},{6,4},{7,5},{8,10},{9,11},{10,... | collective-permute-start | bytes 344072 | tf_op jit(solution)/shard_map/ppermute | solution.py:63
  56.1 1.7 %shard_map.123 = f32[64,16,128]{2,1,0:T(8,128)} custom-call(s32[1]{0:T(128)} %bitcast.3.place_ref, bf16[96,512]{1,0:T(8,128)(2,1)S(1)} %get-tuple-element.48.refs_0_, bf16[96,512]{1,0:T(8,128)(2,1)S(1)} %collective-permute-done.16.refs_1_, bf16[192,512]{1,0:T(8,128)(2,1)S(1)} %collective-permute-done.17.refs_2_, ...), custom_call_target="tpu_custom_call" | custom-call | tf_op jit(solution)/shard_map/pallas_call | solution.py:296
  57.8 1.6 %collective-permute-done.22.refs_2_ = f32[224,128]{1,0:T(8,128)S(1)} collective-permute-done((f32[224,128]{1,0:T(8,128)S(1)}, f32[224,128]{1,0:T(8,128)S(1)}, u32[]{:S(2)}, u32[]{:S(2)}) %collective-permute-start.22) | collective-permute-done | bytes 114720 | tf_op jit(solution)/shard_map/ppermute | solution.py:63
  59.4 0.5 slice_bitcast_fusion.8
  60.0 0.8 %collective-permute-done.24.refs_3_ = f32[224,128]{1,0:T(8,128)S(1)} collective-permute-done((f32[224,128]{1,0:T(8,128)S(1)}, f32[224,128]{1,0:T(8,128)S(1)}, u32[]{:S(2)}, u32[]{:S(2)}) %collective-permute-start.24) | collective-permute-done | bytes 114720 | tf_op jit(solution)/shard_map/ppermute | solution.py:63
  60.8 0.9 %shard_map.124 = (f32[4,128,128]{2,1,0:T(8,128)}, f32[128,384]{1,0:T(8,128)}) custom-call(s32[1]{0:T(128)} %bitcast.3.place_ref, f32[224,128]{1,0:T(8,128)S(1)} %add.87.refs_0_, f32[224,128]{1,0:T(8,128)S(1)} %collective-permute-done.23.refs_1_, f32[224,128]{1,0:T(8,128)S(1)} %collective-permute-done.22.refs_2_, f32[224,128]{1,0:T(8,128)S(1)} %collective-permute-done.24.refs_3_), custom_call_target="tpu_custom_call" | custom-call | tf_op jit(solution)/shard_map/pallas_call | solution.py:296
  (53 shorter events, 0.5 us)
Async XLA Ops:
  0.6 9.2 %copy-start = (f32[8,512]{1,0:T(8,128)S(1)}, f32[8,512]{1,0:T(8,128)}, u32[]{:S(2)}) copy-start(f32[8,512]{1,0:T(8,128)} %param.12) | copy-start | bytes 49156
  0.6 13.6 %copy-start.4 = (f32[128]{0:T(128)S(1)}, f32[128]{0:T(128)}, u32[]{:S(2)}) copy-start(f32[128]{0:T(128)} %param.17) | copy-start | bytes 1540
  0.7 13.6 %copy-start.3 = (f32[3,8,128]{2,1,0:T(8,128)S(1)}, f32[3,8,128]{2,1,0:T(8,128)}, u32[]{:S(2)}) copy-start(f32[3,8,128]{2,1,0:T(8,128)} %param.14) | copy-start | bytes 36868
  0.7 15.3 %copy-start.2 = (bf16[128,384]{1,0:T(8,128)(2,1)S(1)}, bf16[128,384]{1,0:T(8,128)(2,1)}, u32[]{:S(2)}) copy-start(bf16[128,384]{1,0:T(8,128)(2,1)} %refs_8_.1) | copy-start | bytes 294916
  0.7 19.3 %copy-start.5 = (f32[128]{0:T(128)S(1)}, f32[128]{0:T(128)}, u32[]{:S(2)}) copy-start(f32[128]{0:T(128)} %param.13) | copy-start | bytes 1540
  1.8 13.5 %collective-permute-start.1 = (bf16[16,64,128]{2,1,0:T(8,128)(2,1)S(1)}, bf16[16,64,128]{2,1,0:T(8,128)(2,1)S(1)}, u32[]{:S(2)}, u32[]{:S(2)}) collective-permute-start(bf16[16,64,128]{2,1,0:T(8,128)(2,1)S(1)} %bitcast.50), channel_id=1, source_target_pairs={{0,2},{1,3},{2,0},{3,1},{4,6},{5,7},{6,4},{7,5},{8,10},{9,11},{10,... | collective-permute-start | bytes 786440 | tf_op jit(solution)/shard_map/ppermute | solution.py:63
  4.8 16.9 %collective-permute-start = (bf16[16,64,128]{2,1,0:T(8,128)(2,1)S(1)}, bf16[16,64,128]{2,1,0:T(8,128)(2,1)S(1)}, u32[]{:S(2)}, u32[]{:S(2)}) collective-permute-start(bf16[16,64,128]{2,1,0:T(8,128)(2,1)S(1)} %bitcast.51), channel_id=1, source_target_pairs={{0,1},{1,0},{2,3},{3,2},{4,5},{5,4},{6,7},{7,6},{8,9},{9,8},{10,11... | collective-permute-start | bytes 786440 | tf_op jit(solution)/shard_map/ppermute | solution.py:63
  4.8 7.7 %collective-permute-start.4 = (bf16[16,16,128]{2,1,0:T(8,128)(2,1)S(1)}, bf16[16,16,128]{2,1,0:T(8,128)(2,1)S(1)}, u32[]{:S(2)}, u32[]{:S(2)}) collective-permute-start(bf16[16,16,128]{2,1,0:T(8,128)(2,1)S(1)} %get-tuple-element.60), channel_id=1, source_target_pairs={{4,8},{12,16},{20,24},{8,4},{16,12},{24,20},{5,9},{13,17},{21,25},... | collective-permute-start | bytes 196616 | tf_op jit(solution)/shard_map/ppermute | solution.py:70
  5.5 7.0 %collective-permute-start.3 = (bf16[16,16,128]{2,1,0:T(8,128)(2,1)S(1)}, bf16[16,16,128]{2,1,0:T(8,128)(2,1)S(1)}, u32[]{:S(2)}, u32[]{:S(2)}) collective-permute-start(bf16[16,16,128]{2,1,0:T(8,128)(2,1)S(1)} %get-tuple-element.61), channel_id=1, source_target_pairs={{0,4},{8,12},{16,20},{24,28},{4,0},{12,8},{20,16},{28,24},{1,5},{9... | collective-permute-start | bytes 196616 | tf_op jit(solution)/shard_map/ppermute | solution.py:70
  12.6 5.9 %collective-permute-start.6 = (bf16[16,32,128]{2,1,0:T(8,128)(2,1)S(1)}, bf16[16,32,128]{2,1,0:T(8,128)(2,1)S(1)}, u32[]{:S(2)}, u32[]{:S(2)}) collective-permute-start(bf16[16,32,128]{2,1,0:T(8,128)(2,1)S(1)} %constant_dynamic-update-slice_fusion.refs_4_), channel_id=1, source_target_pairs={{0,2},{1,3},{2,0},{3,1},{4,6},{5,7},{6,4},{7,5},{8,10},{9,11},{10,... | collective-permute-start | bytes 393224 | tf_op jit(solution)/shard_map/ppermute | solution.py:63
  14.3 3.5 %collective-permute-start.10 = (f32[40,128]{1,0:T(8,128)S(1)}, f32[40,128]{1,0:T(8,128)S(1)}, u32[]{:S(2)}, u32[]{:S(2)}) collective-permute-start(f32[40,128]{1,0:T(8,128)S(1)} %concatenate.10.refs_0_), channel_id=1, source_target_pairs={{0,3},{1,2},{2,1},{3,0},{4,7},{5,6},{6,5},{7,4},{8,11},{9,10},{10,... | collective-permute-start | bytes 61448 | tf_op jit(solution)/shard_map/ppermute | solution.py:63
  15.3 6.5 %collective-permute-start.2 = (bf16[16,64,128]{2,1,0:T(8,128)(2,1)S(1)}, bf16[16,64,128]{2,1,0:T(8,128)(2,1)S(1)}, u32[]{:S(2)}, u32[]{:S(2)}) collective-permute-start(bf16[16,64,128]{2,1,0:T(8,128)(2,1)S(1)} %collective-permute-done.1.refs_2_), channel_id=1, source_target_pairs={{0,1},{1,0},{2,3},{3,2},{4,5},{5,4},{6,7},{7,6},{8,9},{9,8},{10,11... | collective-permute-start | bytes 786440 | tf_op jit(solution)/shard_map/ppermute | solution.py:63
  16.1 3.8 %collective-permute-start.9 = (f32[40,128]{1,0:T(8,128)S(1)}, f32[40,128]{1,0:T(8,128)S(1)}, u32[]{:S(2)}, u32[]{:S(2)}) collective-permute-start(f32[40,128]{1,0:T(8,128)S(1)} %concatenate.10.refs_0_), channel_id=1, source_target_pairs={{0,2},{1,3},{2,0},{3,1},{4,6},{5,7},{6,4},{7,5},{8,10},{9,11},{10,... | collective-permute-start | bytes 61448 | tf_op jit(solution)/shard_map/ppermute | solution.py:63
  17.8 3.9 %collective-permute-start.5 = (bf16[16,32,128]{2,1,0:T(8,128)(2,1)S(1)}, bf16[16,32,128]{2,1,0:T(8,128)(2,1)S(1)}, u32[]{:S(2)}, u32[]{:S(2)}) collective-permute-start(bf16[16,32,128]{2,1,0:T(8,128)(2,1)S(1)} %constant_dynamic-update-slice_fusion.refs_4_), channel_id=1, source_target_pairs={{0,1},{1,0},{2,3},{3,2},{4,5},{5,4},{6,7},{7,6},{8,9},{9,8},{10,11... | collective-permute-start | bytes 393224 | tf_op jit(solution)/shard_map/ppermute | solution.py:63
  18.4 3.3 %collective-permute-start.7 = (bf16[16,32,128]{2,1,0:T(8,128)(2,1)S(1)}, bf16[16,32,128]{2,1,0:T(8,128)(2,1)S(1)}, u32[]{:S(2)}, u32[]{:S(2)}) collective-permute-start(bf16[16,32,128]{2,1,0:T(8,128)(2,1)S(1)} %collective-permute-done.6.refs_6_), channel_id=1, source_target_pairs={{0,1},{1,0},{2,3},{3,2},{4,5},{5,4},{6,7},{7,6},{8,9},{9,8},{10,11... | collective-permute-start | bytes 393224 | tf_op jit(solution)/shard_map/ppermute | solution.py:63
  20.0 1.2 %collective-permute-start.8 = (f32[40,128]{1,0:T(8,128)S(1)}, f32[40,128]{1,0:T(8,128)S(1)}, u32[]{:S(2)}, u32[]{:S(2)}) collective-permute-start(f32[40,128]{1,0:T(8,128)S(1)} %concatenate.10.refs_0_), channel_id=1, source_target_pairs={{0,1},{1,0},{2,3},{3,2},{4,5},{5,4},{6,7},{7,6},{8,9},{9,8},{10,11... | collective-permute-start | bytes 61448 | tf_op jit(solution)/shard_map/ppermute | solution.py:63
  24.9 3.2 %collective-permute-start.13 = (f32[8,512]{1,0:T(8,128)S(1)}, f32[8,512]{1,0:T(8,128)S(1)}, u32[]{:S(2)}, u32[]{:S(2)}) collective-permute-start(f32[8,512]{1,0:T(8,128)S(1)} %get-tuple-element.36.refs_0_), channel_id=1, source_target_pairs={{0,3},{1,2},{2,1},{3,0},{4,7},{5,6},{6,5},{7,4},{8,11},{9,10},{10,... | collective-permute-start | bytes 49160 | tf_op jit(solution)/shard_map/ppermute | solution.py:63
  25.3 3.7 %collective-permute-start.12 = (f32[8,512]{1,0:T(8,128)S(1)}, f32[8,512]{1,0:T(8,128)S(1)}, u32[]{:S(2)}, u32[]{:S(2)}) collective-permute-start(f32[8,512]{1,0:T(8,128)S(1)} %get-tuple-element.36.refs_0_), channel_id=1, source_target_pairs={{0,2},{1,3},{2,0},{3,1},{4,6},{5,7},{6,4},{7,5},{8,10},{9,11},{10,... | collective-permute-start | bytes 49160 | tf_op jit(solution)/shard_map/ppermute | solution.py:63
  26.8 2.2 %collective-permute-start.11 = (f32[8,512]{1,0:T(8,128)S(1)}, f32[8,512]{1,0:T(8,128)S(1)}, u32[]{:S(2)}, u32[]{:S(2)}) collective-permute-start(f32[8,512]{1,0:T(8,128)S(1)} %get-tuple-element.36.refs_0_), channel_id=1, source_target_pairs={{0,1},{1,0},{2,3},{3,2},{4,5},{5,4},{6,7},{7,6},{8,9},{9,8},{10,11... | collective-permute-start | bytes 49160 | tf_op jit(solution)/shard_map/ppermute | solution.py:63
  29.0 27.0 %copy-start.1 = (bf16[4,128,128]{2,1,0:T(8,128)(2,1)S(1)}, bf16[4,128,128]{2,1,0:T(8,128)(2,1)}, u32[]{:S(2)}) copy-start(bf16[4,128,128]{2,1,0:T(8,128)(2,1)} %refs_7_.1) | copy-start | bytes 393220
  31.8 6.2 %collective-permute-start.17 = (bf16[192,512]{1,0:T(8,128)(2,1)S(1)}, bf16[192,512]{1,0:T(8,128)(2,1)S(1)}, u32[]{:S(2)}, u32[]{:S(2)}) collective-permute-start(bf16[192,512]{1,0:T(8,128)(2,1)S(1)} %get-tuple-element.46), channel_id=1, source_target_pairs={{0,2},{1,3},{2,0},{3,1},{4,6},{5,7},{6,4},{7,5},{8,10},{9,11},{10,... | collective-permute-start | bytes 589832 | tf_op jit(solution)/shard_map/ppermute | solution.py:63
  33.4 5.3 %collective-permute-start.14 = (f32[224,128]{1,0:T(8,128)S(1)}, f32[224,128]{1,0:T(8,128)S(1)}, u32[]{:S(2)}, u32[]{:S(2)}) collective-permute-start(f32[224,128]{1,0:T(8,128)S(1)} %get-tuple-element.43), channel_id=1, source_target_pairs={{0,4},{4,0},{8,12},{12,8},{16,20},{20,16},{24,28},{28,24},{1,5},{5... | collective-permute-start | bytes 344072 | tf_op jit(solution)/shard_map/ppermute | solution.py:63
  38.0 6.5 %collective-permute-start.18 = (bf16[192,512]{1,0:T(8,128)(2,1)S(1)}, bf16[192,512]{1,0:T(8,128)(2,1)S(1)}, u32[]{:S(2)}, u32[]{:S(2)}) collective-permute-start(bf16[192,512]{1,0:T(8,128)(2,1)S(1)} %collective-permute-done.17.refs_2_), channel_id=1, source_target_pairs={{0,1},{1,0},{2,3},{3,2},{4,5},{5,4},{6,7},{7,6},{8,9},{9,8},{10,11... | collective-permute-start | bytes 589832 | tf_op jit(solution)/shard_map/ppermute | solution.py:63
  38.6 5.9 %collective-permute-start.15 = (f32[224,128]{1,0:T(8,128)S(1)}, f32[224,128]{1,0:T(8,128)S(1)}, u32[]{:S(2)}, u32[]{:S(2)}) collective-permute-start(f32[224,128]{1,0:T(8,128)S(1)} %add.85), channel_id=1, source_target_pairs={{0,8},{4,12},{8,0},{12,4},{16,24},{20,28},{24,16},{28,20},{1,9},{5... | collective-permute-start | bytes 344072 | tf_op jit(solution)/shard_map/ppermute | solution.py:63
  40.9 3.7 %collective-permute-start.16 = (bf16[96,512]{1,0:T(8,128)(2,1)S(1)}, bf16[96,512]{1,0:T(8,128)(2,1)S(1)}, u32[]{:S(2)}, u32[]{:S(2)}) collective-permute-start(bf16[96,512]{1,0:T(8,128)(2,1)S(1)} %get-tuple-element.45), channel_id=1, source_target_pairs={{0,1},{1,0},{2,3},{3,2},{4,5},{5,4},{6,7},{7,6},{8,9},{9,8},{10,11... | collective-permute-start | bytes 294920 | tf_op jit(solution)/shard_map/ppermute | solution.py:63
  44.6 5.0 %collective-permute-start.20 = (bf16[4,16,512]{2,1,0:T(8,128)(2,1)S(1)}, bf16[4,16,512]{2,1,0:T(8,128)(2,1)S(1)}, u32[]{:S(2)}, u32[]{:S(2)}) collective-permute-start(bf16[4,16,512]{2,1,0:T(8,128)(2,1)S(1)} %pad_maximum_fusion.1), channel_id=1, source_target_pairs={{0,4},{8,12},{16,20},{24,28},{4,0},{12,8},{20,16},{28,24},{1,5},{9... | collective-permute-start | bytes 196616 | tf_op jit(solution)/shard_map/ppermute | solution.py:70
  46.4 8.2 %collective-permute-start.19 = (f32[224,128]{1,0:T(8,128)S(1)}, f32[224,128]{1,0:T(8,128)S(1)}, u32[]{:S(2)}, u32[]{:S(2)}) collective-permute-start(f32[224,128]{1,0:T(8,128)S(1)} %add.86), channel_id=1, source_target_pairs={{0,16},{4,20},{8,24},{12,28},{16,0},{20,4},{24,8},{28,12},{1,17},{... | collective-permute-start | bytes 344072 | tf_op jit(solution)/shard_map/ppermute | solution.py:63
  48.9 0.7 %collective-permute-start.21 = (bf16[4,16,512]{2,1,0:T(8,128)(2,1)S(1)}, bf16[4,16,512]{2,1,0:T(8,128)(2,1)S(1)}, u32[]{:S(2)}, u32[]{:S(2)}) collective-permute-start(bf16[4,16,512]{2,1,0:T(8,128)(2,1)S(1)} %pad_maximum_fusion.2), channel_id=1, source_target_pairs={{4,8},{12,16},{20,24},{8,4},{16,12},{24,20},{5,9},{13,17},{21,25},... | collective-permute-start | bytes 196616 | tf_op jit(solution)/shard_map/ppermute | solution.py:70
  54.6 4.9 %collective-permute-start.22 = (f32[224,128]{1,0:T(8,128)S(1)}, f32[224,128]{1,0:T(8,128)S(1)}, u32[]{:S(2)}, u32[]{:S(2)}) collective-permute-start(f32[224,128]{1,0:T(8,128)S(1)} %add.87.refs_0_), channel_id=1, source_target_pairs={{0,2},{1,3},{2,0},{3,1},{4,6},{5,7},{6,4},{7,5},{8,10},{9,11},{10,... | collective-permute-start | bytes 344072 | tf_op jit(solution)/shard_map/ppermute | solution.py:63
  56.1 3.9 %collective-permute-start.23 = (f32[224,128]{1,0:T(8,128)S(1)}, f32[224,128]{1,0:T(8,128)S(1)}, u32[]{:S(2)}, u32[]{:S(2)}) collective-permute-start(f32[224,128]{1,0:T(8,128)S(1)} %add.87.refs_0_), channel_id=1, source_target_pairs={{0,1},{1,0},{2,3},{3,2},{4,5},{5,4},{6,7},{7,6},{8,9},{9,8},{10,11... | collective-permute-start | bytes 344072 | tf_op jit(solution)/shard_map/ppermute | solution.py:63
  59.4 1.3 %collective-permute-start.24 = (f32[224,128]{1,0:T(8,128)S(1)}, f32[224,128]{1,0:T(8,128)S(1)}, u32[]{:S(2)}, u32[]{:S(2)}) collective-permute-start(f32[224,128]{1,0:T(8,128)S(1)} %collective-permute-done.22.refs_2_), channel_id=1, source_target_pairs={{0,1},{1,0},{2,3},{3,2},{4,5},{5,4},{6,7},{7,6},{8,9},{9,8},{10,11... | collective-permute-start | bytes 344072 | tf_op jit(solution)/shard_map/ppermute | solution.py:63

commit v4 on v3

--- a/solution.py
+++ b/solution.py
@@ -19,7 +19,7 @@
 VMEM_BYTES = 20 * 2**20
 F32 = jnp.float32
 BF16 = jnp.bfloat16
-LAST_STEP = F32
+LAST_STEP = BF16
 
 
 def harmonics(x, y, z):
@@ -65,8 +65,7 @@
 
 def beside(block, axis, first):
     count = lax.axis_size(axis)
-    start = 0 if first else 1
-    pairs = [(i, i + 1) for i in range(start, count - 1, 2)]
+    pairs = [(i, (i + 1) % count) for i in range(0 if first else 1, count, 2)]
     return lax.ppermute(block, axis, pairs + [(j, i) for i, j in pairs])
 
 
@@ -77,11 +76,15 @@
 
 
 def geometry_kernel(slots, atoms, edge, plane, place_ref, *refs):
-    info = refs[:plane]
+    rows_of = (refs[0].shape[0] - HARM * edge) // 3
+    info = [
+        sum(ref[HARM * edge + i * rows_of : HARM * edge + (i + 1) * rows_of, :].astype(F32) for i in range(3))
+        for ref in refs[:plane]
+    ]
     lhs_ref, coef_ref, harm_ref, column_ref, target_ref = refs[plane:]
 
     def rows(first):
-        return jnp.concatenate([ref[first * slots : (first + 1) * slots, :] for ref in info], axis=1)
+        return jnp.concatenate([x[first * slots : (first + 1) * slots, :] for x in info], axis=1)
 
     harm, r2 = harmonics(rows(0), rows(1), rows(2))
     for lm in range(1, HARM):
@@ -109,12 +112,17 @@
     coef_ref, harm_ref, column_ref, mix_ref, gate_ref, out_w_ref = refs[2 * plane : 2 * plane + 6]
     feats_ref, mixed_ref, gates_ref, msg_ref, dens_ref, source_ref = refs[2 * plane + 6 :]
     atoms = wide[0].shape[1]
-    edge = faces[0].shape[1]
+    edge = (feats_ref.shape[1] - plane * atoms) // plane
+    face = edge // 2
     total = plane * (atoms + edge)
     part = mix_ref.shape[1] // 2
     for j in range(plane):
         feats_ref[:, j * atoms : (j + 1) * atoms, :] = wide[j][...]
-        feats_ref[:, plane * atoms + j * edge : plane * atoms + (j + 1) * edge, :] = faces[j][...]
+        for side in range(2):
+            at = plane * atoms + j * edge + side * face
+            for lm in range(HARM):
+                first = (side * HARM + lm) * face
+                feats_ref[lm, at : at + face, :] = faces[j][first : first + face, :]
     gates_ref[...] = jax.nn.sigmoid(dot_lanes(gate_ref[...], feats_ref[0]))
     for lm in range(HARM):
         degree = DEGREE_OF[lm]
@@ -338,7 +346,7 @@
     offset = jnp.where(step == 0, row, jnp.where(step < 0, below, above))
     code = offset * plane + domain % plane
     tail = jnp.concatenate(
-        [nbr_count.astype(F32)[None], target[None], jnp.zeros((slots - 2, probes), F32)], axis=0
+        [nbr_count.astype(F32)[None], target[None], jnp.zeros((2 * slots - 2, probes), F32)], axis=0
     )
     info = jnp.concatenate([pair_vec.reshape(3 * slots, probes), code.astype(F32), tail], axis=0)
 
@@ -346,10 +354,12 @@
     last = atoms - face
     near = beside(lax.dynamic_slice_in_dim(own, (1 - odd) * last, face, 1), "slab", True)
     far = beside(lax.dynamic_slice_in_dim(own, odd * last, face, 1), "slab", False)
-    faces = jnp.concatenate([near, far], axis=1)
-    info, near = lax.optimization_barrier((info, near))
+    high = lax.reduce_precision(info, 8, 7)
+    middle = lax.reduce_precision(info - high, 8, 7)
+    parts = [x.astype(BF16) for x in (high, middle, info - high - middle)]
+    near, far = near.reshape(-1, channels), far.reshape(-1, channels)
+    faces = jnp.concatenate([near, far, *parts], axis=0)
     bits = [1 << b for b in reversed(range((plane - 1).bit_length()))]
-    infos = [info] + [partner(info, "xy", j) for j in range(1, plane)]
     held = {0: (own, faces)}
     for bit in bits:
         for j in list(held):
@@ -383,7 +393,7 @@
         ),
         [],
         place,
-        *infos,
+        *[p[1] for p in pieces],
         radial_lhs,
     )
     feats, mixed, gates, message, dens = call(

time: 61.9 us -> 58.6 us (0.947)
  starting transfers between devices: 26.2 us -> 20 us
  local copies, waits for them, and re-layouts: 3.52 us -> 4.93 us
  waiting for transfers between devices: 20.2 us -> 21.5 us
    ppermute x21 -> x18, starting transfers between devices: 18.8 us -> 11.4 us  [partner(): return lax.ppermute(block, axis, [(i, i ^ bit) for i in range(count)])]
    concatenate x1, local copies, waits for them, and re-layouts: 0.02 us -> 1.44 us  [body(): jnp.concatenate([pair_vec.reshape(3 * slots, probes), code.astype(F32), t...]
    ppermute x21 -> x18, waiting for transfers between devices: 19.3 us -> 20.5 us  [partner(): return lax.ppermute(block, axis, [(i, i ^ bit) for i in range(count)])]
    ppermute x4, starting transfers between devices: 7.43 us -> 8.61 us  [beside(): return lax.ppermute(block, axis, pairs + [(j, i) for i, j in pairs])]
    dynamic_slice x1, local copies, waits for them, and re-layouts: 1 us -> 0.1 us  [body(): mix_part = lax.dynamic_slice_in_dim(mix_weight, first, part, axis=2)]
    dynamic_slice x1, local copies, waits for them, and re-layouts: 0.02 us -> 0.88 us  [body(): lax.dynamic_slice_in_dim(own, odd * last, face, 1)]
    unnamed x18 -> x15, local copies, waits for them, and re-layouts: 1.4 us -> 1.4 us
  transfers between devices with their start and end apart: 25 -> 22, of which waited for: 12 -> 11; matrix products, arithmetic and copies ran while one was open for 7% -> 9% of each run, Pallas kernels for 4% -> 4%
where the time goes in v4:
time: 58.6 us; the launch traced here: 58.3 us
  waiting for transfers between devices  21.5 us (37%)
  starting transfers between devices  20 us (34%)
  Pallas kernels  9.24 us (16%)
  local copies, waits for them, and re-layouts  4.93 us (8%)
  other arithmetic  1.73 us (3%)
  between operations  0.93 us (2%)
    ppermute x18, waiting for transfers between devices, partner(): return lax.ppermute(block, axis, [(i, i ^ bit) for i in range(count)])  20.5 us
    ppermute x18, starting transfers between devices, partner(): return lax.ppermute(block, axis, [(i, i ^ bit) for i in range(count)])  11.4 us
    pallas_call x5, Pallas kernels, call(): pl.pallas_call(kernel, out_shape=outs, in_specs=[smem if x.shape == (1,)...  9.24 us
    ppermute x4, starting transfers between devices, beside(): return lax.ppermute(block, axis, pairs + [(j, i) for i, j in pairs])  8.61 us
    concatenate x1, local copies, waits for them, and re-layouts, body(): jnp.concatenate([pair_vec.reshape(3 * slots, probes), code.astype(F32), t...  1.44 us
    unnamed x15, local copies, waits for them, and re-layouts  1.4 us
  transfers between devices with their start and end apart: 22, of which 11 were waited for; matrix products, arithmetic and copies ran while one was open for 9% of the time, Pallas kernels for 4%

profile of v4, /device:TPU:0, one launch (start us, length us, event | category | flops | bytes accessed | tf_op | source)
XLA Modules:
  0.0 58.3 jit_solution(14642111414930284305)
XLA Ops:
  0.6 0.0 copy-start
  0.7 1.1 %copy.36 = bf16[64,16,128]{2,0,1:T(8,128)(2,1)S(1)} copy(bf16[64,16,128]{2,1,0:T(8,128)(2,1)} %param.9) | data formatting | bytes 524288 | tf_op args[0]
  1.8 3.0 %collective-permute-start.1 = (bf16[16,64,128]{2,1,0:T(8,128)(2,1)S(1)}, bf16[16,64,128]{2,1,0:T(8,128)(2,1)S(1)}, u32[]{:S(2)}, u32[]{:S(2)}) collective-permute-start(bf16[16,64,128]{2,1,0:T(8,128)(2,1)S(1)} %bitcast.53), channel_id=1, source_target_pairs={{0,2},{1,3},{2,0},{3,1},{4,6},{5,7},{6,4},{7,5},{8,10},{9,11},{10,... | collective-permute-start | bytes 786440 | tf_op jit(solution)/shard_map/ppermute | solution.py:63
  4.8 0.9 %dynamic-slice_bitcast_fusion = (bf16[16,16,128]{2,0,1:T(8,128)(2,1)S(1)}, bf16[16,16,128]{2,0,1:T(8,128)(2,1)S(1)}) fusion(bf16[64,16,128]{2,1,0:T(8,128)(2,1)} %param.9, s32[]{:T(128)S(6)} %select_n.45, s32[]{:T(128)S(6)} %select_n.44), kind=kLoop, calls=%fused_computation.9 | loop fusion | bytes 262152 | tf_op jit(solution)/shard_map/dynamic_slice | solution.py:356
  5.7 4.6 %collective-permute-start.4 = (bf16[16,16,128]{2,0,1:T(8,128)(2,1)S(1)}, bf16[16,16,128]{2,0,1:T(8,128)(2,1)S(1)}, u32[]{:S(2)}, u32[]{:S(2)}) collective-permute-start(bf16[16,16,128]{2,0,1:T(8,128)(2,1)S(1)} %get-tuple-element.58), channel_id=1, source_target_pairs={{4,8},{12,16},{20,24},{28,0},{8,4},{16,12},{24,20},{0,28},{5,9},{1... | collective-permute-start | bytes 196616 | tf_op jit(solution)/shard_map/ppermute | solution.py:69
  10.3 0.1 constant_dynamic-slice_fusion.2
  10.4 0.1 reshape.70
  10.5 0.1 fusion
  10.5 0.2 multiply_convert_fusion
  10.7 0.7 %fusion.7 = f32[8,128]{1,0:T(8,128)S(1)} fusion(s32[8,128]{1,0:T(8,128)} %param.15, s32[]{:T(128)S(6)} %add.76, s32[]{:T(128)S(6)} %add.73, s32[]{:T(128)S(6)} %axis_index.23), kind=kLoop, calls=%fused_computation.44 | loop fusion | flops 50176 | bytes 8204 | tf_op jit(solution)/shard_map/convert_element_type | solution.py:351
  11.4 0.7 %convert_bitcast_fusion = f32[1,128]{1,0:T(1,128)S(1)} fusion(s32[128]{0:T(128)} %param.16), kind=kLoop, calls=%fused_computation.58 | loop fusion | flops 128 | bytes 1024 | tf_op jit(solution)/shard_map/broadcast_in_dim | solution.py:349
  12.1 1.4 %concatenate.9 = f32[48,128]{1,0:T(8,128)S(1)} concatenate(f32[24,128]{1,0:T(8,128)} %bitcast.65, f32[8,128]{1,0:T(8,128)S(1)} %fusion.7, f32[1,128]{1,0:T(1,128)S(1)} %convert_bitcast_fusion, f32[1,128]{1,0:T(1,128)} %bitcast.66, f32[14,128]{1,0:T(8,128)S(1)} %broadcast_in_dim.19), dimensions={0} | concatenate | bytes 49152 | tf_op jit(solution)/shard_map/concatenate | solution.py:351
  13.5 1.0 %collective-permute-done.3 = bf16[16,16,128]{2,0,1:T(8,128)(2,1)S(1)} collective-permute-done((bf16[16,16,128]{2,0,1:T(8,128)(2,1)S(1)}, bf16[16,16,128]{2,0,1:T(8,128)(2,1)S(1)}, u32[]{:S(2)}, u32[]{:S(2)}) %collective-permute-start.3) | collective-permute-done | bytes 65568 | tf_op jit(solution)/shard_map/ppermute | solution.py:69
  14.7 0.6 collective-permute-start.6
  15.2 0.1 constant_dynamic-slice_fusion.1
  15.4 0.1 copy.26
  15.5 0.1 collective-permute-start.2
  15.6 0.5 collective-permute-start.5
  16.1 4.1 %collective-permute-done.6.refs_2_.refs_6_ = bf16[656,128]{1,0:T(8,128)(2,1)S(1)} collective-permute-done((bf16[656,128]{1,0:T(8,128)(2,1)S(1)}, bf16[656,128]{1,0:T(8,128)(2,1)S(1)}, u32[]{:S(2)}, u32[]{:S(2)}) %collective-permute-start.6) | collective-permute-done | bytes 167968 | tf_op jit(solution)/shard_map/ppermute | solution.py:63
  20.2 0.1 dynamic-slice_bitcast_fusion.2
  20.3 0.1 copy.27.refs_13_.refs_12_
  20.4 0.1 copy.30
  20.4 0.1 copy.35
  20.5 0.2 copy.24.refs_4_
  20.8 0.8 %collective-permute-done.7.refs_3_.refs_7_ = bf16[656,128]{1,0:T(8,128)(2,1)S(1)} collective-permute-done((bf16[656,128]{1,0:T(8,128)(2,1)S(1)}, bf16[656,128]{1,0:T(8,128)(2,1)S(1)}, u32[]{:S(2)}, u32[]{:S(2)}) %collective-permute-start.7) | collective-permute-done | bytes 167968 | tf_op jit(solution)/shard_map/ppermute | solution.py:63
  21.6 0.5 shard_map.120
  22.1 3.2 %shard_map.121 = (bf16[16,384,128]{2,1,0:T(8,128)(2,1)S(1)}, f32[512,384]{1,0:T(8,128)S(1)}, f32[96,384]{1,0:T(8,128)S(1)}, f32[32,512]{1,0:T(8,128)S(1)}, f32[8,512]{1,0:T(8,128)S(1)}) custom-call(bf16[16,64,128]{2,1,0:T(8,128)(2,1)S(1)} %bitcast.55, bf16[16,64,128]{2,1,0:T(8,128)(2,1)S(1)} %collective-permute-done.refs_1_, ...), custom_call_target="tpu_custom_call" | custom-call | tf_op jit(solution)/shard_map/pallas_call | solution.py:304
  25.4 0.3 collective-permute-start.10
  25.7 1.5 %collective-permute-start.9 = (f32[8,512]{1,0:T(8,128)S(1)}, f32[8,512]{1,0:T(8,128)S(1)}, u32[]{:S(2)}, u32[]{:S(2)}) collective-permute-start(f32[8,512]{1,0:T(8,128)S(1)} %get-tuple-element.34.refs_0_), channel_id=1, source_target_pairs={{0,2},{1,3},{2,0},{3,1},{4,6},{5,7},{6,4},{7,5},{8,10},{9,11},{10,... | collective-permute-start | bytes 49160 | tf_op jit(solution)/shard_map/ppermute | solution.py:63
  27.2 0.1 collective-permute-start.8
  27.3 1.3 %collective-permute-done.10.refs_3_ = f32[8,512]{1,0:T(8,128)S(1)} collective-permute-done((f32[8,512]{1,0:T(8,128)S(1)}, f32[8,512]{1,0:T(8,128)S(1)}, u32[]{:S(2)}, u32[]{:S(2)}) %collective-permute-start.10) | collective-permute-done | bytes 16416 | tf_op jit(solution)/shard_map/ppermute | solution.py:63
  28.6 0.8 %collective-permute-done.9.refs_2_ = f32[8,512]{1,0:T(8,128)S(1)} collective-permute-done((f32[8,512]{1,0:T(8,128)S(1)}, f32[8,512]{1,0:T(8,128)S(1)}, u32[]{:S(2)}, u32[]{:S(2)}) %collective-permute-start.9) | collective-permute-done | bytes 16416 | tf_op jit(solution)/shard_map/ppermute | solution.py:63
  29.4 2.8 %shard_map.122 = (f32[224,128]{1,0:T(8,128)S(1)}, f32[8,128]{1,0:T(8,128)S(1)}, bf16[96,512]{1,0:T(8,128)(2,1)S(1)}, bf16[96,512]{1,0:T(8,128)(2,1)S(1)}, bf16[192,512]{1,0:T(8,128)(2,1)S(1)}) custom-call(f32[8,512]{1,0:T(8,128)S(1)} %get-tuple-element.34.refs_0_, f32[8,512]{1,0:T(8,128)S(1)} %collective-permute-done.8.refs_1_, ...), custom_call_target="tpu_custom_call" | custom-call | tf_op jit(solution)/shard_map/pallas_call | solution.py:304
  32.3 1.8 %collective-permute-start.11 = (f32[224,128]{1,0:T(8,128)S(1)}, f32[224,128]{1,0:T(8,128)S(1)}, u32[]{:S(2)}, u32[]{:S(2)}) collective-permute-start(f32[224,128]{1,0:T(8,128)S(1)} %get-tuple-element.41), channel_id=1, source_target_pairs={{0,4},{4,0},{8,12},{12,8},{16,20},{20,16},{24,28},{28,24},{1,5},{5... | collective-permute-start | bytes 344072 | tf_op jit(solution)/shard_map/ppermute | solution.py:63
  34.0 1.5 %collective-permute-start.14 = (bf16[192,512]{1,0:T(8,128)(2,1)S(1)}, bf16[192,512]{1,0:T(8,128)(2,1)S(1)}, u32[]{:S(2)}, u32[]{:S(2)}) collective-permute-start(bf16[192,512]{1,0:T(8,128)(2,1)S(1)} %get-tuple-element.44), channel_id=1, source_target_pairs={{0,2},{1,3},{2,0},{3,1},{4,6},{5,7},{6,4},{7,5},{8,10},{9,11},{10,... | collective-permute-start | bytes 589832 | tf_op jit(solution)/shard_map/ppermute | solution.py:63
  35.6 1.5 %collective-permute-done.11 = f32[224,128]{1,0:T(8,128)S(1)} collective-permute-done((f32[224,128]{1,0:T(8,128)S(1)}, f32[224,128]{1,0:T(8,128)S(1)}, u32[]{:S(2)}, u32[]{:S(2)}) %collective-permute-start.11) | collective-permute-done | bytes 114720 | tf_op jit(solution)/shard_map/ppermute | solution.py:63
  37.1 0.4 collective-permute-start.12
  37.6 2.4 %collective-permute-done.14.refs_2_ = bf16[192,512]{1,0:T(8,128)(2,1)S(1)} collective-permute-done((bf16[192,512]{1,0:T(8,128)(2,1)S(1)}, bf16[192,512]{1,0:T(8,128)(2,1)S(1)}, u32[]{:S(2)}, u32[]{:S(2)}) %collective-permute-start.14) | collective-permute-done | bytes 196640 | tf_op jit(solution)/shard_map/ppermute | solution.py:63
  40.0 2.0 %collective-permute-done.12 = f32[224,128]{1,0:T(8,128)S(1)} collective-permute-done((f32[224,128]{1,0:T(8,128)S(1)}, f32[224,128]{1,0:T(8,128)S(1)}, u32[]{:S(2)}, u32[]{:S(2)}) %collective-permute-start.12) | collective-permute-done | bytes 114720 | tf_op jit(solution)/shard_map/ppermute | solution.py:63
  42.1 1.8 %collective-permute-start.17 = (bf16[4,16,512]{2,1,0:T(8,128)(2,1)S(1)}, bf16[4,16,512]{2,1,0:T(8,128)(2,1)S(1)}, u32[]{:S(2)}, u32[]{:S(2)}) collective-permute-start(bf16[4,16,512]{2,1,0:T(8,128)(2,1)S(1)} %pad_maximum_fusion.1), channel_id=1, source_target_pairs={{0,4},{8,12},{16,20},{24,28},{4,0},{12,8},{20,16},{28,24},{1,5},{9... | collective-permute-start | bytes 196616 | tf_op jit(solution)/shard_map/ppermute | solution.py:69
  43.9 2.2 %collective-permute-start.18 = (bf16[4,16,512]{2,1,0:T(8,128)(2,1)S(1)}, bf16[4,16,512]{2,1,0:T(8,128)(2,1)S(1)}, u32[]{:S(2)}, u32[]{:S(2)}) collective-permute-start(bf16[4,16,512]{2,1,0:T(8,128)(2,1)S(1)} %pad_maximum_fusion.2), channel_id=1, source_target_pairs={{4,8},{12,16},{20,24},{28,0},{8,4},{16,12},{24,20},{0,28},{5,9},{1... | collective-permute-start | bytes 196616 | tf_op jit(solution)/shard_map/ppermute | solution.py:69
  46.1 5.1 %collective-permute-done.16 = bf16[224,128]{1,0:T(8,128)(2,1)S(1)} collective-permute-done((bf16[224,128]{1,0:T(8,128)(2,1)S(1)}, bf16[224,128]{1,0:T(8,128)(2,1)S(1)}, u32[]{:S(2)}, u32[]{:S(2)}) %collective-permute-start.16) | collective-permute-done | bytes 57376 | tf_op jit(solution)/shard_map/ppermute | solution.py:63
  51.2 1.6 %collective-permute-start.19 = (f32[224,128]{1,0:T(8,128)S(1)}, f32[224,128]{1,0:T(8,128)S(1)}, u32[]{:S(2)}, u32[]{:S(2)}) collective-permute-start(f32[224,128]{1,0:T(8,128)S(1)} %convert_add_fusion.refs_0_), channel_id=1, source_target_pairs={{0,2},{1,3},{2,0},{3,1},{4,6},{5,7},{6,4},{7,5},{8,10},{9,11},{10,... | collective-permute-start | bytes 344072 | tf_op jit(solution)/shard_map/ppermute | solution.py:63
  52.8 1.7 %shard_map.123 = f32[64,16,128]{2,1,0:T(8,128)} custom-call(s32[1]{0:T(128)} %bitcast.8.place_ref, bf16[96,512]{1,0:T(8,128)(2,1)S(1)} %get-tuple-element.46.refs_0_, bf16[96,512]{1,0:T(8,128)(2,1)S(1)} %collective-permute-done.13.refs_1_, bf16[192,512]{1,0:T(8,128)(2,1)S(1)} %collective-permute-done.14.refs_2_, ...), custom_call_target="tpu_custom_call" | custom-call | tf_op jit(solution)/shard_map/pallas_call | solution.py:304
  54.5 1.5 %collective-permute-done.19.refs_2_ = f32[224,128]{1,0:T(8,128)S(1)} collective-permute-done((f32[224,128]{1,0:T(8,128)S(1)}, f32[224,128]{1,0:T(8,128)S(1)}, u32[]{:S(2)}, u32[]{:S(2)}) %collective-permute-start.19) | collective-permute-done | bytes 114720 | tf_op jit(solution)/shard_map/ppermute | solution.py:63
  56.1 0.5 slice_bitcast_fusion.8
  56.6 0.8 %collective-permute-done.21.refs_3_ = f32[224,128]{1,0:T(8,128)S(1)} collective-permute-done((f32[224,128]{1,0:T(8,128)S(1)}, f32[224,128]{1,0:T(8,128)S(1)}, u32[]{:S(2)}, u32[]{:S(2)}) %collective-permute-start.21) | collective-permute-done | bytes 114720 | tf_op jit(solution)/shard_map/ppermute | solution.py:63
  57.4 0.9 %shard_map.124 = (f32[4,128,128]{2,1,0:T(8,128)}, f32[128,384]{1,0:T(8,128)}) custom-call(s32[1]{0:T(128)} %bitcast.8.place_ref, f32[224,128]{1,0:T(8,128)S(1)} %convert_add_fusion.refs_0_, f32[224,128]{1,0:T(8,128)S(1)} %collective-permute-done.20.refs_1_, f32[224,128]{1,0:T(8,128)S(1)} %collective-permute-done.19.refs_2_, ...), custom_call_target="tpu_custom_call" | custom-call | tf_op jit(solution)/shard_map/pallas_call | solution.py:304
  (48 shorter events, 0.3 us)
Async XLA Ops:
  0.6 9.7 %copy-start = (f32[8,512]{1,0:T(8,128)S(1)}, f32[8,512]{1,0:T(8,128)}, u32[]{:S(2)}) copy-start(f32[8,512]{1,0:T(8,128)} %param.12) | copy-start | bytes 49156
  0.6 14.6 %copy-start.1 = (bf16[4,128,128]{2,1,0:T(8,128)(2,1)S(1)}, bf16[4,128,128]{2,1,0:T(8,128)(2,1)}, u32[]{:S(2)}) copy-start(bf16[4,128,128]{2,1,0:T(8,128)(2,1)} %refs_7_.1) | copy-start | bytes 393220
  0.7 14.7 %copy-start.2 = (bf16[128,384]{1,0:T(8,128)(2,1)S(1)}, bf16[128,384]{1,0:T(8,128)(2,1)}, u32[]{:S(2)}) copy-start(bf16[128,384]{1,0:T(8,128)(2,1)} %refs_8_.1) | copy-start | bytes 294916
  0.7 19.5 %copy-start.3 = (f32[128]{0:T(128)S(1)}, f32[128]{0:T(128)}, u32[]{:S(2)}) copy-start(f32[128]{0:T(128)} %param.13) | copy-start | bytes 1540
  1.8 13.7 %collective-permute-start.1 = (bf16[16,64,128]{2,1,0:T(8,128)(2,1)S(1)}, bf16[16,64,128]{2,1,0:T(8,128)(2,1)S(1)}, u32[]{:S(2)}, u32[]{:S(2)}) collective-permute-start(bf16[16,64,128]{2,1,0:T(8,128)(2,1)S(1)} %bitcast.53), channel_id=1, source_target_pairs={{0,2},{1,3},{2,0},{3,1},{4,6},{5,7},{6,4},{7,5},{8,10},{9,11},{10,... | collective-permute-start | bytes 786440 | tf_op jit(solution)/shard_map/ppermute | solution.py:63
  4.8 17.3 %collective-permute-start = (bf16[16,64,128]{2,1,0:T(8,128)(2,1)S(1)}, bf16[16,64,128]{2,1,0:T(8,128)(2,1)S(1)}, u32[]{:S(2)}, u32[]{:S(2)}) collective-permute-start(bf16[16,64,128]{2,1,0:T(8,128)(2,1)S(1)} %bitcast.54), channel_id=1, source_target_pairs={{0,1},{1,0},{2,3},{3,2},{4,5},{5,4},{6,7},{7,6},{8,9},{9,8},{10,11... | collective-permute-start | bytes 786440 | tf_op jit(solution)/shard_map/ppermute | solution.py:63
  5.7 8.9 %collective-permute-start.4 = (bf16[16,16,128]{2,0,1:T(8,128)(2,1)S(1)}, bf16[16,16,128]{2,0,1:T(8,128)(2,1)S(1)}, u32[]{:S(2)}, u32[]{:S(2)}) collective-permute-start(bf16[16,16,128]{2,0,1:T(8,128)(2,1)S(1)} %get-tuple-element.58), channel_id=1, source_target_pairs={{4,8},{12,16},{20,24},{28,0},{8,4},{16,12},{24,20},{0,28},{5,9},{1... | collective-permute-start | bytes 196616 | tf_op jit(solution)/shard_map/ppermute | solution.py:69
  10.3 4.3 %collective-permute-start.3 = (bf16[16,16,128]{2,0,1:T(8,128)(2,1)S(1)}, bf16[16,16,128]{2,0,1:T(8,128)(2,1)S(1)}, u32[]{:S(2)}, u32[]{:S(2)}) collective-permute-start(bf16[16,16,128]{2,0,1:T(8,128)(2,1)S(1)} %get-tuple-element.59), channel_id=1, source_target_pairs={{0,4},{8,12},{16,20},{24,28},{4,0},{12,8},{20,16},{28,24},{1,5},{9... | collective-permute-start | bytes 196616 | tf_op jit(solution)/shard_map/ppermute | solution.py:69
  14.7 5.5 %collective-permute-start.6 = (bf16[656,128]{1,0:T(8,128)(2,1)S(1)}, bf16[656,128]{1,0:T(8,128)(2,1)S(1)}, u32[]{:S(2)}, u32[]{:S(2)}) collective-permute-start(bf16[656,128]{1,0:T(8,128)(2,1)S(1)} %fusion.2.refs_0_.refs_4_), channel_id=1, source_target_pairs={{0,2},{1,3},{2,0},{3,1},{4,6},{5,7},{6,4},{7,5},{8,10},{9,11},{10,... | collective-permute-start | bytes 503816 | tf_op jit(solution)/shard_map/ppermute | solution.py:63
  15.5 6.6 %collective-permute-start.2 = (bf16[16,64,128]{2,1,0:T(8,128)(2,1)S(1)}, bf16[16,64,128]{2,1,0:T(8,128)(2,1)S(1)}, u32[]{:S(2)}, u32[]{:S(2)}) collective-permute-start(bf16[16,64,128]{2,1,0:T(8,128)(2,1)S(1)} %collective-permute-done.1.refs_2_), channel_id=1, source_target_pairs={{0,1},{1,0},{2,3},{3,2},{4,5},{5,4},{6,7},{7,6},{8,9},{9,8},{10,11... | collective-permute-start | bytes 786440 | tf_op jit(solution)/shard_map/ppermute | solution.py:63
  15.6 5.1 %collective-permute-start.5 = (bf16[656,128]{1,0:T(8,128)(2,1)S(1)}, bf16[656,128]{1,0:T(8,128)(2,1)S(1)}, u32[]{:S(2)}, u32[]{:S(2)}) collective-permute-start(bf16[656,128]{1,0:T(8,128)(2,1)S(1)} %fusion.2.refs_0_.refs_4_), channel_id=1, source_target_pairs={{0,1},{1,0},{2,3},{3,2},{4,5},{5,4},{6,7},{7,6},{8,9},{9,8},{10,11... | collective-permute-start | bytes 503816 | tf_op jit(solution)/shard_map/ppermute | solution.py:63
  20.2 1.4 %collective-permute-start.7 = (bf16[656,128]{1,0:T(8,128)(2,1)S(1)}, bf16[656,128]{1,0:T(8,128)(2,1)S(1)}, u32[]{:S(2)}, u32[]{:S(2)}) collective-permute-start(bf16[656,128]{1,0:T(8,128)(2,1)S(1)} %collective-permute-done.6.refs_2_.refs_6_), channel_id=1, source_target_pairs={{0,1},{1,0},{2,3},{3,2},{4,5},{5,4},{6,7},{7,6},{8,9},{9,8},{10,11... | collective-permute-start | bytes 503816 | tf_op jit(solution)/shard_map/ppermute | solution.py:63
  25.4 3.2 %collective-permute-start.10 = (f32[8,512]{1,0:T(8,128)S(1)}, f32[8,512]{1,0:T(8,128)S(1)}, u32[]{:S(2)}, u32[]{:S(2)}) collective-permute-start(f32[8,512]{1,0:T(8,128)S(1)} %get-tuple-element.34.refs_0_), channel_id=1, source_target_pairs={{0,3},{1,2},{2,1},{3,0},{4,7},{5,6},{6,5},{7,4},{8,11},{9,10},{10,... | collective-permute-start | bytes 49160 | tf_op jit(solution)/shard_map/ppermute | solution.py:63
  25.7 3.8 %collective-permute-start.9 = (f32[8,512]{1,0:T(8,128)S(1)}, f32[8,512]{1,0:T(8,128)S(1)}, u32[]{:S(2)}, u32[]{:S(2)}) collective-permute-start(f32[8,512]{1,0:T(8,128)S(1)} %get-tuple-element.34.refs_0_), channel_id=1, source_target_pairs={{0,2},{1,3},{2,0},{3,1},{4,6},{5,7},{6,4},{7,5},{8,10},{9,11},{10,... | collective-permute-start | bytes 49160 | tf_op jit(solution)/shard_map/ppermute | solution.py:63
  27.2 2.2 %collective-permute-start.8 = (f32[8,512]{1,0:T(8,128)S(1)}, f32[8,512]{1,0:T(8,128)S(1)}, u32[]{:S(2)}, u32[]{:S(2)}) collective-permute-start(f32[8,512]{1,0:T(8,128)S(1)} %get-tuple-element.34.refs_0_), channel_id=1, source_target_pairs={{0,1},{1,0},{2,3},{3,2},{4,5},{5,4},{6,7},{7,6},{8,9},{9,8},{10,11... | collective-permute-start | bytes 49160 | tf_op jit(solution)/shard_map/ppermute | solution.py:63
  32.3 4.8 %collective-permute-start.11 = (f32[224,128]{1,0:T(8,128)S(1)}, f32[224,128]{1,0:T(8,128)S(1)}, u32[]{:S(2)}, u32[]{:S(2)}) collective-permute-start(f32[224,128]{1,0:T(8,128)S(1)} %get-tuple-element.41), channel_id=1, source_target_pairs={{0,4},{4,0},{8,12},{12,8},{16,20},{20,16},{24,28},{28,24},{1,5},{5... | collective-permute-start | bytes 344072 | tf_op jit(solution)/shard_map/ppermute | solution.py:63
  34.0 5.9 %collective-permute-start.14 = (bf16[192,512]{1,0:T(8,128)(2,1)S(1)}, bf16[192,512]{1,0:T(8,128)(2,1)S(1)}, u32[]{:S(2)}, u32[]{:S(2)}) collective-permute-start(bf16[192,512]{1,0:T(8,128)(2,1)S(1)} %get-tuple-element.44), channel_id=1, source_target_pairs={{0,2},{1,3},{2,0},{3,1},{4,6},{5,7},{6,4},{7,5},{8,10},{9,11},{10,... | collective-permute-start | bytes 589832 | tf_op jit(solution)/shard_map/ppermute | solution.py:63
  37.1 4.9 %collective-permute-start.12 = (f32[224,128]{1,0:T(8,128)S(1)}, f32[224,128]{1,0:T(8,128)S(1)}, u32[]{:S(2)}, u32[]{:S(2)}) collective-permute-start(f32[224,128]{1,0:T(8,128)S(1)} %add.85), channel_id=1, source_target_pairs={{0,8},{4,12},{8,0},{12,4},{16,24},{20,28},{24,16},{28,20},{1,9},{5... | collective-permute-start | bytes 344072 | tf_op jit(solution)/shard_map/ppermute | solution.py:63
  37.6 4.4 %collective-permute-start.13 = (bf16[96,512]{1,0:T(8,128)(2,1)S(1)}, bf16[96,512]{1,0:T(8,128)(2,1)S(1)}, u32[]{:S(2)}, u32[]{:S(2)}) collective-permute-start(bf16[96,512]{1,0:T(8,128)(2,1)S(1)} %get-tuple-element.43), channel_id=1, source_target_pairs={{0,1},{1,0},{2,3},{3,2},{4,5},{5,4},{6,7},{7,6},{8,9},{9,8},{10,11... | collective-permute-start | bytes 294920 | tf_op jit(solution)/shard_map/ppermute | solution.py:63
  40.0 2.1 %collective-permute-start.15 = (bf16[192,512]{1,0:T(8,128)(2,1)S(1)}, bf16[192,512]{1,0:T(8,128)(2,1)S(1)}, u32[]{:S(2)}, u32[]{:S(2)}) collective-permute-start(bf16[192,512]{1,0:T(8,128)(2,1)S(1)} %collective-permute-done.14.refs_2_), channel_id=1, source_target_pairs={{0,1},{1,0},{2,3},{3,2},{4,5},{5,4},{6,7},{7,6},{8,9},{9,8},{10,11... | collective-permute-start | bytes 589832 | tf_op jit(solution)/shard_map/ppermute | solution.py:63
  42.1 9.1 %collective-permute-start.17 = (bf16[4,16,512]{2,1,0:T(8,128)(2,1)S(1)}, bf16[4,16,512]{2,1,0:T(8,128)(2,1)S(1)}, u32[]{:S(2)}, u32[]{:S(2)}) collective-permute-start(bf16[4,16,512]{2,1,0:T(8,128)(2,1)S(1)} %pad_maximum_fusion.1), channel_id=1, source_target_pairs={{0,4},{8,12},{16,20},{24,28},{4,0},{12,8},{20,16},{28,24},{1,5},{9... | collective-permute-start | bytes 196616 | tf_op jit(solution)/shard_map/ppermute | solution.py:69
  43.9 7.3 %collective-permute-start.18 = (bf16[4,16,512]{2,1,0:T(8,128)(2,1)S(1)}, bf16[4,16,512]{2,1,0:T(8,128)(2,1)S(1)}, u32[]{:S(2)}, u32[]{:S(2)}) collective-permute-start(bf16[4,16,512]{2,1,0:T(8,128)(2,1)S(1)} %pad_maximum_fusion.2), channel_id=1, source_target_pairs={{4,8},{12,16},{20,24},{28,0},{8,4},{16,12},{24,20},{0,28},{5,9},{1... | collective-permute-start | bytes 196616 | tf_op jit(solution)/shard_map/ppermute | solution.py:69
  46.1 5.1 %collective-permute-start.16 = (bf16[224,128]{1,0:T(8,128)(2,1)S(1)}, bf16[224,128]{1,0:T(8,128)(2,1)S(1)}, u32[]{:S(2)}, u32[]{:S(2)}) collective-permute-start(bf16[224,128]{1,0:T(8,128)(2,1)S(1)} %add_convert_fusion), channel_id=1, source_target_pairs={{0,16},{4,20},{8,24},{12,28},{16,0},{20,4},{24,8},{28,12},{1,17},{... | collective-permute-start | bytes 172040 | tf_op jit(solution)/shard_map/ppermute | solution.py:63
  51.2 4.9 %collective-permute-start.19 = (f32[224,128]{1,0:T(8,128)S(1)}, f32[224,128]{1,0:T(8,128)S(1)}, u32[]{:S(2)}, u32[]{:S(2)}) collective-permute-start(f32[224,128]{1,0:T(8,128)S(1)} %convert_add_fusion.refs_0_), channel_id=1, source_target_pairs={{0,2},{1,3},{2,0},{3,1},{4,6},{5,7},{6,4},{7,5},{8,10},{9,11},{10,... | collective-permute-start | bytes 344072 | tf_op jit(solution)/shard_map/ppermute | solution.py:63
  52.8 3.8 %collective-permute-start.20 = (f32[224,128]{1,0:T(8,128)S(1)}, f32[224,128]{1,0:T(8,128)S(1)}, u32[]{:S(2)}, u32[]{:S(2)}) collective-permute-start(f32[224,128]{1,0:T(8,128)S(1)} %convert_add_fusion.refs_0_), channel_id=1, source_target_pairs={{0,1},{1,0},{2,3},{3,2},{4,5},{5,4},{6,7},{7,6},{8,9},{9,8},{10,11... | collective-permute-start | bytes 344072 | tf_op jit(solution)/shard_map/ppermute | solution.py:63
  56.1 1.3 %collective-permute-start.21 = (f32[224,128]{1,0:T(8,128)S(1)}, f32[224,128]{1,0:T(8,128)S(1)}, u32[]{:S(2)}, u32[]{:S(2)}) collective-permute-start(f32[224,128]{1,0:T(8,128)S(1)} %collective-permute-done.19.refs_2_), channel_id=1, source_target_pairs={{0,1},{1,0},{2,3},{3,2},{4,5},{5,4},{6,7},{7,6},{8,9},{9,8},{10,11... | collective-permute-start | bytes 344072 | tf_op jit(solution)/shard_map/ppermute | solution.py:63

commit v5 on v4

--- a/solution.py
+++ b/solution.py
@@ -19,7 +19,6 @@
 VMEM_BYTES = 20 * 2**20
 F32 = jnp.float32
 BF16 = jnp.bfloat16
-LAST_STEP = BF16
 
 
 def harmonics(x, y, z):
@@ -61,6 +60,12 @@
 def partner(block, axis, bit):
     count = lax.axis_size(axis)
     return lax.ppermute(block, axis, [(i, i ^ bit) for i in range(count)])
+
+
+def inner(block, axis):
+    count = lax.axis_size(axis)
+    pairs = [(i, i + 1) for i in range(1, count - 1, 2)]
+    return lax.ppermute(block, axis, pairs + [(j, i) for i, j in pairs])
 
 
 def beside(block, axis, first):
@@ -452,16 +457,33 @@
     mine = {source: (block, places[0]) for source, block, places in entries if 0 in places}
     slices = [mine[j][0] for j in range(plane)]
     firsts = tuple(mine[j][1] for j in range(plane))
-    for bit in steps[:-1]:
+    for bit in steps[:-2]:
         weight = weight + partner(weight, "slab", bit)
-    weight = weight.astype(LAST_STEP)
-    weight, *slices = lax.optimization_barrier((weight, *slices))
-    weight = (weight, partner(weight, "slab", steps[-1]))
+    weight = weight.astype(BF16)
+    one, two = steps[-2:]
+    weight = [weight] + [partner(weight, "slab", bit) for bit in (one, two, one + two)]
+    *weight, last_slice = lax.optimization_barrier((*weight, slices[-1]))
+    slices = slices[:-1] + [last_slice]
     edges = [s[f + atoms : f + size] for s, f in zip(slices, firsts)]
     near_grad = beside(jnp.stack([e[:face] for e in edges], axis=0), "slab", True)
-    far_grad = beside(jnp.stack([e[face:] for e in edges], axis=0), "slab", False)
-    *weight, near_grad, far_grad = lax.optimization_barrier((*weight, near_grad, far_grad))
-    weight = weight[0].astype(F32) + weight[1].astype(F32)
+    far_grad = inner(jnp.stack([e[face:] for e in edges], axis=0), "slab")
+    near_sum = weight[0].astype(F32) + weight[1].astype(F32)
+    weight = near_sum + (weight[2].astype(F32) + weight[3].astype(F32))
+    columns = {0: weight}
+    for bit in bits:
+        arrived = {j ^ bit: partner(columns[j], "xy", bit) for j in columns}
+        columns.update(arrived)
+    mix_grad, gate_grad = call(
+        functools.partial(assemble_kernel, plane),
+        (
+            jax.ShapeDtypeStruct((4, channels, channels), F32),
+            jax.ShapeDtypeStruct((channels, 3 * channels), F32),
+        ),
+        [pltpu.VMEM((7, channels, channels), F32)],
+        place,
+        *[columns[j] for j in range(plane)],
+    )
+    mix_grad, gate_grad, near_grad, far_grad = lax.optimization_barrier((mix_grad, gate_grad, near_grad, far_grad))
     feat_grad = call(
         functools.partial(finish_kernel, plane, firsts),
         jax.ShapeDtypeStruct((atoms, harm_count, channels), F32),
@@ -474,24 +496,6 @@
         mix_weight,
         gate_weight,
     )
-
-    columns = {0: weight}
-    for bit in bits:
-        arrived = {j ^ bit: partner(columns[j], "xy", bit) for j in columns}
-        if bit == bits[0]:
-            *values, feat_grad = lax.optimization_barrier((*arrived.values(), feat_grad))
-            arrived = dict(zip(arrived, values))
-        columns.update(arrived)
-    mix_grad, gate_grad = call(
-        functools.partial(assemble_kernel, plane),
-        (
-            jax.ShapeDtypeStruct((4, channels, channels), F32),
-            jax.ShapeDtypeStruct((channels, 3 * channels), F32),
-        ),
-        [pltpu.VMEM((7, channels, channels), F32)],
-        place,
-        *[columns[j] for j in range(plane)],
-    )
     return (density[0], feat_grad, mix_grad, gate_grad)
 
 

time: 58.6 us -> 56.1 us (0.957)
  the two profiles are of different devices: /device:TPU:0 before, /device:TPU:8 now
where the time goes in v5:
time: 56.1 us; the launch traced here: 55.8 us
  starting transfers between devices  21.3 us (38%)
  waiting for transfers between devices  17.6 us (31%)
  Pallas kernels  9.23 us (16%)
  local copies, waits for them, and re-layouts  4.93 us (9%)
  other arithmetic  1.74 us (3%)
  between operations  0.92 us (2%)
    ppermute x19, waiting for transfers between devices, partner(): return lax.ppermute(block, axis, [(i, i ^ bit) for i in range(count)])  15.2 us
    ppermute x19, starting transfers between devices, partner(): return lax.ppermute(block, axis, [(i, i ^ bit) for i in range(count)])  13.6 us
    pallas_call x5, Pallas kernels, call(): pl.pallas_call(kernel, out_shape=outs, in_specs=[smem if x.shape == (1,)...  9.23 us
    ppermute x3, starting transfers between devices, beside(): return lax.ppermute(block, axis, pairs + [(j, i) for i, j in pairs])  4.9 us
    ppermute x1, starting transfers between devices, inner(): return lax.ppermute(block, axis, pairs + [(j, i) for i, j in pairs])  2.82 us
    ppermute x1, waiting for transfers between devices, inner(): return lax.ppermute(block, axis, pairs + [(j, i) for i, j in pairs])  1.89 us
    concatenate x1, local copies, waits for them, and re-layouts, body(): jnp.concatenate([pair_vec.reshape(3 * slots, probes), code.astype(F32), t...  1.44 us
    unnamed x15, local copies, waits for them, and re-layouts  1.4 us
  transfers between devices with their start and end apart: 23, of which 11 were waited for; matrix products, arithmetic and copies ran while one was open for 10% of the time, Pallas kernels for 3%

profile of v5, /device:TPU:8, one launch (start us, length us, event | category | flops | bytes accessed | tf_op | source)
XLA Modules:
  0.0 55.8 jit_solution(5133718794316934164)
XLA Ops:
  0.7 1.1 %copy.36 = bf16[64,16,128]{2,0,1:T(8,128)(2,1)S(1)} copy(bf16[64,16,128]{2,1,0:T(8,128)(2,1)} %param.9) | data formatting | bytes 524288 | tf_op args[0]
  1.8 1.6 %collective-permute-start.1 = (bf16[16,64,128]{2,1,0:T(8,128)(2,1)S(1)}, bf16[16,64,128]{2,1,0:T(8,128)(2,1)S(1)}, u32[]{:S(2)}, u32[]{:S(2)}) collective-permute-start(bf16[16,64,128]{2,1,0:T(8,128)(2,1)S(1)} %bitcast.53), channel_id=1, source_target_pairs={{0,2},{1,3},{2,0},{3,1},{4,6},{5,7},{6,4},{7,5},{8,10},{9,11},{10,... | collective-permute-start | bytes 786440 | tf_op jit(solution)/shard_map/ppermute | solution.py:62
  3.3 0.9 %dynamic-slice_bitcast_fusion = (bf16[16,16,128]{2,0,1:T(8,128)(2,1)S(1)}, bf16[16,16,128]{2,0,1:T(8,128)(2,1)S(1)}) fusion(bf16[64,16,128]{2,1,0:T(8,128)(2,1)} %param.9, s32[]{:T(128)S(6)} %select_n.45, s32[]{:T(128)S(6)} %select_n.44), kind=kLoop, calls=%fused_computation.9 | loop fusion | bytes 262152 | tf_op jit(solution)/shard_map/dynamic_slice | solution.py:361
  4.2 1.4 %collective-permute-start.4 = (bf16[16,16,128]{2,0,1:T(8,128)(2,1)S(1)}, bf16[16,16,128]{2,0,1:T(8,128)(2,1)S(1)}, u32[]{:S(2)}, u32[]{:S(2)}) collective-permute-start(bf16[16,16,128]{2,0,1:T(8,128)(2,1)S(1)} %get-tuple-element.54), channel_id=1, source_target_pairs={{4,8},{12,16},{20,24},{28,0},{8,4},{16,12},{24,20},{0,28},{5,9},{1... | collective-permute-start | bytes 196616 | tf_op jit(solution)/shard_map/ppermute | solution.py:74
  5.7 1.7 %collective-permute-start.3 = (bf16[16,16,128]{2,0,1:T(8,128)(2,1)S(1)}, bf16[16,16,128]{2,0,1:T(8,128)(2,1)S(1)}, u32[]{:S(2)}, u32[]{:S(2)}) collective-permute-start(bf16[16,16,128]{2,0,1:T(8,128)(2,1)S(1)} %get-tuple-element.55), channel_id=1, source_target_pairs={{0,4},{8,12},{16,20},{24,28},{4,0},{12,8},{20,16},{28,24},{1,5},{9... | collective-permute-start | bytes 196616 | tf_op jit(solution)/shard_map/ppermute | solution.py:74
  7.3 0.1 constant_dynamic-slice_fusion.2
  7.4 0.1 reshape.70
  7.5 0.1 fusion
  7.6 0.2 multiply_convert_fusion
  7.8 0.7 %fusion.7 = f32[8,128]{1,0:T(8,128)S(1)} fusion(s32[8,128]{1,0:T(8,128)} %param.15, s32[]{:T(128)S(6)} %add.79, s32[]{:T(128)S(6)} %add.76, s32[]{:T(128)S(6)} %axis_index.23), kind=kLoop, calls=%fused_computation.44 | loop fusion | flops 50176 | bytes 8204 | tf_op jit(solution)/shard_map/convert_element_type | solution.py:356
  8.5 0.7 %convert_bitcast_fusion = f32[1,128]{1,0:T(1,128)S(1)} fusion(s32[128]{0:T(128)} %param.16), kind=kLoop, calls=%fused_computation.58 | loop fusion | flops 128 | bytes 1024 | tf_op jit(solution)/shard_map/broadcast_in_dim | solution.py:354
  9.1 1.4 %concatenate.9 = f32[48,128]{1,0:T(8,128)S(1)} concatenate(f32[24,128]{1,0:T(8,128)} %bitcast.65, f32[8,128]{1,0:T(8,128)S(1)} %fusion.7, f32[1,128]{1,0:T(1,128)S(1)} %convert_bitcast_fusion, f32[1,128]{1,0:T(1,128)} %bitcast.66, f32[14,128]{1,0:T(8,128)S(1)} %broadcast_in_dim.19), dimensions={0} | concatenate | bytes 49152 | tf_op jit(solution)/shard_map/concatenate | solution.py:356
  10.6 0.5 collective-permute-done.3
  11.2 0.6 %collective-permute-start.6 = (bf16[656,128]{1,0:T(8,128)(2,1)S(1)}, bf16[656,128]{1,0:T(8,128)(2,1)S(1)}, u32[]{:S(2)}, u32[]{:S(2)}) collective-permute-start(bf16[656,128]{1,0:T(8,128)(2,1)S(1)} %fusion.2.refs_0_.refs_4_), channel_id=1, source_target_pairs={{0,2},{1,3},{2,0},{3,1},{4,6},{5,7},{6,4},{7,5},{8,10},{9,11},{10,... | collective-permute-start | bytes 503816 | tf_op jit(solution)/shard_map/ppermute | solution.py:62
  11.8 0.1 constant_dynamic-slice_fusion.1
  11.9 0.1 copy.26
  12.2 0.5 collective-permute-start.5
  12.6 4.9 %collective-permute-done.6.refs_2_.refs_6_ = bf16[656,128]{1,0:T(8,128)(2,1)S(1)} collective-permute-done((bf16[656,128]{1,0:T(8,128)(2,1)S(1)}, bf16[656,128]{1,0:T(8,128)(2,1)S(1)}, u32[]{:S(2)}, u32[]{:S(2)}) %collective-permute-start.6) | collective-permute-done | bytes 167968 | tf_op jit(solution)/shard_map/ppermute | solution.py:62
  17.5 0.1 dynamic-slice_bitcast_fusion.2
  17.6 0.1 copy.27.refs_13_.refs_12_
  17.7 0.1 copy.30
  17.9 0.2 copy.24.refs_4_
  18.1 0.8 %collective-permute-done.7.refs_3_.refs_7_ = bf16[656,128]{1,0:T(8,128)(2,1)S(1)} collective-permute-done((bf16[656,128]{1,0:T(8,128)(2,1)S(1)}, bf16[656,128]{1,0:T(8,128)(2,1)S(1)}, u32[]{:S(2)}, u32[]{:S(2)}) %collective-permute-start.7) | collective-permute-done | bytes 167968 | tf_op jit(solution)/shard_map/ppermute | solution.py:62
  18.9 0.5 shard_map.120
  19.5 3.2 %shard_map.121 = (bf16[16,384,128]{2,1,0:T(8,128)(2,1)S(1)}, f32[512,384]{1,0:T(8,128)S(1)}, f32[96,384]{1,0:T(8,128)S(1)}, f32[32,512]{1,0:T(8,128)S(1)}, f32[8,512]{1,0:T(8,128)S(1)}) custom-call(bf16[16,64,128]{2,1,0:T(8,128)(2,1)S(1)} %bitcast.55, bf16[16,64,128]{2,1,0:T(8,128)(2,1)S(1)} %collective-permute-done.refs_1_, ...), custom_call_target="tpu_custom_call" | custom-call | tf_op jit(solution)/shard_map/pallas_call | solution.py:309
  22.7 0.3 collective-permute-start.10
  23.0 1.5 %collective-permute-start.9 = (f32[8,512]{1,0:T(8,128)S(1)}, f32[8,512]{1,0:T(8,128)S(1)}, u32[]{:S(2)}, u32[]{:S(2)}) collective-permute-start(f32[8,512]{1,0:T(8,128)S(1)} %get-tuple-element.32.refs_0_), channel_id=1, source_target_pairs={{0,2},{1,3},{2,0},{3,1},{4,6},{5,7},{6,4},{7,5},{8,10},{9,11},{10,... | collective-permute-start | bytes 49160 | tf_op jit(solution)/shard_map/ppermute | solution.py:62
  24.6 0.1 collective-permute-start.8
  24.6 1.3 %collective-permute-done.10.refs_3_ = f32[8,512]{1,0:T(8,128)S(1)} collective-permute-done((f32[8,512]{1,0:T(8,128)S(1)}, f32[8,512]{1,0:T(8,128)S(1)}, u32[]{:S(2)}, u32[]{:S(2)}) %collective-permute-start.10) | collective-permute-done | bytes 16416 | tf_op jit(solution)/shard_map/ppermute | solution.py:62
  25.9 0.8 %collective-permute-done.9.refs_2_ = f32[8,512]{1,0:T(8,128)S(1)} collective-permute-done((f32[8,512]{1,0:T(8,128)S(1)}, f32[8,512]{1,0:T(8,128)S(1)}, u32[]{:S(2)}, u32[]{:S(2)}) %collective-permute-start.9) | collective-permute-done | bytes 16416 | tf_op jit(solution)/shard_map/ppermute | solution.py:62
  26.8 2.8 %shard_map.122 = (f32[224,128]{1,0:T(8,128)S(1)}, f32[8,128]{1,0:T(8,128)S(1)}, bf16[96,512]{1,0:T(8,128)(2,1)S(1)}, bf16[96,512]{1,0:T(8,128)(2,1)S(1)}, bf16[192,512]{1,0:T(8,128)(2,1)S(1)}) custom-call(f32[8,512]{1,0:T(8,128)S(1)} %get-tuple-element.32.refs_0_, f32[8,512]{1,0:T(8,128)S(1)} %collective-permute-done.8.refs_1_, ...), custom_call_target="tpu_custom_call" | custom-call | tf_op jit(solution)/shard_map/pallas_call | solution.py:309
  29.7 1.6 %collective-permute-start.13 = (f32[224,128]{1,0:T(8,128)S(1)}, f32[224,128]{1,0:T(8,128)S(1)}, u32[]{:S(2)}, u32[]{:S(2)}) collective-permute-start(f32[224,128]{1,0:T(8,128)S(1)} %get-tuple-element.42), channel_id=1, source_target_pairs={{0,4},{4,0},{8,12},{12,8},{16,20},{20,16},{24,28},{28,24},{1,5},{5... | collective-permute-start | bytes 344072 | tf_op jit(solution)/shard_map/ppermute | solution.py:62
  31.3 1.5 %collective-permute-start.12 = (bf16[192,512]{1,0:T(8,128)(2,1)S(1)}, bf16[192,512]{1,0:T(8,128)(2,1)S(1)}, u32[]{:S(2)}, u32[]{:S(2)}) collective-permute-start(bf16[192,512]{1,0:T(8,128)(2,1)S(1)} %get-tuple-element.41), channel_id=1, source_target_pairs={{0,2},{1,3},{2,0},{3,1},{4,6},{5,7},{6,4},{7,5},{8,10},{9,11},{10,... | collective-permute-start | bytes 589832 | tf_op jit(solution)/shard_map/ppermute | solution.py:62
  32.8 2.5 %collective-permute-done.13 = f32[224,128]{1,0:T(8,128)S(1)} collective-permute-done((f32[224,128]{1,0:T(8,128)S(1)}, f32[224,128]{1,0:T(8,128)S(1)}, u32[]{:S(2)}, u32[]{:S(2)}) %collective-permute-start.13) | collective-permute-done | bytes 114720 | tf_op jit(solution)/shard_map/ppermute | solution.py:62
  35.3 1.6 %collective-permute-start.16 = (bf16[224,128]{1,0:T(8,128)(2,1)S(1)}, bf16[224,128]{1,0:T(8,128)(2,1)S(1)}, u32[]{:S(2)}, u32[]{:S(2)}) collective-permute-start(bf16[224,128]{1,0:T(8,128)(2,1)S(1)} %add_convert_fusion), channel_id=1, source_target_pairs={{0,24},{4,28},{8,16},{12,20},{16,8},{20,12},{24,0},{28,4},{1,25},{... | collective-permute-start | bytes 172040 | tf_op jit(solution)/shard_map/ppermute | solution.py:62
  36.9 2.4 %collective-permute-start.15 = (bf16[224,128]{1,0:T(8,128)(2,1)S(1)}, bf16[224,128]{1,0:T(8,128)(2,1)S(1)}, u32[]{:S(2)}, u32[]{:S(2)}) collective-permute-start(bf16[224,128]{1,0:T(8,128)(2,1)S(1)} %add_convert_fusion), channel_id=1, source_target_pairs={{0,16},{4,20},{8,24},{12,28},{16,0},{20,4},{24,8},{28,12},{1,17},{... | collective-permute-start | bytes 172040 | tf_op jit(solution)/shard_map/ppermute | solution.py:62
  39.4 0.1 collective-permute-done.16
  39.5 2.8 %collective-permute-done.15 = bf16[224,128]{1,0:T(8,128)(2,1)S(1)} collective-permute-done((bf16[224,128]{1,0:T(8,128)(2,1)S(1)}, bf16[224,128]{1,0:T(8,128)(2,1)S(1)}, u32[]{:S(2)}, u32[]{:S(2)}) %collective-permute-start.15) | collective-permute-done | bytes 57376 | tf_op jit(solution)/shard_map/ppermute | solution.py:62
  42.3 1.2 %collective-permute-done.14 = bf16[224,128]{1,0:T(8,128)(2,1)S(1)} collective-permute-done((bf16[224,128]{1,0:T(8,128)(2,1)S(1)}, bf16[224,128]{1,0:T(8,128)(2,1)S(1)}, u32[]{:S(2)}, u32[]{:S(2)}) %collective-permute-start.14) | collective-permute-done | bytes 57376 | tf_op jit(solution)/shard_map/ppermute | solution.py:62
  43.6 1.6 %collective-permute-start.19 = (f32[224,128]{1,0:T(8,128)S(1)}, f32[224,128]{1,0:T(8,128)S(1)}, u32[]{:S(2)}, u32[]{:S(2)}) collective-permute-start(f32[224,128]{1,0:T(8,128)S(1)} %add_add_fusion.refs_0_), channel_id=1, source_target_pairs={{0,2},{1,3},{2,0},{3,1},{4,6},{5,7},{6,4},{7,5},{8,10},{9,11},{10,... | collective-permute-start | bytes 344072 | tf_op jit(solution)/shard_map/ppermute | solution.py:62
  45.2 1.8 %collective-permute-start.21 = (bf16[4,16,512]{2,1,0:T(8,128)(2,1)S(1)}, bf16[4,16,512]{2,1,0:T(8,128)(2,1)S(1)}, u32[]{:S(2)}, u32[]{:S(2)}) collective-permute-start(bf16[4,16,512]{2,1,0:T(8,128)(2,1)S(1)} %pad_maximum_fusion.1), channel_id=1, source_target_pairs={{0,4},{8,12},{16,20},{24,28},{4,0},{12,8},{20,16},{28,24},{1,5},{9... | collective-permute-start | bytes 196616 | tf_op jit(solution)/shard_map/ppermute | solution.py:74
  47.0 2.8 %collective-permute-start.22 = (bf16[4,16,512]{2,1,0:T(8,128)(2,1)S(1)}, bf16[4,16,512]{2,1,0:T(8,128)(2,1)S(1)}, u32[]{:S(2)}, u32[]{:S(2)}) collective-permute-start(bf16[4,16,512]{2,1,0:T(8,128)(2,1)S(1)} %pad_maximum_fusion.2), channel_id=1, source_target_pairs={{4,8},{12,16},{20,24},{8,4},{16,12},{24,20},{5,9},{13,17},{21,25},... | collective-permute-start | bytes 196616 | tf_op jit(solution)/shard_map/ppermute | solution.py:68
  49.8 0.1 collective-permute-start.20
  49.9 0.5 slice_bitcast_fusion.8
  50.4 0.8 %collective-permute-done.20.refs_3_ = f32[224,128]{1,0:T(8,128)S(1)} collective-permute-done((f32[224,128]{1,0:T(8,128)S(1)}, f32[224,128]{1,0:T(8,128)S(1)}, u32[]{:S(2)}, u32[]{:S(2)}) %collective-permute-start.20) | collective-permute-done | bytes 114720 | tf_op jit(solution)/shard_map/ppermute | solution.py:62
  51.2 0.9 %shard_map.123 = (f32[4,128,128]{2,1,0:T(8,128)}, f32[128,384]{1,0:T(8,128)}) custom-call(s32[1]{0:T(128)} %bitcast.8.place_ref, f32[224,128]{1,0:T(8,128)S(1)} %add_add_fusion.refs_0_, f32[224,128]{1,0:T(8,128)S(1)} %collective-permute-done.18.refs_1_, f32[224,128]{1,0:T(8,128)S(1)} %collective-permute-done.19.refs_2_, ...), custom_call_target="tpu_custom_call" | custom-call | tf_op jit(solution)/shard_map/pallas_call | solution.py:309
  52.1 1.9 %collective-permute-done.22.refs_5_ = bf16[4,16,512]{2,1,0:T(8,128)(2,1)S(1)} collective-permute-done((bf16[4,16,512]{2,1,0:T(8,128)(2,1)S(1)}, bf16[4,16,512]{2,1,0:T(8,128)(2,1)S(1)}, u32[]{:S(2)}, u32[]{:S(2)}) %collective-permute-start.22) | collective-permute-done | bytes 65568 | tf_op jit(solution)/shard_map/ppermute | solution.py:68
  54.0 1.7 %shard_map.124 = f32[64,16,128]{2,1,0:T(8,128)} custom-call(s32[1]{0:T(128)} %bitcast.8.place_ref, bf16[96,512]{1,0:T(8,128)(2,1)S(1)} %get-tuple-element.39.refs_0_, bf16[96,512]{1,0:T(8,128)(2,1)S(1)} %collective-permute-done.11.refs_1_, bf16[192,512]{1,0:T(8,128)(2,1)S(1)} %collective-permute-done.12.refs_2_, ...), custom_call_target="tpu_custom_call" | custom-call | tf_op jit(solution)/shard_map/pallas_call | solution.py:309
  (51 shorter events, 0.6 us)
Async XLA Ops:
  0.6 6.7 %copy-start = (f32[8,512]{1,0:T(8,128)S(1)}, f32[8,512]{1,0:T(8,128)}, u32[]{:S(2)}) copy-start(f32[8,512]{1,0:T(8,128)} %param.12) | copy-start | bytes 49156
  0.6 11.2 %copy-start.1 = (bf16[4,128,128]{2,1,0:T(8,128)(2,1)S(1)}, bf16[4,128,128]{2,1,0:T(8,128)(2,1)}, u32[]{:S(2)}) copy-start(bf16[4,128,128]{2,1,0:T(8,128)(2,1)} %refs_7_.1) | copy-start | bytes 393220
  0.7 11.3 %copy-start.2 = (bf16[128,384]{1,0:T(8,128)(2,1)S(1)}, bf16[128,384]{1,0:T(8,128)(2,1)}, u32[]{:S(2)}) copy-start(bf16[128,384]{1,0:T(8,128)(2,1)} %refs_8_.1) | copy-start | bytes 294916
  0.7 16.9 %copy-start.3 = (f32[128]{0:T(128)S(1)}, f32[128]{0:T(128)}, u32[]{:S(2)}) copy-start(f32[128]{0:T(128)} %param.13) | copy-start | bytes 1540
  1.8 10.3 %collective-permute-start.1 = (bf16[16,64,128]{2,1,0:T(8,128)(2,1)S(1)}, bf16[16,64,128]{2,1,0:T(8,128)(2,1)S(1)}, u32[]{:S(2)}, u32[]{:S(2)}) collective-permute-start(bf16[16,64,128]{2,1,0:T(8,128)(2,1)S(1)} %bitcast.53), channel_id=1, source_target_pairs={{0,2},{1,3},{2,0},{3,1},{4,6},{5,7},{6,4},{7,5},{8,10},{9,11},{10,... | collective-permute-start | bytes 786440 | tf_op jit(solution)/shard_map/ppermute | solution.py:62
  3.3 16.1 %collective-permute-start = (bf16[16,64,128]{2,1,0:T(8,128)(2,1)S(1)}, bf16[16,64,128]{2,1,0:T(8,128)(2,1)S(1)}, u32[]{:S(2)}, u32[]{:S(2)}) collective-permute-start(bf16[16,64,128]{2,1,0:T(8,128)(2,1)S(1)} %bitcast.54), channel_id=1, source_target_pairs={{0,1},{1,0},{2,3},{3,2},{4,5},{5,4},{6,7},{7,6},{8,9},{9,8},{10,11... | collective-permute-start | bytes 786440 | tf_op jit(solution)/shard_map/ppermute | solution.py:62
  4.2 6.9 %collective-permute-start.4 = (bf16[16,16,128]{2,0,1:T(8,128)(2,1)S(1)}, bf16[16,16,128]{2,0,1:T(8,128)(2,1)S(1)}, u32[]{:S(2)}, u32[]{:S(2)}) collective-permute-start(bf16[16,16,128]{2,0,1:T(8,128)(2,1)S(1)} %get-tuple-element.54), channel_id=1, source_target_pairs={{4,8},{12,16},{20,24},{28,0},{8,4},{16,12},{24,20},{0,28},{5,9},{1... | collective-permute-start | bytes 196616 | tf_op jit(solution)/shard_map/ppermute | solution.py:74
  5.7 5.4 %collective-permute-start.3 = (bf16[16,16,128]{2,0,1:T(8,128)(2,1)S(1)}, bf16[16,16,128]{2,0,1:T(8,128)(2,1)S(1)}, u32[]{:S(2)}, u32[]{:S(2)}) collective-permute-start(bf16[16,16,128]{2,0,1:T(8,128)(2,1)S(1)} %get-tuple-element.55), channel_id=1, source_target_pairs={{0,4},{8,12},{16,20},{24,28},{4,0},{12,8},{20,16},{28,24},{1,5},{9... | collective-permute-start | bytes 196616 | tf_op jit(solution)/shard_map/ppermute | solution.py:74
  11.2 6.3 %collective-permute-start.6 = (bf16[656,128]{1,0:T(8,128)(2,1)S(1)}, bf16[656,128]{1,0:T(8,128)(2,1)S(1)}, u32[]{:S(2)}, u32[]{:S(2)}) collective-permute-start(bf16[656,128]{1,0:T(8,128)(2,1)S(1)} %fusion.2.refs_0_.refs_4_), channel_id=1, source_target_pairs={{0,2},{1,3},{2,0},{3,1},{4,6},{5,7},{6,4},{7,5},{8,10},{9,11},{10,... | collective-permute-start | bytes 503816 | tf_op jit(solution)/shard_map/ppermute | solution.py:62
  12.1 7.4 %collective-permute-start.2 = (bf16[16,64,128]{2,1,0:T(8,128)(2,1)S(1)}, bf16[16,64,128]{2,1,0:T(8,128)(2,1)S(1)}, u32[]{:S(2)}, u32[]{:S(2)}) collective-permute-start(bf16[16,64,128]{2,1,0:T(8,128)(2,1)S(1)} %collective-permute-done.1.refs_2_), channel_id=1, source_target_pairs={{0,1},{1,0},{2,3},{3,2},{4,5},{5,4},{6,7},{7,6},{8,9},{9,8},{10,11... | collective-permute-start | bytes 786440 | tf_op jit(solution)/shard_map/ppermute | solution.py:62
  12.2 5.9 %collective-permute-start.5 = (bf16[656,128]{1,0:T(8,128)(2,1)S(1)}, bf16[656,128]{1,0:T(8,128)(2,1)S(1)}, u32[]{:S(2)}, u32[]{:S(2)}) collective-permute-start(bf16[656,128]{1,0:T(8,128)(2,1)S(1)} %fusion.2.refs_0_.refs_4_), channel_id=1, source_target_pairs={{0,1},{1,0},{2,3},{3,2},{4,5},{5,4},{6,7},{7,6},{8,9},{9,8},{10,11... | collective-permute-start | bytes 503816 | tf_op jit(solution)/shard_map/ppermute | solution.py:62
  17.5 1.4 %collective-permute-start.7 = (bf16[656,128]{1,0:T(8,128)(2,1)S(1)}, bf16[656,128]{1,0:T(8,128)(2,1)S(1)}, u32[]{:S(2)}, u32[]{:S(2)}) collective-permute-start(bf16[656,128]{1,0:T(8,128)(2,1)S(1)} %collective-permute-done.6.refs_2_.refs_6_), channel_id=1, source_target_pairs={{0,1},{1,0},{2,3},{3,2},{4,5},{5,4},{6,7},{7,6},{8,9},{9,8},{10,11... | collective-permute-start | bytes 503816 | tf_op jit(solution)/shard_map/ppermute | solution.py:62
  22.7 3.2 %collective-permute-start.10 = (f32[8,512]{1,0:T(8,128)S(1)}, f32[8,512]{1,0:T(8,128)S(1)}, u32[]{:S(2)}, u32[]{:S(2)}) collective-permute-start(f32[8,512]{1,0:T(8,128)S(1)} %get-tuple-element.32.refs_0_), channel_id=1, source_target_pairs={{0,3},{1,2},{2,1},{3,0},{4,7},{5,6},{6,5},{7,4},{8,11},{9,10},{10,... | collective-permute-start | bytes 49160 | tf_op jit(solution)/shard_map/ppermute | solution.py:62
  23.0 3.8 %collective-permute-start.9 = (f32[8,512]{1,0:T(8,128)S(1)}, f32[8,512]{1,0:T(8,128)S(1)}, u32[]{:S(2)}, u32[]{:S(2)}) collective-permute-start(f32[8,512]{1,0:T(8,128)S(1)} %get-tuple-element.32.refs_0_), channel_id=1, source_target_pairs={{0,2},{1,3},{2,0},{3,1},{4,6},{5,7},{6,4},{7,5},{8,10},{9,11},{10,... | collective-permute-start | bytes 49160 | tf_op jit(solution)/shard_map/ppermute | solution.py:62
  24.6 2.2 %collective-permute-start.8 = (f32[8,512]{1,0:T(8,128)S(1)}, f32[8,512]{1,0:T(8,128)S(1)}, u32[]{:S(2)}, u32[]{:S(2)}) collective-permute-start(f32[8,512]{1,0:T(8,128)S(1)} %get-tuple-element.32.refs_0_), channel_id=1, source_target_pairs={{0,1},{1,0},{2,3},{3,2},{4,5},{5,4},{6,7},{7,6},{8,9},{9,8},{10,11... | collective-permute-start | bytes 49160 | tf_op jit(solution)/shard_map/ppermute | solution.py:62
  29.6 3.2 %collective-permute-start.11 = (bf16[96,512]{1,0:T(8,128)(2,1)S(1)}, bf16[96,512]{1,0:T(8,128)(2,1)S(1)}, u32[]{:S(2)}, u32[]{:S(2)}) collective-permute-start(bf16[96,512]{1,0:T(8,128)(2,1)S(1)} %get-tuple-element.40), channel_id=1, source_target_pairs={{0,1},{1,0},{2,3},{3,2},{4,5},{5,4},{6,7},{7,6},{8,9},{9,8},{10,11... | collective-permute-start | bytes 294920 | tf_op jit(solution)/shard_map/ppermute | solution.py:62
  29.7 5.6 %collective-permute-start.13 = (f32[224,128]{1,0:T(8,128)S(1)}, f32[224,128]{1,0:T(8,128)S(1)}, u32[]{:S(2)}, u32[]{:S(2)}) collective-permute-start(f32[224,128]{1,0:T(8,128)S(1)} %get-tuple-element.42), channel_id=1, source_target_pairs={{0,4},{4,0},{8,12},{12,8},{16,20},{20,16},{24,28},{28,24},{1,5},{5... | collective-permute-start | bytes 344072 | tf_op jit(solution)/shard_map/ppermute | solution.py:62
  31.3 8.2 %collective-permute-start.12 = (bf16[192,512]{1,0:T(8,128)(2,1)S(1)}, bf16[192,512]{1,0:T(8,128)(2,1)S(1)}, u32[]{:S(2)}, u32[]{:S(2)}) collective-permute-start(bf16[192,512]{1,0:T(8,128)(2,1)S(1)} %get-tuple-element.41), channel_id=1, source_target_pairs={{0,2},{1,3},{2,0},{3,1},{4,6},{5,7},{6,4},{7,5},{8,10},{9,11},{10,... | collective-permute-start | bytes 589832 | tf_op jit(solution)/shard_map/ppermute | solution.py:62
  35.3 4.2 %collective-permute-start.16 = (bf16[224,128]{1,0:T(8,128)(2,1)S(1)}, bf16[224,128]{1,0:T(8,128)(2,1)S(1)}, u32[]{:S(2)}, u32[]{:S(2)}) collective-permute-start(bf16[224,128]{1,0:T(8,128)(2,1)S(1)} %add_convert_fusion), channel_id=1, source_target_pairs={{0,24},{4,28},{8,16},{12,20},{16,8},{20,12},{24,0},{28,4},{1,25},{... | collective-permute-start | bytes 172040 | tf_op jit(solution)/shard_map/ppermute | solution.py:62
  36.9 5.4 %collective-permute-start.15 = (bf16[224,128]{1,0:T(8,128)(2,1)S(1)}, bf16[224,128]{1,0:T(8,128)(2,1)S(1)}, u32[]{:S(2)}, u32[]{:S(2)}) collective-permute-start(bf16[224,128]{1,0:T(8,128)(2,1)S(1)} %add_convert_fusion), channel_id=1, source_target_pairs={{0,16},{4,20},{8,24},{12,28},{16,0},{20,4},{24,8},{28,12},{1,17},{... | collective-permute-start | bytes 172040 | tf_op jit(solution)/shard_map/ppermute | solution.py:62
  39.3 4.2 %collective-permute-start.14 = (bf16[224,128]{1,0:T(8,128)(2,1)S(1)}, bf16[224,128]{1,0:T(8,128)(2,1)S(1)}, u32[]{:S(2)}, u32[]{:S(2)}) collective-permute-start(bf16[224,128]{1,0:T(8,128)(2,1)S(1)} %add_convert_fusion), channel_id=1, source_target_pairs={{0,8},{4,12},{8,0},{12,4},{16,24},{20,28},{24,16},{28,20},{1,9},{5... | collective-permute-start | bytes 172040 | tf_op jit(solution)/shard_map/ppermute | solution.py:62
  39.4 4.1 %collective-permute-start.17 = (bf16[192,512]{1,0:T(8,128)(2,1)S(1)}, bf16[192,512]{1,0:T(8,128)(2,1)S(1)}, u32[]{:S(2)}, u32[]{:S(2)}) collective-permute-start(bf16[192,512]{1,0:T(8,128)(2,1)S(1)} %collective-permute-done.12.refs_2_), channel_id=1, source_target_pairs={{0,1},{1,0},{2,3},{3,2},{4,5},{5,4},{6,7},{7,6},{8,9},{9,8},{10,11... | collective-permute-start | bytes 589832 | tf_op jit(solution)/shard_map/ppermute | solution.py:62
  43.6 6.2 %collective-permute-start.19 = (f32[224,128]{1,0:T(8,128)S(1)}, f32[224,128]{1,0:T(8,128)S(1)}, u32[]{:S(2)}, u32[]{:S(2)}) collective-permute-start(f32[224,128]{1,0:T(8,128)S(1)} %add_add_fusion.refs_0_), channel_id=1, source_target_pairs={{0,2},{1,3},{2,0},{3,1},{4,6},{5,7},{6,4},{7,5},{8,10},{9,11},{10,... | collective-permute-start | bytes 344072 | tf_op jit(solution)/shard_map/ppermute | solution.py:62
  45.1 5.3 %collective-permute-start.18 = (f32[224,128]{1,0:T(8,128)S(1)}, f32[224,128]{1,0:T(8,128)S(1)}, u32[]{:S(2)}, u32[]{:S(2)}) collective-permute-start(f32[224,128]{1,0:T(8,128)S(1)} %add_add_fusion.refs_0_), channel_id=1, source_target_pairs={{0,1},{1,0},{2,3},{3,2},{4,5},{5,4},{6,7},{7,6},{8,9},{9,8},{10,11... | collective-permute-start | bytes 344072 | tf_op jit(solution)/shard_map/ppermute | solution.py:62
  45.2 7.0 %collective-permute-start.21 = (bf16[4,16,512]{2,1,0:T(8,128)(2,1)S(1)}, bf16[4,16,512]{2,1,0:T(8,128)(2,1)S(1)}, u32[]{:S(2)}, u32[]{:S(2)}) collective-permute-start(bf16[4,16,512]{2,1,0:T(8,128)(2,1)S(1)} %pad_maximum_fusion.1), channel_id=1, source_target_pairs={{0,4},{8,12},{16,20},{24,28},{4,0},{12,8},{20,16},{28,24},{1,5},{9... | collective-permute-start | bytes 196616 | tf_op jit(solution)/shard_map/ppermute | solution.py:74
  47.0 7.1 %collective-permute-start.22 = (bf16[4,16,512]{2,1,0:T(8,128)(2,1)S(1)}, bf16[4,16,512]{2,1,0:T(8,128)(2,1)S(1)}, u32[]{:S(2)}, u32[]{:S(2)}) collective-permute-start(bf16[4,16,512]{2,1,0:T(8,128)(2,1)S(1)} %pad_maximum_fusion.2), channel_id=1, source_target_pairs={{4,8},{12,16},{20,24},{8,4},{16,12},{24,20},{5,9},{13,17},{21,25},... | collective-permute-start | bytes 196616 | tf_op jit(solution)/shard_map/ppermute | solution.py:68
  49.8 1.4 %collective-permute-start.20 = (f32[224,128]{1,0:T(8,128)S(1)}, f32[224,128]{1,0:T(8,128)S(1)}, u32[]{:S(2)}, u32[]{:S(2)}) collective-permute-start(f32[224,128]{1,0:T(8,128)S(1)} %collective-permute-done.19.refs_2_), channel_id=1, source_target_pairs={{0,1},{1,0},{2,3},{3,2},{4,5},{5,4},{6,7},{7,6},{8,9},{9,8},{10,11... | collective-permute-start | bytes 344072 | tf_op jit(solution)/shard_map/ppermute | solution.py:62

commit v6 on v5

--- a/solution.py
+++ b/solution.py
@@ -80,13 +80,12 @@
     return jnp.where(rows == column, 1.0, 0.0).astype(BF16)
 
 
-def geometry_kernel(slots, atoms, edge, plane, place_ref, *refs):
-    rows_of = (refs[0].shape[0] - HARM * edge) // 3
-    info = [
-        sum(ref[HARM * edge + i * rows_of : HARM * edge + (i + 1) * rows_of, :].astype(F32) for i in range(3))
-        for ref in refs[:plane]
-    ]
-    lhs_ref, coef_ref, harm_ref, column_ref, target_ref = refs[plane:]
+def pair_geometry(slots, atoms, edge, plane, place_ref, faces, lhs_ref, coef_ref, harm_ref, column_ref, target_ref):
+    groups = (faces[0].shape[0] - 2 * HARM) // 3
+    info = []
+    for ref in faces:
+        parts = [ref[2 * HARM + i * groups : 2 * HARM + (i + 1) * groups].astype(F32) for i in range(3)]
+        info.append((parts[0] + parts[1] + parts[2]).reshape(groups * ref.shape[1], -1))
 
     def rows(first):
         return jnp.concatenate([x[first * slots : (first + 1) * slots, :] for x in info], axis=1)
@@ -111,11 +110,12 @@
     coef_ref[...] = dot(lhs_ref[...], jnp.concatenate([high, low, high], axis=0))
 
 
-def forward_kernel(slots, plane, *refs):
+def forward_kernel(slots, plane, place_ref, *refs):
     wide = refs[:plane]
     faces = refs[plane : 2 * plane]
-    coef_ref, harm_ref, column_ref, mix_ref, gate_ref, out_w_ref = refs[2 * plane : 2 * plane + 6]
-    feats_ref, mixed_ref, gates_ref, msg_ref, dens_ref, source_ref = refs[2 * plane + 6 :]
+    lhs_ref, mix_ref, gate_ref, out_w_ref = refs[2 * plane : 2 * plane + 4]
+    feats_ref, mixed_ref, gates_ref, msg_ref, dens_ref = refs[2 * plane + 4 : 2 * plane + 9]
+    coef_ref, harm_ref, column_ref, target_ref, source_ref = refs[2 * plane + 9 :]
     atoms = wide[0].shape[1]
     edge = (feats_ref.shape[1] - plane * atoms) // plane
     face = edge // 2
@@ -125,9 +125,8 @@
         feats_ref[:, j * atoms : (j + 1) * atoms, :] = wide[j][...]
         for side in range(2):
             at = plane * atoms + j * edge + side * face
-            for lm in range(HARM):
-                first = (side * HARM + lm) * face
-                feats_ref[lm, at : at + face, :] = faces[j][first : first + face, :]
+            feats_ref[:, at : at + face, :] = faces[j][side * HARM : (side + 1) * HARM]
+    pair_geometry(slots, atoms, edge, plane, place_ref, faces, lhs_ref, coef_ref, harm_ref, column_ref, target_ref)
     gates_ref[...] = jax.nn.sigmoid(dot_lanes(gate_ref[...], feats_ref[0]))
     for lm in range(HARM):
         degree = DEGREE_OF[lm]
@@ -262,19 +261,24 @@
     zero_row = None
     for degree, (start, end) in enumerate(DEGREE_SPANS):
         weight = mix_ref[degree]
+        mixed_all = dot(feats_ref[start:end].reshape(-1, channels), weight)
         gate_sum = None
+        d_mixed = []
         for lm in range(start, end):
-            mixed = dot(feats_ref[lm], weight)
+            mixed = mixed_all[(lm - start) * atoms : (lm - start + 1) * atoms]
             if degree == 0:
                 s = jax.nn.sigmoid(mixed)
-                d_mixed = upstream[lm] * (s * (1.0 + mixed * (1.0 - s)))
+                d_mixed.append(upstream[lm] * (s * (1.0 + mixed * (1.0 - s))))
             else:
-                d_mixed = upstream[lm] * gates[:, (degree - 1) * channels : degree * channels]
+                d_mixed.append(upstream[lm] * gates[:, (degree - 1) * channels : degree * channels])
                 product = upstream[lm] * mixed
                 gate_sum = product if gate_sum is None else gate_sum + product
-            high, low = split_high_low(d_mixed)
-            back = dot_lanes(jnp.concatenate([high, low], axis=0), weight)
-            result = upstream[lm] + back[:atoms] + back[atoms:]
+        high, low = split_high_low(jnp.concatenate(d_mixed, axis=0))
+        rows = high.shape[0]
+        back = dot_lanes(jnp.concatenate([high, low], axis=0), weight)
+        back = back[:rows] + back[rows:]
+        for lm in range(start, end):
+            result = upstream[lm] + back[(lm - start) * atoms : (lm - start + 1) * atoms]
             if degree == 0:
                 zero_row = result
             else:
@@ -362,8 +366,7 @@
     high = lax.reduce_precision(info, 8, 7)
     middle = lax.reduce_precision(info - high, 8, 7)
     parts = [x.astype(BF16) for x in (high, middle, info - high - middle)]
-    near, far = near.reshape(-1, channels), far.reshape(-1, channels)
-    faces = jnp.concatenate([near, far, *parts], axis=0)
+    faces = jnp.concatenate([near, far] + [x.reshape(-1, face, channels) for x in parts], axis=0)
     bits = [1 << b for b in reversed(range((plane - 1).bit_length()))]
     held = {0: (own, faces)}
     for bit in bits:
@@ -388,20 +391,7 @@
     radial_lhs = radial_lhs.reshape(slots * 4 * part, 3 * nbasis * slots).astype(BF16)
     out_part = lax.dynamic_slice_in_dim(out_weight, first, part)[:, None]
 
-    coef, harm, column, goals = call(
-        functools.partial(geometry_kernel, slots, atoms, edge, plane),
-        (
-            jax.ShapeDtypeStruct((slots * 4 * part, lanes), F32),
-            jax.ShapeDtypeStruct((harm_count * slots, lanes), F32),
-            jax.ShapeDtypeStruct((slots, lanes), jnp.int32),
-            jax.ShapeDtypeStruct((slots, lanes), F32),
-        ),
-        [],
-        place,
-        *[p[1] for p in pieces],
-        radial_lhs,
-    )
-    feats, mixed, gates, message, dens = call(
+    feats, mixed, gates, message, dens, coef, harm, column, goals = call(
         functools.partial(forward_kernel, slots, plane),
         (
             jax.ShapeDtypeStruct((harm_count, total, channels), BF16),
@@ -409,13 +399,16 @@
             jax.ShapeDtypeStruct((3 * part, total), F32),
             jax.ShapeDtypeStruct((part, lanes), F32),
             jax.ShapeDtypeStruct((8, lanes), F32),
+            jax.ShapeDtypeStruct((slots * 4 * part, lanes), F32),
+            jax.ShapeDtypeStruct((harm_count * slots, lanes), F32),
+            jax.ShapeDtypeStruct((slots, lanes), jnp.int32),
+            jax.ShapeDtypeStruct((slots, lanes), F32),
         ),
         [pltpu.VMEM((harm_count * part, total), BF16)],
+        place,
         *[p[0] for p in pieces],
         *[p[1] for p in pieces],
-        coef,
-        harm,
-        column,
+        radial_lhs,
         mix_part,
         gate_part,
         out_part,

time: 56.1 us -> 55 us (0.980)
  waiting for transfers between devices: 17.6 us -> 16.8 us
    dynamic_slice x1, local copies, waits for them, and re-layouts: 0.1 us -> 1 us  [body(): mix_part = lax.dynamic_slice_in_dim(mix_weight, first, part, axis=2)]
    ppermute x19, waiting for transfers between devices: 15.2 us -> 14.4 us  [partner(): return lax.ppermute(block, axis, [(i, i ^ bit) for i in range(count)])]
    dynamic_slice x1, local copies, waits for them, and re-layouts: 0.88 us -> 0.02 us  [body(): lax.dynamic_slice_in_dim(own, odd * last, face, 1)]
    pallas_call x5 -> x4, Pallas kernels: 9.23 us -> 9.1 us  [call(): pl.pallas_call(kernel, out_shape=outs, in_specs=[smem if x.shape == (1,)...]
  transfers between devices with their start and end apart: 23 -> 23, of which waited for: 11 -> 11; matrix products, arithmetic and copies ran while one was open for 10% -> 10% of each run, Pallas kernels for 3% -> 2%
where the time goes in v6:
time: 55 us; the launch traced here: 54.7 us
  starting transfers between devices  21.3 us (39%)
  waiting for transfers between devices  16.8 us (31%)
  Pallas kernels  9.1 us (17%)
  local copies, waits for them, and re-layouts  4.93 us (9%)
  other arithmetic  1.74 us (3%)
  between operations  0.88 us (2%)
    ppermute x19, waiting for transfers between devices, partner(): return lax.ppermute(block, axis, [(i, i ^ bit) for i in range(count)])  14.4 us
    ppermute x19, starting transfers between devices, partner(): return lax.ppermute(block, axis, [(i, i ^ bit) for i in range(count)])  13.6 us
    pallas_call x4, Pallas kernels, call(): pl.pallas_call(kernel, out_shape=outs, in_specs=[smem if x.shape == (1,)...  9.1 us
    ppermute x3, starting transfers between devices, beside(): return lax.ppermute(block, axis, pairs + [(j, i) for i, j in pairs])  4.9 us
    ppermute x1, starting transfers between devices, inner(): return lax.ppermute(block, axis, pairs + [(j, i) for i, j in pairs])  2.82 us
    ppermute x1, waiting for transfers between devices, inner(): return lax.ppermute(block, axis, pairs + [(j, i) for i, j in pairs])  1.89 us
    concatenate x1, local copies, waits for them, and re-layouts, body(): jnp.concatenate([pair_vec.reshape(3 * slots, probes), code.astype(F32), t...  1.44 us
    unnamed x15, local copies, waits for them, and re-layouts  1.4 us
  transfers between devices with their start and end apart: 23, of which 11 were waited for; matrix products, arithmetic and copies ran while one was open for 10% of the time, Pallas kernels for 2%

profile of v6, /device:TPU:8, one launch (start us, length us, event | category | flops | bytes accessed | tf_op | source)
XLA Modules:
  0.0 54.7 jit_solution(2907050855148612378)
XLA Ops:
  0.7 1.1 %copy.38 = bf16[64,16,128]{2,0,1:T(8,128)(2,1)S(1)} copy(bf16[64,16,128]{2,1,0:T(8,128)(2,1)} %param.9) | data formatting | bytes 524288 | tf_op args[0]
  1.7 1.6 %collective-permute-start.1 = (bf16[16,64,128]{2,1,0:T(8,128)(2,1)S(1)}, bf16[16,64,128]{2,1,0:T(8,128)(2,1)S(1)}, u32[]{:S(2)}, u32[]{:S(2)}) collective-permute-start(bf16[16,64,128]{2,1,0:T(8,128)(2,1)S(1)} %bitcast.51), channel_id=1, source_target_pairs={{0,2},{1,3},{2,0},{3,1},{4,6},{5,7},{6,4},{7,5},{8,10},{9,11},{10,... | collective-permute-start | bytes 786440 | tf_op jit(solution)/shard_map/ppermute | solution.py:62
  3.3 1.4 %collective-permute-start.4 = (bf16[16,16,128]{2,1,0:T(8,128)(2,1)S(1)}, bf16[16,16,128]{2,1,0:T(8,128)(2,1)S(1)}, u32[]{:S(2)}, u32[]{:S(2)}) collective-permute-start(bf16[16,16,128]{2,1,0:T(8,128)(2,1)S(1)} %get-tuple-element.54), channel_id=1, source_target_pairs={{4,8},{12,16},{20,24},{28,0},{8,4},{16,12},{24,20},{0,28},{5,9},{1... | collective-permute-start | bytes 196616 | tf_op jit(solution)/shard_map/ppermute | solution.py:74
  4.8 1.7 %collective-permute-start.3 = (bf16[16,16,128]{2,1,0:T(8,128)(2,1)S(1)}, bf16[16,16,128]{2,1,0:T(8,128)(2,1)S(1)}, u32[]{:S(2)}, u32[]{:S(2)}) collective-permute-start(bf16[16,16,128]{2,1,0:T(8,128)(2,1)S(1)} %get-tuple-element.55), channel_id=1, source_target_pairs={{0,4},{8,12},{16,20},{24,28},{4,0},{12,8},{20,16},{28,24},{1,5},{9... | collective-permute-start | bytes 196616 | tf_op jit(solution)/shard_map/ppermute | solution.py:74
  6.5 0.1 constant_dynamic-slice_fusion.2
  6.5 0.1 reshape.68
  6.6 0.1 fusion
  6.7 0.2 multiply_convert_fusion
  6.9 0.7 %fusion.7 = f32[8,128]{1,0:T(8,128)S(1)} fusion(s32[8,128]{1,0:T(8,128)} %param.15, s32[]{:T(128)S(6)} %add.80, s32[]{:T(128)S(6)} %add.77, s32[]{:T(128)S(6)} %axis_index.25), kind=kLoop, calls=%fused_computation.43 | loop fusion | flops 50176 | bytes 8204 | tf_op jit(solution)/shard_map/convert_element_type | solution.py:360
  7.6 0.7 %convert_bitcast_fusion = f32[1,128]{1,0:T(1,128)S(1)} fusion(s32[128]{0:T(128)} %param.16), kind=kLoop, calls=%fused_computation.57 | loop fusion | flops 128 | bytes 1024 | tf_op jit(solution)/shard_map/broadcast_in_dim | solution.py:358
  8.3 1.4 %concatenate.11 = f32[48,128]{1,0:T(8,128)S(1)} concatenate(f32[24,128]{1,0:T(8,128)} %bitcast.64, f32[8,128]{1,0:T(8,128)S(1)} %fusion.7, f32[1,128]{1,0:T(1,128)S(1)} %convert_bitcast_fusion, f32[1,128]{1,0:T(1,128)} %bitcast.65, f32[14,128]{1,0:T(8,128)S(1)} %broadcast_in_dim.20), dimensions={0} | concatenate | bytes 49152 | tf_op jit(solution)/shard_map/concatenate | solution.py:360
  9.7 0.5 collective-permute-done.3
  10.3 0.6 %collective-permute-start.6 = (bf16[41,16,128]{2,1,0:T(8,128)(2,1)S(1)}, bf16[41,16,128]{2,1,0:T(8,128)(2,1)S(1)}, u32[]{:S(2)}, u32[]{:S(2)}) collective-permute-start(bf16[41,16,128]{2,1,0:T(8,128)(2,1)S(1)} %fusion.2.refs_4_), channel_id=1, source_target_pairs={{0,2},{1,3},{2,0},{3,1},{4,6},{5,7},{6,4},{7,5},{8,10},{9,11},{10,... | collective-permute-start | bytes 503816 | tf_op jit(solution)/shard_map/ppermute | solution.py:62
  10.9 1.0 %constant_dynamic-slice_fusion.1 = bf16[4,128,32]{2,1,0:T(8,128)(2,1)S(1)} fusion(bf16[4,128,128]{2,1,0:T(8,128)(2,1)} %refs_7_.1, s32[]{:T(128)S(6)} %select_n.52), kind=kLoop, calls=%fused_computation.52 | loop fusion | bytes 65540 | tf_op jit(solution)/shard_map/dynamic_slice | solution.py:378
  11.9 0.1 copy.25
  12.0 0.1 collective-permute-start.2
  12.1 0.5 collective-permute-start.5
  12.6 4.0 %collective-permute-done.6.refs_6_ = bf16[41,16,128]{2,1,0:T(8,128)(2,1)S(1)} collective-permute-done((bf16[41,16,128]{2,1,0:T(8,128)(2,1)S(1)}, bf16[41,16,128]{2,1,0:T(8,128)(2,1)S(1)}, u32[]{:S(2)}, u32[]{:S(2)}) %collective-permute-start.6) | collective-permute-done | bytes 167968 | tf_op jit(solution)/shard_map/ppermute | solution.py:62
  16.6 0.1 dynamic-slice_bitcast_fusion.2
  16.7 0.1 copy.27.refs_11_.refs_12_
  16.8 0.1 copy.30
  16.9 0.1 copy.36
  16.9 0.2 copy.26.refs_8_
  17.2 0.8 %collective-permute-done.7.refs_7_ = bf16[41,16,128]{2,1,0:T(8,128)(2,1)S(1)} collective-permute-done((bf16[41,16,128]{2,1,0:T(8,128)(2,1)S(1)}, bf16[41,16,128]{2,1,0:T(8,128)(2,1)S(1)}, u32[]{:S(2)}, u32[]{:S(2)}) %collective-permute-start.7) | collective-permute-done | bytes 167968 | tf_op jit(solution)/shard_map/ppermute | solution.py:62
  18.0 3.6 %shard_map.120 = (bf16[16,384,128]{2,1,0:T(8,128)(2,1)S(1)}, f32[512,384]{1,0:T(8,128)S(1)}, f32[96,384]{1,0:T(8,128)S(1)}, f32[32,512]{1,0:T(8,128)S(1)}, f32[8...) custom-call(s32[1]{0:T(128)} %bitcast.place_ref, ...), custom_call_target="tpu_custom_call" | custom-call | tf_op jit(solution)/shard_map/pallas_call | solution.py:313
  21.6 0.3 collective-permute-start.10
  21.9 1.5 %collective-permute-start.9 = (f32[8,512]{1,0:T(8,128)S(1)}, f32[8,512]{1,0:T(8,128)S(1)}, u32[]{:S(2)}, u32[]{:S(2)}) collective-permute-start(f32[8,512]{1,0:T(8,128)S(1)} %get-tuple-element.29.refs_0_), channel_id=1, source_target_pairs={{0,2},{1,3},{2,0},{3,1},{4,6},{5,7},{6,4},{7,5},{8,10},{9,11},{10,... | collective-permute-start | bytes 49160 | tf_op jit(solution)/shard_map/ppermute | solution.py:62
  23.5 0.1 collective-permute-start.8
  23.5 1.3 %collective-permute-done.10.refs_3_ = f32[8,512]{1,0:T(8,128)S(1)} collective-permute-done((f32[8,512]{1,0:T(8,128)S(1)}, f32[8,512]{1,0:T(8,128)S(1)}, u32[]{:S(2)}, u32[]{:S(2)}) %collective-permute-start.10) | collective-permute-done | bytes 16416 | tf_op jit(solution)/shard_map/ppermute | solution.py:62
  24.8 0.8 %collective-permute-done.9.refs_2_ = f32[8,512]{1,0:T(8,128)S(1)} collective-permute-done((f32[8,512]{1,0:T(8,128)S(1)}, f32[8,512]{1,0:T(8,128)S(1)}, u32[]{:S(2)}, u32[]{:S(2)}) %collective-permute-start.9) | collective-permute-done | bytes 16416 | tf_op jit(solution)/shard_map/ppermute | solution.py:62
  25.7 2.8 %shard_map.121 = (f32[224,128]{1,0:T(8,128)S(1)}, f32[8,128]{1,0:T(8,128)S(1)}, bf16[96,512]{1,0:T(8,128)(2,1)S(1)}, bf16[96,512]{1,0:T(8,128)(2,1)S(1)}, bf16[192,512]{1,0:T(8,128)(2,1)S(1)}) custom-call(f32[8,512]{1,0:T(8,128)S(1)} %get-tuple-element.29.refs_0_, f32[8,512]{1,0:T(8,128)S(1)} %collective-permute-done.8.refs_1_, ...), custom_call_target="tpu_custom_call" | custom-call | tf_op jit(solution)/shard_map/pallas_call | solution.py:313
  28.6 1.6 %collective-permute-start.13 = (f32[224,128]{1,0:T(8,128)S(1)}, f32[224,128]{1,0:T(8,128)S(1)}, u32[]{:S(2)}, u32[]{:S(2)}) collective-permute-start(f32[224,128]{1,0:T(8,128)S(1)} %get-tuple-element.42), channel_id=1, source_target_pairs={{0,4},{4,0},{8,12},{12,8},{16,20},{20,16},{24,28},{28,24},{1,5},{5... | collective-permute-start | bytes 344072 | tf_op jit(solution)/shard_map/ppermute | solution.py:62
  30.1 1.5 %collective-permute-start.12 = (bf16[192,512]{1,0:T(8,128)(2,1)S(1)}, bf16[192,512]{1,0:T(8,128)(2,1)S(1)}, u32[]{:S(2)}, u32[]{:S(2)}) collective-permute-start(bf16[192,512]{1,0:T(8,128)(2,1)S(1)} %get-tuple-element.41), channel_id=1, source_target_pairs={{0,2},{1,3},{2,0},{3,1},{4,6},{5,7},{6,4},{7,5},{8,10},{9,11},{10,... | collective-permute-start | bytes 589832 | tf_op jit(solution)/shard_map/ppermute | solution.py:62
  31.7 2.5 %collective-permute-done.13 = f32[224,128]{1,0:T(8,128)S(1)} collective-permute-done((f32[224,128]{1,0:T(8,128)S(1)}, f32[224,128]{1,0:T(8,128)S(1)}, u32[]{:S(2)}, u32[]{:S(2)}) %collective-permute-start.13) | collective-permute-done | bytes 114720 | tf_op jit(solution)/shard_map/ppermute | solution.py:62
  34.2 1.6 %collective-permute-start.16 = (bf16[224,128]{1,0:T(8,128)(2,1)S(1)}, bf16[224,128]{1,0:T(8,128)(2,1)S(1)}, u32[]{:S(2)}, u32[]{:S(2)}) collective-permute-start(bf16[224,128]{1,0:T(8,128)(2,1)S(1)} %add_convert_fusion), channel_id=1, source_target_pairs={{0,24},{4,28},{8,16},{12,20},{16,8},{20,12},{24,0},{28,4},{1,25},{... | collective-permute-start | bytes 172040 | tf_op jit(solution)/shard_map/ppermute | solution.py:62
  35.8 2.4 %collective-permute-start.15 = (bf16[224,128]{1,0:T(8,128)(2,1)S(1)}, bf16[224,128]{1,0:T(8,128)(2,1)S(1)}, u32[]{:S(2)}, u32[]{:S(2)}) collective-permute-start(bf16[224,128]{1,0:T(8,128)(2,1)S(1)} %add_convert_fusion), channel_id=1, source_target_pairs={{0,16},{4,20},{8,24},{12,28},{16,0},{20,4},{24,8},{28,12},{1,17},{... | collective-permute-start | bytes 172040 | tf_op jit(solution)/shard_map/ppermute | solution.py:62
  38.3 0.1 collective-permute-done.16
  38.4 2.8 %collective-permute-done.15 = bf16[224,128]{1,0:T(8,128)(2,1)S(1)} collective-permute-done((bf16[224,128]{1,0:T(8,128)(2,1)S(1)}, bf16[224,128]{1,0:T(8,128)(2,1)S(1)}, u32[]{:S(2)}, u32[]{:S(2)}) %collective-permute-start.15) | collective-permute-done | bytes 57376 | tf_op jit(solution)/shard_map/ppermute | solution.py:62
  41.2 1.2 %collective-permute-done.14 = bf16[224,128]{1,0:T(8,128)(2,1)S(1)} collective-permute-done((bf16[224,128]{1,0:T(8,128)(2,1)S(1)}, bf16[224,128]{1,0:T(8,128)(2,1)S(1)}, u32[]{:S(2)}, u32[]{:S(2)}) %collective-permute-start.14) | collective-permute-done | bytes 57376 | tf_op jit(solution)/shard_map/ppermute | solution.py:62
  42.5 1.6 %collective-permute-start.19 = (f32[224,128]{1,0:T(8,128)S(1)}, f32[224,128]{1,0:T(8,128)S(1)}, u32[]{:S(2)}, u32[]{:S(2)}) collective-permute-start(f32[224,128]{1,0:T(8,128)S(1)} %add_add_fusion.refs_0_), channel_id=1, source_target_pairs={{0,2},{1,3},{2,0},{3,1},{4,6},{5,7},{6,4},{7,5},{8,10},{9,11},{10,... | collective-permute-start | bytes 344072 | tf_op jit(solution)/shard_map/ppermute | solution.py:62
  44.1 1.8 %collective-permute-start.21 = (bf16[4,16,512]{2,1,0:T(8,128)(2,1)S(1)}, bf16[4,16,512]{2,1,0:T(8,128)(2,1)S(1)}, u32[]{:S(2)}, u32[]{:S(2)}) collective-permute-start(bf16[4,16,512]{2,1,0:T(8,128)(2,1)S(1)} %pad_maximum_fusion.1), channel_id=1, source_target_pairs={{0,4},{8,12},{16,20},{24,28},{4,0},{12,8},{20,16},{28,24},{1,5},{9... | collective-permute-start | bytes 196616 | tf_op jit(solution)/shard_map/ppermute | solution.py:74
  45.9 2.8 %collective-permute-start.22 = (bf16[4,16,512]{2,1,0:T(8,128)(2,1)S(1)}, bf16[4,16,512]{2,1,0:T(8,128)(2,1)S(1)}, u32[]{:S(2)}, u32[]{:S(2)}) collective-permute-start(bf16[4,16,512]{2,1,0:T(8,128)(2,1)S(1)} %pad_maximum_fusion.2), channel_id=1, source_target_pairs={{4,8},{12,16},{20,24},{8,4},{16,12},{24,20},{5,9},{13,17},{21,25},... | collective-permute-start | bytes 196616 | tf_op jit(solution)/shard_map/ppermute | solution.py:68
  48.7 0.1 collective-permute-start.20
  48.8 0.5 slice_bitcast_fusion.8
  49.3 0.8 %collective-permute-done.20.refs_3_ = f32[224,128]{1,0:T(8,128)S(1)} collective-permute-done((f32[224,128]{1,0:T(8,128)S(1)}, f32[224,128]{1,0:T(8,128)S(1)}, u32[]{:S(2)}, u32[]{:S(2)}) %collective-permute-start.20) | collective-permute-done | bytes 114720 | tf_op jit(solution)/shard_map/ppermute | solution.py:62
  50.1 0.9 %shard_map.122 = (f32[4,128,128]{2,1,0:T(8,128)}, f32[128,384]{1,0:T(8,128)}) custom-call(s32[1]{0:T(128)} %bitcast.place_ref, f32[224,128]{1,0:T(8,128)S(1)} %add_add_fusion.refs_0_, f32[224,128]{1,0:T(8,128)S(1)} %collective-permute-done.18.refs_1_, f32[224,128]{1,0:T(8,128)S(1)} %collective-permute-done.19.refs_2_, ...), custom_call_target="tpu_custom_call" | custom-call | tf_op jit(solution)/shard_map/pallas_call | solution.py:313
  51.0 1.9 %collective-permute-done.22.refs_5_ = bf16[4,16,512]{2,1,0:T(8,128)(2,1)S(1)} collective-permute-done((bf16[4,16,512]{2,1,0:T(8,128)(2,1)S(1)}, bf16[4,16,512]{2,1,0:T(8,128)(2,1)S(1)}, u32[]{:S(2)}, u32[]{:S(2)}) %collective-permute-start.22) | collective-permute-done | bytes 65568 | tf_op jit(solution)/shard_map/ppermute | solution.py:68
  52.9 1.8 %shard_map.123 = f32[64,16,128]{2,1,0:T(8,128)} custom-call(s32[1]{0:T(128)} %bitcast.place_ref, bf16[96,512]{1,0:T(8,128)(2,1)S(1)} %get-tuple-element.39.refs_0_, bf16[96,512]{1,0:T(8,128)(2,1)S(1)} %collective-permute-done.11.refs_1_, bf16[192,512]{1,0:T(8,128)(2,1)S(1)} %collective-permute-done.12.refs_2_, ...), custom_call_target="tpu_custom_call" | custom-call | tf_op jit(solution)/shard_map/pallas_call | solution.py:313
  (48 shorter events, 0.4 us)
Async XLA Ops:
  0.6 5.8 %copy-start = (f32[8,512]{1,0:T(8,128)S(1)}, f32[8,512]{1,0:T(8,128)}, u32[]{:S(2)}) copy-start(f32[8,512]{1,0:T(8,128)} %param.12) | copy-start | bytes 49156
  0.6 11.2 %copy-start.2 = (bf16[128,384]{1,0:T(8,128)(2,1)S(1)}, bf16[128,384]{1,0:T(8,128)(2,1)}, u32[]{:S(2)}) copy-start(bf16[128,384]{1,0:T(8,128)(2,1)} %refs_8_.1) | copy-start | bytes 294916
  0.7 16.0 %copy-start.3 = (f32[128]{0:T(128)S(1)}, f32[128]{0:T(128)}, u32[]{:S(2)}) copy-start(f32[128]{0:T(128)} %param.13) | copy-start | bytes 1540
  1.7 10.3 %collective-permute-start.1 = (bf16[16,64,128]{2,1,0:T(8,128)(2,1)S(1)}, bf16[16,64,128]{2,1,0:T(8,128)(2,1)S(1)}, u32[]{:S(2)}, u32[]{:S(2)}) collective-permute-start(bf16[16,64,128]{2,1,0:T(8,128)(2,1)S(1)} %bitcast.51), channel_id=1, source_target_pairs={{0,2},{1,3},{2,0},{3,1},{4,6},{5,7},{6,4},{7,5},{8,10},{9,11},{10,... | collective-permute-start | bytes 786440 | tf_op jit(solution)/shard_map/ppermute | solution.py:62
  3.3 13.9 %collective-permute-start = (bf16[16,64,128]{2,1,0:T(8,128)(2,1)S(1)}, bf16[16,64,128]{2,1,0:T(8,128)(2,1)S(1)}, u32[]{:S(2)}, u32[]{:S(2)}) collective-permute-start(bf16[16,64,128]{2,1,0:T(8,128)(2,1)S(1)} %bitcast.52), channel_id=1, source_target_pairs={{0,1},{1,0},{2,3},{3,2},{4,5},{5,4},{6,7},{7,6},{8,9},{9,8},{10,11... | collective-permute-start | bytes 786440 | tf_op jit(solution)/shard_map/ppermute | solution.py:62
  3.3 6.9 %collective-permute-start.4 = (bf16[16,16,128]{2,1,0:T(8,128)(2,1)S(1)}, bf16[16,16,128]{2,1,0:T(8,128)(2,1)S(1)}, u32[]{:S(2)}, u32[]{:S(2)}) collective-permute-start(bf16[16,16,128]{2,1,0:T(8,128)(2,1)S(1)} %get-tuple-element.54), channel_id=1, source_target_pairs={{4,8},{12,16},{20,24},{28,0},{8,4},{16,12},{24,20},{0,28},{5,9},{1... | collective-permute-start | bytes 196616 | tf_op jit(solution)/shard_map/ppermute | solution.py:74
  4.8 5.4 %collective-permute-start.3 = (bf16[16,16,128]{2,1,0:T(8,128)(2,1)S(1)}, bf16[16,16,128]{2,1,0:T(8,128)(2,1)S(1)}, u32[]{:S(2)}, u32[]{:S(2)}) collective-permute-start(bf16[16,16,128]{2,1,0:T(8,128)(2,1)S(1)} %get-tuple-element.55), channel_id=1, source_target_pairs={{0,4},{8,12},{16,20},{24,28},{4,0},{12,8},{20,16},{28,24},{1,5},{9... | collective-permute-start | bytes 196616 | tf_op jit(solution)/shard_map/ppermute | solution.py:74
  10.3 6.3 %collective-permute-start.6 = (bf16[41,16,128]{2,1,0:T(8,128)(2,1)S(1)}, bf16[41,16,128]{2,1,0:T(8,128)(2,1)S(1)}, u32[]{:S(2)}, u32[]{:S(2)}) collective-permute-start(bf16[41,16,128]{2,1,0:T(8,128)(2,1)S(1)} %fusion.2.refs_4_), channel_id=1, source_target_pairs={{0,2},{1,3},{2,0},{3,1},{4,6},{5,7},{6,4},{7,5},{8,10},{9,11},{10,... | collective-permute-start | bytes 503816 | tf_op jit(solution)/shard_map/ppermute | solution.py:62
  12.0 6.0 %collective-permute-start.2 = (bf16[16,64,128]{2,1,0:T(8,128)(2,1)S(1)}, bf16[16,64,128]{2,1,0:T(8,128)(2,1)S(1)}, u32[]{:S(2)}, u32[]{:S(2)}) collective-permute-start(bf16[16,64,128]{2,1,0:T(8,128)(2,1)S(1)} %collective-permute-done.1.refs_2_), channel_id=1, source_target_pairs={{0,1},{1,0},{2,3},{3,2},{4,5},{5,4},{6,7},{7,6},{8,9},{9,8},{10,11... | collective-permute-start | bytes 786440 | tf_op jit(solution)/shard_map/ppermute | solution.py:62
  12.1 5.0 %collective-permute-start.5 = (bf16[41,16,128]{2,1,0:T(8,128)(2,1)S(1)}, bf16[41,16,128]{2,1,0:T(8,128)(2,1)S(1)}, u32[]{:S(2)}, u32[]{:S(2)}) collective-permute-start(bf16[41,16,128]{2,1,0:T(8,128)(2,1)S(1)} %fusion.2.refs_4_), channel_id=1, source_target_pairs={{0,1},{1,0},{2,3},{3,2},{4,5},{5,4},{6,7},{7,6},{8,9},{9,8},{10,11... | collective-permute-start | bytes 503816 | tf_op jit(solution)/shard_map/ppermute | solution.py:62
  16.6 1.4 %collective-permute-start.7 = (bf16[41,16,128]{2,1,0:T(8,128)(2,1)S(1)}, bf16[41,16,128]{2,1,0:T(8,128)(2,1)S(1)}, u32[]{:S(2)}, u32[]{:S(2)}) collective-permute-start(bf16[41,16,128]{2,1,0:T(8,128)(2,1)S(1)} %collective-permute-done.6.refs_6_), channel_id=1, source_target_pairs={{0,1},{1,0},{2,3},{3,2},{4,5},{5,4},{6,7},{7,6},{8,9},{9,8},{10,11... | collective-permute-start | bytes 503816 | tf_op jit(solution)/shard_map/ppermute | solution.py:62
  21.6 3.2 %collective-permute-start.10 = (f32[8,512]{1,0:T(8,128)S(1)}, f32[8,512]{1,0:T(8,128)S(1)}, u32[]{:S(2)}, u32[]{:S(2)}) collective-permute-start(f32[8,512]{1,0:T(8,128)S(1)} %get-tuple-element.29.refs_0_), channel_id=1, source_target_pairs={{0,3},{1,2},{2,1},{3,0},{4,7},{5,6},{6,5},{7,4},{8,11},{9,10},{10,... | collective-permute-start | bytes 49160 | tf_op jit(solution)/shard_map/ppermute | solution.py:62
  21.9 3.8 %collective-permute-start.9 = (f32[8,512]{1,0:T(8,128)S(1)}, f32[8,512]{1,0:T(8,128)S(1)}, u32[]{:S(2)}, u32[]{:S(2)}) collective-permute-start(f32[8,512]{1,0:T(8,128)S(1)} %get-tuple-element.29.refs_0_), channel_id=1, source_target_pairs={{0,2},{1,3},{2,0},{3,1},{4,6},{5,7},{6,4},{7,5},{8,10},{9,11},{10,... | collective-permute-start | bytes 49160 | tf_op jit(solution)/shard_map/ppermute | solution.py:62
  23.5 2.2 %collective-permute-start.8 = (f32[8,512]{1,0:T(8,128)S(1)}, f32[8,512]{1,0:T(8,128)S(1)}, u32[]{:S(2)}, u32[]{:S(2)}) collective-permute-start(f32[8,512]{1,0:T(8,128)S(1)} %get-tuple-element.29.refs_0_), channel_id=1, source_target_pairs={{0,1},{1,0},{2,3},{3,2},{4,5},{5,4},{6,7},{7,6},{8,9},{9,8},{10,11... | collective-permute-start | bytes 49160 | tf_op jit(solution)/shard_map/ppermute | solution.py:62
  25.7 27.3 %copy-start.1 = (bf16[4,128,128]{2,1,0:T(8,128)(2,1)S(1)}, bf16[4,128,128]{2,1,0:T(8,128)(2,1)}, u32[]{:S(2)}) copy-start(bf16[4,128,128]{2,1,0:T(8,128)(2,1)} %refs_7_.1) | copy-start | bytes 393220
  28.5 3.2 %collective-permute-start.11 = (bf16[96,512]{1,0:T(8,128)(2,1)S(1)}, bf16[96,512]{1,0:T(8,128)(2,1)S(1)}, u32[]{:S(2)}, u32[]{:S(2)}) collective-permute-start(bf16[96,512]{1,0:T(8,128)(2,1)S(1)} %get-tuple-element.40), channel_id=1, source_target_pairs={{0,1},{1,0},{2,3},{3,2},{4,5},{5,4},{6,7},{7,6},{8,9},{9,8},{10,11... | collective-permute-start | bytes 294920 | tf_op jit(solution)/shard_map/ppermute | solution.py:62
  28.6 5.6 %collective-permute-start.13 = (f32[224,128]{1,0:T(8,128)S(1)}, f32[224,128]{1,0:T(8,128)S(1)}, u32[]{:S(2)}, u32[]{:S(2)}) collective-permute-start(f32[224,128]{1,0:T(8,128)S(1)} %get-tuple-element.42), channel_id=1, source_target_pairs={{0,4},{4,0},{8,12},{12,8},{16,20},{20,16},{24,28},{28,24},{1,5},{5... | collective-permute-start | bytes 344072 | tf_op jit(solution)/shard_map/ppermute | solution.py:62
  30.1 8.1 %collective-permute-start.12 = (bf16[192,512]{1,0:T(8,128)(2,1)S(1)}, bf16[192,512]{1,0:T(8,128)(2,1)S(1)}, u32[]{:S(2)}, u32[]{:S(2)}) collective-permute-start(bf16[192,512]{1,0:T(8,128)(2,1)S(1)} %get-tuple-element.41), channel_id=1, source_target_pairs={{0,2},{1,3},{2,0},{3,1},{4,6},{5,7},{6,4},{7,5},{8,10},{9,11},{10,... | collective-permute-start | bytes 589832 | tf_op jit(solution)/shard_map/ppermute | solution.py:62
  34.2 4.2 %collective-permute-start.16 = (bf16[224,128]{1,0:T(8,128)(2,1)S(1)}, bf16[224,128]{1,0:T(8,128)(2,1)S(1)}, u32[]{:S(2)}, u32[]{:S(2)}) collective-permute-start(bf16[224,128]{1,0:T(8,128)(2,1)S(1)} %add_convert_fusion), channel_id=1, source_target_pairs={{0,24},{4,28},{8,16},{12,20},{16,8},{20,12},{24,0},{28,4},{1,25},{... | collective-permute-start | bytes 172040 | tf_op jit(solution)/shard_map/ppermute | solution.py:62
  35.8 5.4 %collective-permute-start.15 = (bf16[224,128]{1,0:T(8,128)(2,1)S(1)}, bf16[224,128]{1,0:T(8,128)(2,1)S(1)}, u32[]{:S(2)}, u32[]{:S(2)}) collective-permute-start(bf16[224,128]{1,0:T(8,128)(2,1)S(1)} %add_convert_fusion), channel_id=1, source_target_pairs={{0,16},{4,20},{8,24},{12,28},{16,0},{20,4},{24,8},{28,12},{1,17},{... | collective-permute-start | bytes 172040 | tf_op jit(solution)/shard_map/ppermute | solution.py:62
  38.2 4.2 %collective-permute-start.14 = (bf16[224,128]{1,0:T(8,128)(2,1)S(1)}, bf16[224,128]{1,0:T(8,128)(2,1)S(1)}, u32[]{:S(2)}, u32[]{:S(2)}) collective-permute-start(bf16[224,128]{1,0:T(8,128)(2,1)S(1)} %add_convert_fusion), channel_id=1, source_target_pairs={{0,8},{4,12},{8,0},{12,4},{16,24},{20,28},{24,16},{28,20},{1,9},{5... | collective-permute-start | bytes 172040 | tf_op jit(solution)/shard_map/ppermute | solution.py:62
  38.3 4.1 %collective-permute-start.17 = (bf16[192,512]{1,0:T(8,128)(2,1)S(1)}, bf16[192,512]{1,0:T(8,128)(2,1)S(1)}, u32[]{:S(2)}, u32[]{:S(2)}) collective-permute-start(bf16[192,512]{1,0:T(8,128)(2,1)S(1)} %collective-permute-done.12.refs_2_), channel_id=1, source_target_pairs={{0,1},{1,0},{2,3},{3,2},{4,5},{5,4},{6,7},{7,6},{8,9},{9,8},{10,11... | collective-permute-start | bytes 589832 | tf_op jit(solution)/shard_map/ppermute | solution.py:62
  42.5 6.3 %collective-permute-start.19 = (f32[224,128]{1,0:T(8,128)S(1)}, f32[224,128]{1,0:T(8,128)S(1)}, u32[]{:S(2)}, u32[]{:S(2)}) collective-permute-start(f32[224,128]{1,0:T(8,128)S(1)} %add_add_fusion.refs_0_), channel_id=1, source_target_pairs={{0,2},{1,3},{2,0},{3,1},{4,6},{5,7},{6,4},{7,5},{8,10},{9,11},{10,... | collective-permute-start | bytes 344072 | tf_op jit(solution)/shard_map/ppermute | solution.py:62
  44.0 5.3 %collective-permute-start.18 = (f32[224,128]{1,0:T(8,128)S(1)}, f32[224,128]{1,0:T(8,128)S(1)}, u32[]{:S(2)}, u32[]{:S(2)}) collective-permute-start(f32[224,128]{1,0:T(8,128)S(1)} %add_add_fusion.refs_0_), channel_id=1, source_target_pairs={{0,1},{1,0},{2,3},{3,2},{4,5},{5,4},{6,7},{7,6},{8,9},{9,8},{10,11... | collective-permute-start | bytes 344072 | tf_op jit(solution)/shard_map/ppermute | solution.py:62
  44.1 7.0 %collective-permute-start.21 = (bf16[4,16,512]{2,1,0:T(8,128)(2,1)S(1)}, bf16[4,16,512]{2,1,0:T(8,128)(2,1)S(1)}, u32[]{:S(2)}, u32[]{:S(2)}) collective-permute-start(bf16[4,16,512]{2,1,0:T(8,128)(2,1)S(1)} %pad_maximum_fusion.1), channel_id=1, source_target_pairs={{0,4},{8,12},{16,20},{24,28},{4,0},{12,8},{20,16},{28,24},{1,5},{9... | collective-permute-start | bytes 196616 | tf_op jit(solution)/shard_map/ppermute | solution.py:74
  45.9 7.1 %collective-permute-start.22 = (bf16[4,16,512]{2,1,0:T(8,128)(2,1)S(1)}, bf16[4,16,512]{2,1,0:T(8,128)(2,1)S(1)}, u32[]{:S(2)}, u32[]{:S(2)}) collective-permute-start(bf16[4,16,512]{2,1,0:T(8,128)(2,1)S(1)} %pad_maximum_fusion.2), channel_id=1, source_target_pairs={{4,8},{12,16},{20,24},{8,4},{16,12},{24,20},{5,9},{13,17},{21,25},... | collective-permute-start | bytes 196616 | tf_op jit(solution)/shard_map/ppermute | solution.py:68
  48.7 1.4 %collective-permute-start.20 = (f32[224,128]{1,0:T(8,128)S(1)}, f32[224,128]{1,0:T(8,128)S(1)}, u32[]{:S(2)}, u32[]{:S(2)}) collective-permute-start(f32[224,128]{1,0:T(8,128)S(1)} %collective-permute-done.19.refs_2_), channel_id=1, source_target_pairs={{0,1},{1,0},{2,3},{3,2},{4,5},{5,4},{6,7},{7,6},{8,9},{9,8},{10,11... | collective-permute-start | bytes 344072 | tf_op jit(solution)/shard_map/ppermute | solution.py:62

commit v7 on v6

--- a/solution.py
+++ b/solution.py
@@ -62,16 +62,15 @@
     return lax.ppermute(block, axis, [(i, i ^ bit) for i in range(count)])
 
 
-def inner(block, axis):
-    count = lax.axis_size(axis)
-    pairs = [(i, i + 1) for i in range(1, count - 1, 2)]
-    return lax.ppermute(block, axis, pairs + [(j, i) for i, j in pairs])
-
-
-def beside(block, axis, first):
-    count = lax.axis_size(axis)
-    pairs = [(i, (i + 1) % count) for i in range(0 if first else 1, count, 2)]
-    return lax.ppermute(block, axis, pairs + [(j, i) for i, j in pairs])
+def beside(block, first):
+    slabs, plane = lax.axis_size("slab"), lax.axis_size("xy")
+    route = []
+    for slab in range(slabs):
+        other = slab ^ 1 if first else ((slab + 1) ^ 1) - 1
+        for j in range(plane):
+            target = other * plane + j if 0 <= other < slabs else slab * plane + (j ^ 1)
+            route.append((slab * plane + j, target))
+    return lax.ppermute(block, ("slab", "xy"), route)
 
 
 def table(column_ref, k, total):
@@ -361,8 +360,8 @@
 
     own = jnp.transpose(atom_feats, (1, 0, 2))
     last = atoms - face
-    near = beside(lax.dynamic_slice_in_dim(own, (1 - odd) * last, face, 1), "slab", True)
-    far = beside(lax.dynamic_slice_in_dim(own, odd * last, face, 1), "slab", False)
+    near = beside(lax.dynamic_slice_in_dim(own, (1 - odd) * last, face, 1), True)
+    far = beside(lax.dynamic_slice_in_dim(own, odd * last, face, 1), False)
     high = lax.reduce_precision(info, 8, 7)
     middle = lax.reduce_precision(info - high, 8, 7)
     parts = [x.astype(BF16) for x in (high, middle, info - high - middle)]
@@ -458,8 +457,8 @@
     *weight, last_slice = lax.optimization_barrier((*weight, slices[-1]))
     slices = slices[:-1] + [last_slice]
     edges = [s[f + atoms : f + size] for s, f in zip(slices, firsts)]
-    near_grad = beside(jnp.stack([e[:face] for e in edges], axis=0), "slab", True)
-    far_grad = inner(jnp.stack([e[face:] for e in edges], axis=0), "slab")
+    near_grad = beside(jnp.stack([e[:face] for e in edges], axis=0), True)
+    far_grad = beside(jnp.stack([e[face:] for e in edges], axis=0), False)
     near_sum = weight[0].astype(F32) + weight[1].astype(F32)
     weight = near_sum + (weight[2].astype(F32) + weight[3].astype(F32))
     columns = {0: weight}

time: 55 us -> 53.6 us (0.975)
  the two profiles are of different devices: /device:TPU:8 before, /device:TPU:0 now
where the time goes in v7:
time: 53.6 us; the launch traced here: 53.3 us
  starting transfers between devices  20.7 us (39%)
  waiting for transfers between devices  15.9 us (30%)
  Pallas kernels  9.11 us (17%)
  local copies, waits for them, and re-layouts  4.93 us (9%)
  other arithmetic  1.74 us (3%)
  between operations  0.88 us (2%)
    ppermute x19, starting transfers between devices, partner(): return lax.ppermute(block, axis, [(i, i ^ bit) for i in range(count)])  16 us
    ppermute x19, waiting for transfers between devices, partner(): return lax.ppermute(block, axis, [(i, i ^ bit) for i in range(count)])  15.9 us
    pallas_call x4, Pallas kernels, call(): pl.pallas_call(kernel, out_shape=outs, in_specs=[smem if x.shape == (1,)...  9.11 us
    ppermute x4, starting transfers between devices, beside(): return lax.ppermute(block, ('slab', 'xy'), route)  4.71 us
    concatenate x1, local copies, waits for them, and re-layouts, body(): jnp.concatenate([pair_vec.reshape(3 * slots, probes), code.astype(F32), t...  1.44 us
    unnamed x15, local copies, waits for them, and re-layouts  1.4 us
  transfers between devices with their start and end apart: 23, of which 9 were waited for; matrix products, arithmetic and copies ran while one was open for 10% of the time, Pallas kernels for 2%

profile of v7, /device:TPU:0, one launch (start us, length us, event | category | flops | bytes accessed | tf_op | source)
XLA Modules:
  0.0 53.3 jit_solution(6532327637401012649)
XLA Ops:
  0.6 0.0 copy-start
  0.7 1.1 %copy.38 = bf16[64,16,128]{2,0,1:T(8,128)(2,1)S(1)} copy(bf16[64,16,128]{2,1,0:T(8,128)(2,1)} %param.9) | data formatting | bytes 524288 | tf_op args[0]
  1.7 3.0 %collective-permute-start.1 = (bf16[16,64,128]{2,1,0:T(8,128)(2,1)S(1)}, bf16[16,64,128]{2,1,0:T(8,128)(2,1)S(1)}, u32[]{:S(2)}, u32[]{:S(2)}) collective-permute-start(bf16[16,64,128]{2,1,0:T(8,128)(2,1)S(1)} %bitcast.51), channel_id=1, source_target_pairs={{0,2},{1,3},{2,0},{3,1},{4,6},{5,7},{6,4},{7,5},{8,10},{9,11},{10,... | collective-permute-start | bytes 786440 | tf_op jit(solution)/shard_map/ppermute | solution.py:62
  4.8 0.0 collective-permute-start
  4.8 0.6 %collective-permute-start.4 = (bf16[16,16,128]{2,1,0:T(8,128)(2,1)S(1)}, bf16[16,16,128]{2,1,0:T(8,128)(2,1)S(1)}, u32[]{:S(2)}, u32[]{:S(2)}) collective-permute-start(bf16[16,16,128]{2,1,0:T(8,128)(2,1)S(1)} %get-tuple-element.54), channel_id=1, source_target_pairs={{0,1},{1,0},{2,3},{3,2},{4,8},{5,9},{6,10},{7,11},{8,4},{9,5},{10,... | collective-permute-start | bytes 196616 | tf_op jit(solution)/shard_map/ppermute | solution.py:73
  5.4 2.5 %collective-permute-start.3 = (bf16[16,16,128]{2,1,0:T(8,128)(2,1)S(1)}, bf16[16,16,128]{2,1,0:T(8,128)(2,1)S(1)}, u32[]{:S(2)}, u32[]{:S(2)}) collective-permute-start(bf16[16,16,128]{2,1,0:T(8,128)(2,1)S(1)} %get-tuple-element.55), channel_id=1, source_target_pairs={{0,4},{1,5},{2,6},{3,7},{4,0},{5,1},{6,2},{7,3},{8,12},{9,13},{10,... | collective-permute-start | bytes 196616 | tf_op jit(solution)/shard_map/ppermute | solution.py:73
  7.9 0.1 constant_dynamic-slice_fusion.2
  8.0 0.1 reshape.68
  8.1 0.1 fusion
  8.2 0.2 multiply_convert_fusion
  8.3 0.7 %fusion.7 = f32[8,128]{1,0:T(8,128)S(1)} fusion(s32[8,128]{1,0:T(8,128)} %param.15, s32[]{:T(128)S(6)} %add.80, s32[]{:T(128)S(6)} %add.77, s32[]{:T(128)S(6)} %axis_index.25), kind=kLoop, calls=%fused_computation.43 | loop fusion | flops 50176 | bytes 8204 | tf_op jit(solution)/shard_map/convert_element_type | solution.py:359
  9.0 0.7 %convert_bitcast_fusion = f32[1,128]{1,0:T(1,128)S(1)} fusion(s32[128]{0:T(128)} %param.16), kind=kLoop, calls=%fused_computation.57 | loop fusion | flops 128 | bytes 1024 | tf_op jit(solution)/shard_map/broadcast_in_dim | solution.py:357
  9.7 1.4 %concatenate.11 = f32[48,128]{1,0:T(8,128)S(1)} concatenate(f32[24,128]{1,0:T(8,128)} %bitcast.64, f32[8,128]{1,0:T(8,128)S(1)} %fusion.7, f32[1,128]{1,0:T(1,128)S(1)} %convert_bitcast_fusion, f32[1,128]{1,0:T(1,128)} %bitcast.65, f32[14,128]{1,0:T(8,128)S(1)} %broadcast_in_dim.20), dimensions={0} | concatenate | bytes 49152 | tf_op jit(solution)/shard_map/concatenate | solution.py:359
  11.3 0.6 %collective-permute-start.6 = (bf16[41,16,128]{2,1,0:T(8,128)(2,1)S(1)}, bf16[41,16,128]{2,1,0:T(8,128)(2,1)S(1)}, u32[]{:S(2)}, u32[]{:S(2)}) collective-permute-start(bf16[41,16,128]{2,1,0:T(8,128)(2,1)S(1)} %fusion.2.refs_4_), channel_id=1, source_target_pairs={{0,2},{1,3},{2,0},{3,1},{4,6},{5,7},{6,4},{7,5},{8,10},{9,11},{10,... | collective-permute-start | bytes 503816 | tf_op jit(solution)/shard_map/ppermute | solution.py:62
  11.8 1.0 %constant_dynamic-slice_fusion.1 = bf16[4,128,32]{2,1,0:T(8,128)(2,1)S(1)} fusion(bf16[4,128,128]{2,1,0:T(8,128)(2,1)} %refs_7_.1, s32[]{:T(128)S(6)} %select_n.52), kind=kLoop, calls=%fused_computation.52 | loop fusion | bytes 65540 | tf_op jit(solution)/shard_map/dynamic_slice | solution.py:377
  12.9 0.1 copy.25
  13.0 0.1 collective-permute-start.2
  13.1 0.5 collective-permute-start.5
  13.6 3.9 %collective-permute-done.6.refs_6_ = bf16[41,16,128]{2,1,0:T(8,128)(2,1)S(1)} collective-permute-done((bf16[41,16,128]{2,1,0:T(8,128)(2,1)S(1)}, bf16[41,16,128]{2,1,0:T(8,128)(2,1)S(1)}, u32[]{:S(2)}, u32[]{:S(2)}) %collective-permute-start.6) | collective-permute-done | bytes 167968 | tf_op jit(solution)/shard_map/ppermute | solution.py:62
  17.5 0.1 dynamic-slice_bitcast_fusion.2
  17.5 0.1 copy.27.refs_11_.refs_12_
  17.6 0.1 copy.30
  17.7 0.1 copy.36
  17.8 0.2 copy.26.refs_8_
  18.1 0.8 %collective-permute-done.7.refs_7_ = bf16[41,16,128]{2,1,0:T(8,128)(2,1)S(1)} collective-permute-done((bf16[41,16,128]{2,1,0:T(8,128)(2,1)S(1)}, bf16[41,16,128]{2,1,0:T(8,128)(2,1)S(1)}, u32[]{:S(2)}, u32[]{:S(2)}) %collective-permute-start.7) | collective-permute-done | bytes 167968 | tf_op jit(solution)/shard_map/ppermute | solution.py:62
  18.9 3.6 %shard_map.120 = (bf16[16,384,128]{2,1,0:T(8,128)(2,1)S(1)}, f32[512,384]{1,0:T(8,128)S(1)}, f32[96,384]{1,0:T(8,128)S(1)}, f32[32,512]{1,0:T(8,128)S(1)}, f32[8...) custom-call(s32[1]{0:T(128)} %bitcast.place_ref, ...), custom_call_target="tpu_custom_call" | custom-call | tf_op jit(solution)/shard_map/pallas_call | solution.py:312
  22.5 0.3 collective-permute-start.10
  22.8 1.5 %collective-permute-start.9 = (f32[8,512]{1,0:T(8,128)S(1)}, f32[8,512]{1,0:T(8,128)S(1)}, u32[]{:S(2)}, u32[]{:S(2)}) collective-permute-start(f32[8,512]{1,0:T(8,128)S(1)} %get-tuple-element.29.refs_0_), channel_id=1, source_target_pairs={{0,2},{1,3},{2,0},{3,1},{4,6},{5,7},{6,4},{7,5},{8,10},{9,11},{10,... | collective-permute-start | bytes 49160 | tf_op jit(solution)/shard_map/ppermute | solution.py:62
  24.3 0.1 collective-permute-start.8
  24.4 1.3 %collective-permute-done.10.refs_3_ = f32[8,512]{1,0:T(8,128)S(1)} collective-permute-done((f32[8,512]{1,0:T(8,128)S(1)}, f32[8,512]{1,0:T(8,128)S(1)}, u32[]{:S(2)}, u32[]{:S(2)}) %collective-permute-start.10) | collective-permute-done | bytes 16416 | tf_op jit(solution)/shard_map/ppermute | solution.py:62
  25.7 0.8 %collective-permute-done.9.refs_2_ = f32[8,512]{1,0:T(8,128)S(1)} collective-permute-done((f32[8,512]{1,0:T(8,128)S(1)}, f32[8,512]{1,0:T(8,128)S(1)}, u32[]{:S(2)}, u32[]{:S(2)}) %collective-permute-start.9) | collective-permute-done | bytes 16416 | tf_op jit(solution)/shard_map/ppermute | solution.py:62
  26.5 2.8 %shard_map.121 = (f32[224,128]{1,0:T(8,128)S(1)}, f32[8,128]{1,0:T(8,128)S(1)}, bf16[96,512]{1,0:T(8,128)(2,1)S(1)}, bf16[96,512]{1,0:T(8,128)(2,1)S(1)}, bf16[192,512]{1,0:T(8,128)(2,1)S(1)}) custom-call(f32[8,512]{1,0:T(8,128)S(1)} %get-tuple-element.29.refs_0_, f32[8,512]{1,0:T(8,128)S(1)} %collective-permute-done.8.refs_1_, ...), custom_call_target="tpu_custom_call" | custom-call | tf_op jit(solution)/shard_map/pallas_call | solution.py:312
  29.4 0.1 collective-permute-start.11
  29.5 2.1 %collective-permute-start.13 = (f32[224,128]{1,0:T(8,128)S(1)}, f32[224,128]{1,0:T(8,128)S(1)}, u32[]{:S(2)}, u32[]{:S(2)}) collective-permute-start(f32[224,128]{1,0:T(8,128)S(1)} %get-tuple-element.42), channel_id=1, source_target_pairs={{0,4},{4,0},{8,12},{12,8},{16,20},{20,16},{24,28},{28,24},{1,5},{5... | collective-permute-start | bytes 344072 | tf_op jit(solution)/shard_map/ppermute | solution.py:62
  31.6 1.5 %collective-permute-start.12 = (bf16[192,512]{1,0:T(8,128)(2,1)S(1)}, bf16[192,512]{1,0:T(8,128)(2,1)S(1)}, u32[]{:S(2)}, u32[]{:S(2)}) collective-permute-start(bf16[192,512]{1,0:T(8,128)(2,1)S(1)} %get-tuple-element.41), channel_id=1, source_target_pairs={{0,2},{1,3},{2,0},{3,1},{4,6},{5,7},{6,4},{7,5},{8,10},{9,11},{10,... | collective-permute-start | bytes 589832 | tf_op jit(solution)/shard_map/ppermute | solution.py:62
  33.1 2.2 %collective-permute-done.13 = f32[224,128]{1,0:T(8,128)S(1)} collective-permute-done((f32[224,128]{1,0:T(8,128)S(1)}, f32[224,128]{1,0:T(8,128)S(1)}, u32[]{:S(2)}, u32[]{:S(2)}) %collective-permute-start.13) | collective-permute-done | bytes 114720 | tf_op jit(solution)/shard_map/ppermute | solution.py:62
  35.3 3.9 %collective-permute-start.16 = (bf16[224,128]{1,0:T(8,128)(2,1)S(1)}, bf16[224,128]{1,0:T(8,128)(2,1)S(1)}, u32[]{:S(2)}, u32[]{:S(2)}) collective-permute-start(bf16[224,128]{1,0:T(8,128)(2,1)S(1)} %add_convert_fusion), channel_id=1, source_target_pairs={{0,24},{4,28},{8,16},{12,20},{16,8},{20,12},{24,0},{28,4},{1,25},{... | collective-permute-start | bytes 172040 | tf_op jit(solution)/shard_map/ppermute | solution.py:62
  39.3 0.6 %collective-permute-start.14 = (bf16[224,128]{1,0:T(8,128)(2,1)S(1)}, bf16[224,128]{1,0:T(8,128)(2,1)S(1)}, u32[]{:S(2)}, u32[]{:S(2)}) collective-permute-start(bf16[224,128]{1,0:T(8,128)(2,1)S(1)} %add_convert_fusion), channel_id=1, source_target_pairs={{0,8},{4,12},{8,0},{12,4},{16,24},{20,28},{24,16},{28,20},{1,9},{5... | collective-permute-start | bytes 172040 | tf_op jit(solution)/shard_map/ppermute | solution.py:62
  39.9 1.9 %collective-permute-done.16 = bf16[224,128]{1,0:T(8,128)(2,1)S(1)} collective-permute-done((bf16[224,128]{1,0:T(8,128)(2,1)S(1)}, bf16[224,128]{1,0:T(8,128)(2,1)S(1)}, u32[]{:S(2)}, u32[]{:S(2)}) %collective-permute-start.16) | collective-permute-done | bytes 57376 | tf_op jit(solution)/shard_map/ppermute | solution.py:62
  41.8 2.6 %collective-permute-done.15 = bf16[224,128]{1,0:T(8,128)(2,1)S(1)} collective-permute-done((bf16[224,128]{1,0:T(8,128)(2,1)S(1)}, bf16[224,128]{1,0:T(8,128)(2,1)S(1)}, u32[]{:S(2)}, u32[]{:S(2)}) %collective-permute-start.15) | collective-permute-done | bytes 57376 | tf_op jit(solution)/shard_map/ppermute | solution.py:62
  44.4 1.6 %collective-permute-start.19 = (f32[224,128]{1,0:T(8,128)S(1)}, f32[224,128]{1,0:T(8,128)S(1)}, u32[]{:S(2)}, u32[]{:S(2)}) collective-permute-start(f32[224,128]{1,0:T(8,128)S(1)} %add_add_fusion.refs_0_), channel_id=1, source_target_pairs={{0,2},{1,3},{2,0},{3,1},{4,6},{5,7},{6,4},{7,5},{8,10},{9,11},{10,... | collective-permute-start | bytes 344072 | tf_op jit(solution)/shard_map/ppermute | solution.py:62
  46.0 1.3 %collective-permute-start.21 = (bf16[4,16,512]{2,1,0:T(8,128)(2,1)S(1)}, bf16[4,16,512]{2,1,0:T(8,128)(2,1)S(1)}, u32[]{:S(2)}, u32[]{:S(2)}) collective-permute-start(bf16[4,16,512]{2,1,0:T(8,128)(2,1)S(1)} %pad_maximum_fusion.1), channel_id=1, source_target_pairs={{0,4},{1,5},{2,6},{3,7},{4,0},{5,1},{6,2},{7,3},{8,12},{9,13},{10,... | collective-permute-start | bytes 196616 | tf_op jit(solution)/shard_map/ppermute | solution.py:73
  47.3 0.3 collective-permute-start.22
  47.6 1.6 %collective-permute-done.19.refs_2_ = f32[224,128]{1,0:T(8,128)S(1)} collective-permute-done((f32[224,128]{1,0:T(8,128)S(1)}, f32[224,128]{1,0:T(8,128)S(1)}, u32[]{:S(2)}, u32[]{:S(2)}) %collective-permute-start.19) | collective-permute-done | bytes 114720 | tf_op jit(solution)/shard_map/ppermute | solution.py:62
  49.3 0.5 slice_bitcast_fusion.8
  49.8 0.8 %collective-permute-done.20.refs_3_ = f32[224,128]{1,0:T(8,128)S(1)} collective-permute-done((f32[224,128]{1,0:T(8,128)S(1)}, f32[224,128]{1,0:T(8,128)S(1)}, u32[]{:S(2)}, u32[]{:S(2)}) %collective-permute-start.20) | collective-permute-done | bytes 114720 | tf_op jit(solution)/shard_map/ppermute | solution.py:62
  50.6 0.9 %shard_map.122 = (f32[4,128,128]{2,1,0:T(8,128)}, f32[128,384]{1,0:T(8,128)}) custom-call(s32[1]{0:T(128)} %bitcast.place_ref, f32[224,128]{1,0:T(8,128)S(1)} %add_add_fusion.refs_0_, f32[224,128]{1,0:T(8,128)S(1)} %collective-permute-done.18.refs_1_, f32[224,128]{1,0:T(8,128)S(1)} %collective-permute-done.19.refs_2_, ...), custom_call_target="tpu_custom_call" | custom-call | tf_op jit(solution)/shard_map/pallas_call | solution.py:312
  51.5 1.8 %shard_map.123 = f32[64,16,128]{2,1,0:T(8,128)} custom-call(s32[1]{0:T(128)} %bitcast.place_ref, bf16[96,512]{1,0:T(8,128)(2,1)S(1)} %get-tuple-element.39.refs_0_, bf16[96,512]{1,0:T(8,128)(2,1)S(1)} %collective-permute-done.11.refs_1_, bf16[192,512]{1,0:T(8,128)(2,1)S(1)} %collective-permute-done.12.refs_2_, ...), custom_call_target="tpu_custom_call" | custom-call | tf_op jit(solution)/shard_map/pallas_call | solution.py:312
  (48 shorter events, 0.3 us)
Async XLA Ops:
  0.6 7.3 %copy-start = (f32[8,512]{1,0:T(8,128)S(1)}, f32[8,512]{1,0:T(8,128)}, u32[]{:S(2)}) copy-start(f32[8,512]{1,0:T(8,128)} %param.12) | copy-start | bytes 49156
  0.6 12.2 %copy-start.2 = (bf16[128,384]{1,0:T(8,128)(2,1)S(1)}, bf16[128,384]{1,0:T(8,128)(2,1)}, u32[]{:S(2)}) copy-start(bf16[128,384]{1,0:T(8,128)(2,1)} %refs_8_.1) | copy-start | bytes 294916
  0.7 16.8 %copy-start.3 = (f32[128]{0:T(128)S(1)}, f32[128]{0:T(128)}, u32[]{:S(2)}) copy-start(f32[128]{0:T(128)} %param.13) | copy-start | bytes 1540
  1.7 11.2 %collective-permute-start.1 = (bf16[16,64,128]{2,1,0:T(8,128)(2,1)S(1)}, bf16[16,64,128]{2,1,0:T(8,128)(2,1)S(1)}, u32[]{:S(2)}, u32[]{:S(2)}) collective-permute-start(bf16[16,64,128]{2,1,0:T(8,128)(2,1)S(1)} %bitcast.51), channel_id=1, source_target_pairs={{0,2},{1,3},{2,0},{3,1},{4,6},{5,7},{6,4},{7,5},{8,10},{9,11},{10,... | collective-permute-start | bytes 786440 | tf_op jit(solution)/shard_map/ppermute | solution.py:62
  4.8 13.3 %collective-permute-start = (bf16[16,64,128]{2,1,0:T(8,128)(2,1)S(1)}, bf16[16,64,128]{2,1,0:T(8,128)(2,1)S(1)}, u32[]{:S(2)}, u32[]{:S(2)}) collective-permute-start(bf16[16,64,128]{2,1,0:T(8,128)(2,1)S(1)} %bitcast.52), channel_id=1, source_target_pairs={{0,1},{1,0},{2,3},{3,2},{4,5},{5,4},{6,7},{7,6},{8,9},{9,8},{10,11... | collective-permute-start | bytes 786440 | tf_op jit(solution)/shard_map/ppermute | solution.py:62
  4.8 6.4 %collective-permute-start.4 = (bf16[16,16,128]{2,1,0:T(8,128)(2,1)S(1)}, bf16[16,16,128]{2,1,0:T(8,128)(2,1)S(1)}, u32[]{:S(2)}, u32[]{:S(2)}) collective-permute-start(bf16[16,16,128]{2,1,0:T(8,128)(2,1)S(1)} %get-tuple-element.54), channel_id=1, source_target_pairs={{0,1},{1,0},{2,3},{3,2},{4,8},{5,9},{6,10},{7,11},{8,4},{9,5},{10,... | collective-permute-start | bytes 196616 | tf_op jit(solution)/shard_map/ppermute | solution.py:73
  5.4 5.8 %collective-permute-start.3 = (bf16[16,16,128]{2,1,0:T(8,128)(2,1)S(1)}, bf16[16,16,128]{2,1,0:T(8,128)(2,1)S(1)}, u32[]{:S(2)}, u32[]{:S(2)}) collective-permute-start(bf16[16,16,128]{2,1,0:T(8,128)(2,1)S(1)} %get-tuple-element.55), channel_id=1, source_target_pairs={{0,4},{1,5},{2,6},{3,7},{4,0},{5,1},{6,2},{7,3},{8,12},{9,13},{10,... | collective-permute-start | bytes 196616 | tf_op jit(solution)/shard_map/ppermute | solution.py:73
  11.3 6.2 %collective-permute-start.6 = (bf16[41,16,128]{2,1,0:T(8,128)(2,1)S(1)}, bf16[41,16,128]{2,1,0:T(8,128)(2,1)S(1)}, u32[]{:S(2)}, u32[]{:S(2)}) collective-permute-start(bf16[41,16,128]{2,1,0:T(8,128)(2,1)S(1)} %fusion.2.refs_4_), channel_id=1, source_target_pairs={{0,2},{1,3},{2,0},{3,1},{4,6},{5,7},{6,4},{7,5},{8,10},{9,11},{10,... | collective-permute-start | bytes 503816 | tf_op jit(solution)/shard_map/ppermute | solution.py:62
  13.0 5.9 %collective-permute-start.2 = (bf16[16,64,128]{2,1,0:T(8,128)(2,1)S(1)}, bf16[16,64,128]{2,1,0:T(8,128)(2,1)S(1)}, u32[]{:S(2)}, u32[]{:S(2)}) collective-permute-start(bf16[16,64,128]{2,1,0:T(8,128)(2,1)S(1)} %collective-permute-done.1.refs_2_), channel_id=1, source_target_pairs={{0,1},{1,0},{2,3},{3,2},{4,5},{5,4},{6,7},{7,6},{8,9},{9,8},{10,11... | collective-permute-start | bytes 786440 | tf_op jit(solution)/shard_map/ppermute | solution.py:62
  13.1 4.9 %collective-permute-start.5 = (bf16[41,16,128]{2,1,0:T(8,128)(2,1)S(1)}, bf16[41,16,128]{2,1,0:T(8,128)(2,1)S(1)}, u32[]{:S(2)}, u32[]{:S(2)}) collective-permute-start(bf16[41,16,128]{2,1,0:T(8,128)(2,1)S(1)} %fusion.2.refs_4_), channel_id=1, source_target_pairs={{0,1},{1,0},{2,3},{3,2},{4,5},{5,4},{6,7},{7,6},{8,9},{9,8},{10,11... | collective-permute-start | bytes 503816 | tf_op jit(solution)/shard_map/ppermute | solution.py:62
  17.5 1.4 %collective-permute-start.7 = (bf16[41,16,128]{2,1,0:T(8,128)(2,1)S(1)}, bf16[41,16,128]{2,1,0:T(8,128)(2,1)S(1)}, u32[]{:S(2)}, u32[]{:S(2)}) collective-permute-start(bf16[41,16,128]{2,1,0:T(8,128)(2,1)S(1)} %collective-permute-done.6.refs_6_), channel_id=1, source_target_pairs={{0,1},{1,0},{2,3},{3,2},{4,5},{5,4},{6,7},{7,6},{8,9},{9,8},{10,11... | collective-permute-start | bytes 503816 | tf_op jit(solution)/shard_map/ppermute | solution.py:62
  22.5 3.2 %collective-permute-start.10 = (f32[8,512]{1,0:T(8,128)S(1)}, f32[8,512]{1,0:T(8,128)S(1)}, u32[]{:S(2)}, u32[]{:S(2)}) collective-permute-start(f32[8,512]{1,0:T(8,128)S(1)} %get-tuple-element.29.refs_0_), channel_id=1, source_target_pairs={{0,3},{1,2},{2,1},{3,0},{4,7},{5,6},{6,5},{7,4},{8,11},{9,10},{10,... | collective-permute-start | bytes 49160 | tf_op jit(solution)/shard_map/ppermute | solution.py:62
  22.8 3.8 %collective-permute-start.9 = (f32[8,512]{1,0:T(8,128)S(1)}, f32[8,512]{1,0:T(8,128)S(1)}, u32[]{:S(2)}, u32[]{:S(2)}) collective-permute-start(f32[8,512]{1,0:T(8,128)S(1)} %get-tuple-element.29.refs_0_), channel_id=1, source_target_pairs={{0,2},{1,3},{2,0},{3,1},{4,6},{5,7},{6,4},{7,5},{8,10},{9,11},{10,... | collective-permute-start | bytes 49160 | tf_op jit(solution)/shard_map/ppermute | solution.py:62
  24.3 2.2 %collective-permute-start.8 = (f32[8,512]{1,0:T(8,128)S(1)}, f32[8,512]{1,0:T(8,128)S(1)}, u32[]{:S(2)}, u32[]{:S(2)}) collective-permute-start(f32[8,512]{1,0:T(8,128)S(1)} %get-tuple-element.29.refs_0_), channel_id=1, source_target_pairs={{0,1},{1,0},{2,3},{3,2},{4,5},{5,4},{6,7},{7,6},{8,9},{9,8},{10,11... | collective-permute-start | bytes 49160 | tf_op jit(solution)/shard_map/ppermute | solution.py:62
  26.5 25.0 %copy-start.1 = (bf16[4,128,128]{2,1,0:T(8,128)(2,1)S(1)}, bf16[4,128,128]{2,1,0:T(8,128)(2,1)}, u32[]{:S(2)}) copy-start(bf16[4,128,128]{2,1,0:T(8,128)(2,1)} %refs_7_.1) | copy-start | bytes 393220
  29.4 3.7 %collective-permute-start.11 = (bf16[96,512]{1,0:T(8,128)(2,1)S(1)}, bf16[96,512]{1,0:T(8,128)(2,1)S(1)}, u32[]{:S(2)}, u32[]{:S(2)}) collective-permute-start(bf16[96,512]{1,0:T(8,128)(2,1)S(1)} %get-tuple-element.40), channel_id=1, source_target_pairs={{0,1},{1,0},{2,3},{3,2},{4,5},{5,4},{6,7},{7,6},{8,9},{9,8},{10,11... | collective-permute-start | bytes 294920 | tf_op jit(solution)/shard_map/ppermute | solution.py:62
  29.5 5.9 %collective-permute-start.13 = (f32[224,128]{1,0:T(8,128)S(1)}, f32[224,128]{1,0:T(8,128)S(1)}, u32[]{:S(2)}, u32[]{:S(2)}) collective-permute-start(f32[224,128]{1,0:T(8,128)S(1)} %get-tuple-element.42), channel_id=1, source_target_pairs={{0,4},{4,0},{8,12},{12,8},{16,20},{20,16},{24,28},{28,24},{1,5},{5... | collective-permute-start | bytes 344072 | tf_op jit(solution)/shard_map/ppermute | solution.py:62
  31.6 8.3 %collective-permute-start.12 = (bf16[192,512]{1,0:T(8,128)(2,1)S(1)}, bf16[192,512]{1,0:T(8,128)(2,1)S(1)}, u32[]{:S(2)}, u32[]{:S(2)}) collective-permute-start(bf16[192,512]{1,0:T(8,128)(2,1)S(1)} %get-tuple-element.41), channel_id=1, source_target_pairs={{0,2},{1,3},{2,0},{3,1},{4,6},{5,7},{6,4},{7,5},{8,10},{9,11},{10,... | collective-permute-start | bytes 589832 | tf_op jit(solution)/shard_map/ppermute | solution.py:62
  35.3 6.5 %collective-permute-start.16 = (bf16[224,128]{1,0:T(8,128)(2,1)S(1)}, bf16[224,128]{1,0:T(8,128)(2,1)S(1)}, u32[]{:S(2)}, u32[]{:S(2)}) collective-permute-start(bf16[224,128]{1,0:T(8,128)(2,1)S(1)} %add_convert_fusion), channel_id=1, source_target_pairs={{0,24},{4,28},{8,16},{12,20},{16,8},{20,12},{24,0},{28,4},{1,25},{... | collective-permute-start | bytes 172040 | tf_op jit(solution)/shard_map/ppermute | solution.py:62
  39.3 5.1 %collective-permute-start.15 = (bf16[224,128]{1,0:T(8,128)(2,1)S(1)}, bf16[224,128]{1,0:T(8,128)(2,1)S(1)}, u32[]{:S(2)}, u32[]{:S(2)}) collective-permute-start(bf16[224,128]{1,0:T(8,128)(2,1)S(1)} %add_convert_fusion), channel_id=1, source_target_pairs={{0,16},{4,20},{8,24},{12,28},{16,0},{20,4},{24,8},{28,12},{1,17},{... | collective-permute-start | bytes 172040 | tf_op jit(solution)/shard_map/ppermute | solution.py:62
  39.3 5.1 %collective-permute-start.14 = (bf16[224,128]{1,0:T(8,128)(2,1)S(1)}, bf16[224,128]{1,0:T(8,128)(2,1)S(1)}, u32[]{:S(2)}, u32[]{:S(2)}) collective-permute-start(bf16[224,128]{1,0:T(8,128)(2,1)S(1)} %add_convert_fusion), channel_id=1, source_target_pairs={{0,8},{4,12},{8,0},{12,4},{16,24},{20,28},{24,16},{28,20},{1,9},{5... | collective-permute-start | bytes 172040 | tf_op jit(solution)/shard_map/ppermute | solution.py:62
  39.9 4.4 %collective-permute-start.17 = (bf16[192,512]{1,0:T(8,128)(2,1)S(1)}, bf16[192,512]{1,0:T(8,128)(2,1)S(1)}, u32[]{:S(2)}, u32[]{:S(2)}) collective-permute-start(bf16[192,512]{1,0:T(8,128)(2,1)S(1)} %collective-permute-done.12.refs_2_), channel_id=1, source_target_pairs={{0,1},{1,0},{2,3},{3,2},{4,5},{5,4},{6,7},{7,6},{8,9},{9,8},{10,11... | collective-permute-start | bytes 589832 | tf_op jit(solution)/shard_map/ppermute | solution.py:62
  44.4 4.9 %collective-permute-start.19 = (f32[224,128]{1,0:T(8,128)S(1)}, f32[224,128]{1,0:T(8,128)S(1)}, u32[]{:S(2)}, u32[]{:S(2)}) collective-permute-start(f32[224,128]{1,0:T(8,128)S(1)} %add_add_fusion.refs_0_), channel_id=1, source_target_pairs={{0,2},{1,3},{2,0},{3,1},{4,6},{5,7},{6,4},{7,5},{8,10},{9,11},{10,... | collective-permute-start | bytes 344072 | tf_op jit(solution)/shard_map/ppermute | solution.py:62
  46.0 3.8 %collective-permute-start.18 = (f32[224,128]{1,0:T(8,128)S(1)}, f32[224,128]{1,0:T(8,128)S(1)}, u32[]{:S(2)}, u32[]{:S(2)}) collective-permute-start(f32[224,128]{1,0:T(8,128)S(1)} %add_add_fusion.refs_0_), channel_id=1, source_target_pairs={{0,1},{1,0},{2,3},{3,2},{4,5},{5,4},{6,7},{7,6},{8,9},{9,8},{10,11... | collective-permute-start | bytes 344072 | tf_op jit(solution)/shard_map/ppermute | solution.py:62
  46.0 5.5 %collective-permute-start.21 = (bf16[4,16,512]{2,1,0:T(8,128)(2,1)S(1)}, bf16[4,16,512]{2,1,0:T(8,128)(2,1)S(1)}, u32[]{:S(2)}, u32[]{:S(2)}) collective-permute-start(bf16[4,16,512]{2,1,0:T(8,128)(2,1)S(1)} %pad_maximum_fusion.1), channel_id=1, source_target_pairs={{0,4},{1,5},{2,6},{3,7},{4,0},{5,1},{6,2},{7,3},{8,12},{9,13},{10,... | collective-permute-start | bytes 196616 | tf_op jit(solution)/shard_map/ppermute | solution.py:73
  47.3 4.2 %collective-permute-start.22 = (bf16[4,16,512]{2,1,0:T(8,128)(2,1)S(1)}, bf16[4,16,512]{2,1,0:T(8,128)(2,1)S(1)}, u32[]{:S(2)}, u32[]{:S(2)}) collective-permute-start(bf16[4,16,512]{2,1,0:T(8,128)(2,1)S(1)} %pad_maximum_fusion.2), channel_id=1, source_target_pairs={{0,1},{1,0},{2,3},{3,2},{4,8},{5,9},{6,10},{7,11},{8,4},{9,5},{10,... | collective-permute-start | bytes 196616 | tf_op jit(solution)/shard_map/ppermute | solution.py:73
  49.3 1.3 %collective-permute-start.20 = (f32[224,128]{1,0:T(8,128)S(1)}, f32[224,128]{1,0:T(8,128)S(1)}, u32[]{:S(2)}, u32[]{:S(2)}) collective-permute-start(f32[224,128]{1,0:T(8,128)S(1)} %collective-permute-done.19.refs_2_), channel_id=1, source_target_pairs={{0,1},{1,0},{2,3},{3,2},{4,5},{5,4},{6,7},{7,6},{8,9},{9,8},{10,11... | collective-permute-start | bytes 344072 | tf_op jit(solution)/shard_map/ppermute | solution.py:62

commit v8 on v7

--- a/solution.py
+++ b/solution.py
@@ -151,7 +151,7 @@
             message = message + inner * coef_ref[at : at + part, :]
     msg_ref[...] = message
     partial = jnp.sum(message * jax.nn.sigmoid(message) * out_w_ref[...], axis=0, keepdims=True)
-    dens_ref[...] = jnp.broadcast_to(partial, dens_ref.shape)
+    dens_ref[...] = partial
 
 
 def backward_kernel(slots, plane, scale, probes_dev, *refs):
@@ -397,7 +397,7 @@
             jax.ShapeDtypeStruct((harm_count * part, total), F32),
             jax.ShapeDtypeStruct((3 * part, total), F32),
             jax.ShapeDtypeStruct((part, lanes), F32),
-            jax.ShapeDtypeStruct((8, lanes), F32),
+            jax.ShapeDtypeStruct((1, lanes), F32),
             jax.ShapeDtypeStruct((slots * 4 * part, lanes), F32),
             jax.ShapeDtypeStruct((harm_count * slots, lanes), F32),
             jax.ShapeDtypeStruct((slots, lanes), jnp.int32),

time: 53.6 us -> 53.4 us (level)
  no operation moved by 1% of the time
where the time goes in v8:
time: 53.4 us; the launch traced here: 53.1 us
  starting transfers between devices  20.7 us (39%)
  waiting for transfers between devices  15.8 us (30%)
  Pallas kernels  9.07 us (17%)
  local copies, waits for them, and re-layouts  4.93 us (9%)
  other arithmetic  1.74 us (3%)
  between operations  0.88 us (2%)
    ppermute x19, starting transfers between devices, partner(): return lax.ppermute(block, axis, [(i, i ^ bit) for i in range(count)])  16 us
    ppermute x19, waiting for transfers between devices, partner(): return lax.ppermute(block, axis, [(i, i ^ bit) for i in range(count)])  15.8 us
    pallas_call x4, Pallas kernels, call(): pl.pallas_call(kernel, out_shape=outs, in_specs=[smem if x.shape == (1,)...  9.07 us
    ppermute x4, starting transfers between devices, beside(): return lax.ppermute(block, ('slab', 'xy'), route)  4.71 us
    concatenate x1, local copies, waits for them, and re-layouts, body(): jnp.concatenate([pair_vec.reshape(3 * slots, probes), code.astype(F32), t...  1.44 us
    unnamed x15, local copies, waits for them, and re-layouts  1.4 us
  transfers between devices with their start and end apart: 23, of which 9 were waited for; matrix products, arithmetic and copies ran while one was open for 10% of the time, Pallas kernels for 2%

profile of v8, /device:TPU:0, one launch (start us, length us, event | category | flops | bytes accessed | tf_op | source)
XLA Modules:
  0.0 53.1 jit_solution(11279942651510156369)
XLA Ops:
  0.6 0.0 copy-start
  0.7 1.1 %copy.38 = bf16[64,16,128]{2,0,1:T(8,128)(2,1)S(1)} copy(bf16[64,16,128]{2,1,0:T(8,128)(2,1)} %param.9) | data formatting | bytes 524288 | tf_op args[0]
  1.7 3.0 %collective-permute-start.1 = (bf16[16,64,128]{2,1,0:T(8,128)(2,1)S(1)}, bf16[16,64,128]{2,1,0:T(8,128)(2,1)S(1)}, u32[]{:S(2)}, u32[]{:S(2)}) collective-permute-start(bf16[16,64,128]{2,1,0:T(8,128)(2,1)S(1)} %bitcast.51), channel_id=1, source_target_pairs={{0,2},{1,3},{2,0},{3,1},{4,6},{5,7},{6,4},{7,5},{8,10},{9,11},{10,... | collective-permute-start | bytes 786440 | tf_op jit(solution)/shard_map/ppermute | solution.py:62
  4.8 0.6 %collective-permute-start.4 = (bf16[16,16,128]{2,1,0:T(8,128)(2,1)S(1)}, bf16[16,16,128]{2,1,0:T(8,128)(2,1)S(1)}, u32[]{:S(2)}, u32[]{:S(2)}) collective-permute-start(bf16[16,16,128]{2,1,0:T(8,128)(2,1)S(1)} %get-tuple-element.54), channel_id=1, source_target_pairs={{0,1},{1,0},{2,3},{3,2},{4,8},{5,9},{6,10},{7,11},{8,4},{9,5},{10,... | collective-permute-start | bytes 196616 | tf_op jit(solution)/shard_map/ppermute | solution.py:73
  5.4 2.5 %collective-permute-start.3 = (bf16[16,16,128]{2,1,0:T(8,128)(2,1)S(1)}, bf16[16,16,128]{2,1,0:T(8,128)(2,1)S(1)}, u32[]{:S(2)}, u32[]{:S(2)}) collective-permute-start(bf16[16,16,128]{2,1,0:T(8,128)(2,1)S(1)} %get-tuple-element.55), channel_id=1, source_target_pairs={{0,4},{1,5},{2,6},{3,7},{4,0},{5,1},{6,2},{7,3},{8,12},{9,13},{10,... | collective-permute-start | bytes 196616 | tf_op jit(solution)/shard_map/ppermute | solution.py:73
  7.9 0.1 constant_dynamic-slice_fusion.2
  8.0 0.1 reshape.68
  8.1 0.1 fusion
  8.2 0.2 multiply_convert_fusion
  8.3 0.7 %fusion.7 = f32[8,128]{1,0:T(8,128)S(1)} fusion(s32[8,128]{1,0:T(8,128)} %param.15, s32[]{:T(128)S(6)} %add.80, s32[]{:T(128)S(6)} %add.77, s32[]{:T(128)S(6)} %axis_index.25), kind=kLoop, calls=%fused_computation.43 | loop fusion | flops 50176 | bytes 8204 | tf_op jit(solution)/shard_map/convert_element_type | solution.py:359
  9.0 0.7 %convert_bitcast_fusion = f32[1,128]{1,0:T(1,128)S(1)} fusion(s32[128]{0:T(128)} %param.16), kind=kLoop, calls=%fused_computation.57 | loop fusion | flops 128 | bytes 1024 | tf_op jit(solution)/shard_map/broadcast_in_dim | solution.py:357
  9.7 1.4 %concatenate.11 = f32[48,128]{1,0:T(8,128)S(1)} concatenate(f32[24,128]{1,0:T(8,128)} %bitcast.64, f32[8,128]{1,0:T(8,128)S(1)} %fusion.7, f32[1,128]{1,0:T(1,128)S(1)} %convert_bitcast_fusion, f32[1,128]{1,0:T(1,128)} %bitcast.65, f32[14,128]{1,0:T(8,128)S(1)} %broadcast_in_dim.20), dimensions={0} | concatenate | bytes 49152 | tf_op jit(solution)/shard_map/concatenate | solution.py:359
  11.2 0.0 collective-permute-done.3
  11.3 0.6 %collective-permute-start.6 = (bf16[41,16,128]{2,1,0:T(8,128)(2,1)S(1)}, bf16[41,16,128]{2,1,0:T(8,128)(2,1)S(1)}, u32[]{:S(2)}, u32[]{:S(2)}) collective-permute-start(bf16[41,16,128]{2,1,0:T(8,128)(2,1)S(1)} %fusion.2.refs_4_), channel_id=1, source_target_pairs={{0,2},{1,3},{2,0},{3,1},{4,6},{5,7},{6,4},{7,5},{8,10},{9,11},{10,... | collective-permute-start | bytes 503816 | tf_op jit(solution)/shard_map/ppermute | solution.py:62
  11.8 1.0 %constant_dynamic-slice_fusion.1 = bf16[4,128,32]{2,1,0:T(8,128)(2,1)S(1)} fusion(bf16[4,128,128]{2,1,0:T(8,128)(2,1)} %refs_7_.1, s32[]{:T(128)S(6)} %select_n.52), kind=kLoop, calls=%fused_computation.52 | loop fusion | bytes 65540 | tf_op jit(solution)/shard_map/dynamic_slice | solution.py:377
  12.9 0.1 copy.25
  13.0 0.1 collective-permute-start.2
  13.1 0.5 collective-permute-start.5
  13.6 3.9 %collective-permute-done.6.refs_6_ = bf16[41,16,128]{2,1,0:T(8,128)(2,1)S(1)} collective-permute-done((bf16[41,16,128]{2,1,0:T(8,128)(2,1)S(1)}, bf16[41,16,128]{2,1,0:T(8,128)(2,1)S(1)}, u32[]{:S(2)}, u32[]{:S(2)}) %collective-permute-start.6) | collective-permute-done | bytes 167968 | tf_op jit(solution)/shard_map/ppermute | solution.py:62
  17.5 0.1 dynamic-slice_bitcast_fusion.2
  17.5 0.1 copy.27.refs_11_.refs_12_
  17.6 0.1 copy.30
  17.7 0.1 copy.36
  17.8 0.2 copy.26.refs_8_
  18.1 0.8 %collective-permute-done.7.refs_7_ = bf16[41,16,128]{2,1,0:T(8,128)(2,1)S(1)} collective-permute-done((bf16[41,16,128]{2,1,0:T(8,128)(2,1)S(1)}, bf16[41,16,128]{2,1,0:T(8,128)(2,1)S(1)}, u32[]{:S(2)}, u32[]{:S(2)}) %collective-permute-start.7) | collective-permute-done | bytes 167968 | tf_op jit(solution)/shard_map/ppermute | solution.py:62
  18.9 3.6 %shard_map.120 = (bf16[16,384,128]{2,1,0:T(8,128)(2,1)S(1)}, f32[512,384]{1,0:T(8,128)S(1)}, f32[96,384]{1,0:T(8,128)S(1)}, f32[32,512]{1,0:T(8,128)S(1)}, f32[1...) custom-call(s32[1]{0:T(128)} %bitcast.place_ref, ...), custom_call_target="tpu_custom_call" | custom-call | tf_op jit(solution)/shard_map/pallas_call | solution.py:312
  22.4 0.3 collective-permute-start.10
  22.8 1.5 %collective-permute-start.9 = (f32[1,512]{1,0:T(1,128)S(1)}, f32[1,512]{1,0:T(1,128)S(1)}, u32[]{:S(2)}, u32[]{:S(2)}) collective-permute-start(f32[1,512]{1,0:T(1,128)S(1)} %get-tuple-element.29.refs_0_), channel_id=1, source_target_pairs={{0,2},{1,3},{2,0},{3,1},{4,6},{5,7},{6,4},{7,5},{8,10},{9,11},{10,... | collective-permute-start | bytes 6152 | tf_op jit(solution)/shard_map/ppermute | solution.py:62
  24.3 0.1 collective-permute-start.8
  24.4 1.1 %collective-permute-done.10.refs_3_ = f32[1,512]{1,0:T(1,128)S(1)} collective-permute-done((f32[1,512]{1,0:T(1,128)S(1)}, f32[1,512]{1,0:T(1,128)S(1)}, u32[]{:S(2)}, u32[]{:S(2)}) %collective-permute-start.10) | collective-permute-done | bytes 2080 | tf_op jit(solution)/shard_map/ppermute | solution.py:62
  25.5 0.8 %collective-permute-done.9.refs_2_ = f32[1,512]{1,0:T(1,128)S(1)} collective-permute-done((f32[1,512]{1,0:T(1,128)S(1)}, f32[1,512]{1,0:T(1,128)S(1)}, u32[]{:S(2)}, u32[]{:S(2)}) %collective-permute-start.9) | collective-permute-done | bytes 2080 | tf_op jit(solution)/shard_map/ppermute | solution.py:62
  26.4 2.8 %shard_map.121 = (f32[224,128]{1,0:T(8,128)S(1)}, f32[8,128]{1,0:T(8,128)S(1)}, bf16[96,512]{1,0:T(8,128)(2,1)S(1)}, bf16[96,512]{1,0:T(8,128)(2,1)S(1)}, bf16[192,512]{1,0:T(8,128)(2,1)S(1)}) custom-call(f32[1,512]{1,0:T(1,128)S(1)} %get-tuple-element.29.refs_0_, f32[1,512]{1,0:T(1,128)S(1)} %collective-permute-done.8.refs_1_, ...), custom_call_target="tpu_custom_call" | custom-call | tf_op jit(solution)/shard_map/pallas_call | solution.py:312
  29.2 0.1 collective-permute-start.11
  29.3 2.1 %collective-permute-start.13 = (f32[224,128]{1,0:T(8,128)S(1)}, f32[224,128]{1,0:T(8,128)S(1)}, u32[]{:S(2)}, u32[]{:S(2)}) collective-permute-start(f32[224,128]{1,0:T(8,128)S(1)} %get-tuple-element.42), channel_id=1, source_target_pairs={{0,4},{4,0},{8,12},{12,8},{16,20},{20,16},{24,28},{28,24},{1,5},{5... | collective-permute-start | bytes 344072 | tf_op jit(solution)/shard_map/ppermute | solution.py:62
  31.4 1.5 %collective-permute-start.12 = (bf16[192,512]{1,0:T(8,128)(2,1)S(1)}, bf16[192,512]{1,0:T(8,128)(2,1)S(1)}, u32[]{:S(2)}, u32[]{:S(2)}) collective-permute-start(bf16[192,512]{1,0:T(8,128)(2,1)S(1)} %get-tuple-element.41), channel_id=1, source_target_pairs={{0,2},{1,3},{2,0},{3,1},{4,6},{5,7},{6,4},{7,5},{8,10},{9,11},{10,... | collective-permute-start | bytes 589832 | tf_op jit(solution)/shard_map/ppermute | solution.py:62
  32.9 2.2 %collective-permute-done.13 = f32[224,128]{1,0:T(8,128)S(1)} collective-permute-done((f32[224,128]{1,0:T(8,128)S(1)}, f32[224,128]{1,0:T(8,128)S(1)}, u32[]{:S(2)}, u32[]{:S(2)}) %collective-permute-start.13) | collective-permute-done | bytes 114720 | tf_op jit(solution)/shard_map/ppermute | solution.py:62
  35.1 3.9 %collective-permute-start.16 = (bf16[224,128]{1,0:T(8,128)(2,1)S(1)}, bf16[224,128]{1,0:T(8,128)(2,1)S(1)}, u32[]{:S(2)}, u32[]{:S(2)}) collective-permute-start(bf16[224,128]{1,0:T(8,128)(2,1)S(1)} %add_convert_fusion), channel_id=1, source_target_pairs={{0,24},{4,28},{8,16},{12,20},{16,8},{20,12},{24,0},{28,4},{1,25},{... | collective-permute-start | bytes 172040 | tf_op jit(solution)/shard_map/ppermute | solution.py:62
  39.1 0.6 %collective-permute-start.14 = (bf16[224,128]{1,0:T(8,128)(2,1)S(1)}, bf16[224,128]{1,0:T(8,128)(2,1)S(1)}, u32[]{:S(2)}, u32[]{:S(2)}) collective-permute-start(bf16[224,128]{1,0:T(8,128)(2,1)S(1)} %add_convert_fusion), channel_id=1, source_target_pairs={{0,8},{4,12},{8,0},{12,4},{16,24},{20,28},{24,16},{28,20},{1,9},{5... | collective-permute-start | bytes 172040 | tf_op jit(solution)/shard_map/ppermute | solution.py:62
  39.7 1.9 %collective-permute-done.16 = bf16[224,128]{1,0:T(8,128)(2,1)S(1)} collective-permute-done((bf16[224,128]{1,0:T(8,128)(2,1)S(1)}, bf16[224,128]{1,0:T(8,128)(2,1)S(1)}, u32[]{:S(2)}, u32[]{:S(2)}) %collective-permute-start.16) | collective-permute-done | bytes 57376 | tf_op jit(solution)/shard_map/ppermute | solution.py:62
  41.6 2.6 %collective-permute-done.15 = bf16[224,128]{1,0:T(8,128)(2,1)S(1)} collective-permute-done((bf16[224,128]{1,0:T(8,128)(2,1)S(1)}, bf16[224,128]{1,0:T(8,128)(2,1)S(1)}, u32[]{:S(2)}, u32[]{:S(2)}) %collective-permute-start.15) | collective-permute-done | bytes 57376 | tf_op jit(solution)/shard_map/ppermute | solution.py:62
  44.2 1.6 %collective-permute-start.19 = (f32[224,128]{1,0:T(8,128)S(1)}, f32[224,128]{1,0:T(8,128)S(1)}, u32[]{:S(2)}, u32[]{:S(2)}) collective-permute-start(f32[224,128]{1,0:T(8,128)S(1)} %add_add_fusion.refs_0_), channel_id=1, source_target_pairs={{0,2},{1,3},{2,0},{3,1},{4,6},{5,7},{6,4},{7,5},{8,10},{9,11},{10,... | collective-permute-start | bytes 344072 | tf_op jit(solution)/shard_map/ppermute | solution.py:62
  45.8 1.3 %collective-permute-start.21 = (bf16[4,16,512]{2,1,0:T(8,128)(2,1)S(1)}, bf16[4,16,512]{2,1,0:T(8,128)(2,1)S(1)}, u32[]{:S(2)}, u32[]{:S(2)}) collective-permute-start(bf16[4,16,512]{2,1,0:T(8,128)(2,1)S(1)} %pad_maximum_fusion.1), channel_id=1, source_target_pairs={{0,4},{1,5},{2,6},{3,7},{4,0},{5,1},{6,2},{7,3},{8,12},{9,13},{10,... | collective-permute-start | bytes 196616 | tf_op jit(solution)/shard_map/ppermute | solution.py:73
  47.1 0.3 collective-permute-start.22
  47.4 1.6 %collective-permute-done.19.refs_2_ = f32[224,128]{1,0:T(8,128)S(1)} collective-permute-done((f32[224,128]{1,0:T(8,128)S(1)}, f32[224,128]{1,0:T(8,128)S(1)}, u32[]{:S(2)}, u32[]{:S(2)}) %collective-permute-start.19) | collective-permute-done | bytes 114720 | tf_op jit(solution)/shard_map/ppermute | solution.py:62
  49.1 0.5 slice_bitcast_fusion.8
  49.6 0.8 %collective-permute-done.20.refs_3_ = f32[224,128]{1,0:T(8,128)S(1)} collective-permute-done((f32[224,128]{1,0:T(8,128)S(1)}, f32[224,128]{1,0:T(8,128)S(1)}, u32[]{:S(2)}, u32[]{:S(2)}) %collective-permute-start.20) | collective-permute-done | bytes 114720 | tf_op jit(solution)/shard_map/ppermute | solution.py:62
  50.4 0.9 %shard_map.122 = (f32[4,128,128]{2,1,0:T(8,128)}, f32[128,384]{1,0:T(8,128)}) custom-call(s32[1]{0:T(128)} %bitcast.place_ref, f32[224,128]{1,0:T(8,128)S(1)} %add_add_fusion.refs_0_, f32[224,128]{1,0:T(8,128)S(1)} %collective-permute-done.18.refs_1_, f32[224,128]{1,0:T(8,128)S(1)} %collective-permute-done.19.refs_2_, ...), custom_call_target="tpu_custom_call" | custom-call | tf_op jit(solution)/shard_map/pallas_call | solution.py:312
  51.3 1.8 %shard_map.123 = f32[64,16,128]{2,1,0:T(8,128)} custom-call(s32[1]{0:T(128)} %bitcast.place_ref, bf16[96,512]{1,0:T(8,128)(2,1)S(1)} %get-tuple-element.39.refs_0_, bf16[96,512]{1,0:T(8,128)(2,1)S(1)} %collective-permute-done.11.refs_1_, bf16[192,512]{1,0:T(8,128)(2,1)S(1)} %collective-permute-done.12.refs_2_, ...), custom_call_target="tpu_custom_call" | custom-call | tf_op jit(solution)/shard_map/pallas_call | solution.py:312
  (48 shorter events, 0.3 us)
Async XLA Ops:
  0.6 7.3 %copy-start = (f32[8,512]{1,0:T(8,128)S(1)}, f32[8,512]{1,0:T(8,128)}, u32[]{:S(2)}) copy-start(f32[8,512]{1,0:T(8,128)} %param.12) | copy-start | bytes 49156
  0.6 12.2 %copy-start.2 = (bf16[128,384]{1,0:T(8,128)(2,1)S(1)}, bf16[128,384]{1,0:T(8,128)(2,1)}, u32[]{:S(2)}) copy-start(bf16[128,384]{1,0:T(8,128)(2,1)} %refs_8_.1) | copy-start | bytes 294916
  0.7 16.8 %copy-start.3 = (f32[128]{0:T(128)S(1)}, f32[128]{0:T(128)}, u32[]{:S(2)}) copy-start(f32[128]{0:T(128)} %param.13) | copy-start | bytes 1540
  1.7 11.2 %collective-permute-start.1 = (bf16[16,64,128]{2,1,0:T(8,128)(2,1)S(1)}, bf16[16,64,128]{2,1,0:T(8,128)(2,1)S(1)}, u32[]{:S(2)}, u32[]{:S(2)}) collective-permute-start(bf16[16,64,128]{2,1,0:T(8,128)(2,1)S(1)} %bitcast.51), channel_id=1, source_target_pairs={{0,2},{1,3},{2,0},{3,1},{4,6},{5,7},{6,4},{7,5},{8,10},{9,11},{10,... | collective-permute-start | bytes 786440 | tf_op jit(solution)/shard_map/ppermute | solution.py:62
  4.8 13.3 %collective-permute-start = (bf16[16,64,128]{2,1,0:T(8,128)(2,1)S(1)}, bf16[16,64,128]{2,1,0:T(8,128)(2,1)S(1)}, u32[]{:S(2)}, u32[]{:S(2)}) collective-permute-start(bf16[16,64,128]{2,1,0:T(8,128)(2,1)S(1)} %bitcast.52), channel_id=1, source_target_pairs={{0,1},{1,0},{2,3},{3,2},{4,5},{5,4},{6,7},{7,6},{8,9},{9,8},{10,11... | collective-permute-start | bytes 786440 | tf_op jit(solution)/shard_map/ppermute | solution.py:62
  4.8 6.4 %collective-permute-start.4 = (bf16[16,16,128]{2,1,0:T(8,128)(2,1)S(1)}, bf16[16,16,128]{2,1,0:T(8,128)(2,1)S(1)}, u32[]{:S(2)}, u32[]{:S(2)}) collective-permute-start(bf16[16,16,128]{2,1,0:T(8,128)(2,1)S(1)} %get-tuple-element.54), channel_id=1, source_target_pairs={{0,1},{1,0},{2,3},{3,2},{4,8},{5,9},{6,10},{7,11},{8,4},{9,5},{10,... | collective-permute-start | bytes 196616 | tf_op jit(solution)/shard_map/ppermute | solution.py:73
  5.4 5.8 %collective-permute-start.3 = (bf16[16,16,128]{2,1,0:T(8,128)(2,1)S(1)}, bf16[16,16,128]{2,1,0:T(8,128)(2,1)S(1)}, u32[]{:S(2)}, u32[]{:S(2)}) collective-permute-start(bf16[16,16,128]{2,1,0:T(8,128)(2,1)S(1)} %get-tuple-element.55), channel_id=1, source_target_pairs={{0,4},{1,5},{2,6},{3,7},{4,0},{5,1},{6,2},{7,3},{8,12},{9,13},{10,... | collective-permute-start | bytes 196616 | tf_op jit(solution)/shard_map/ppermute | solution.py:73
  11.3 6.2 %collective-permute-start.6 = (bf16[41,16,128]{2,1,0:T(8,128)(2,1)S(1)}, bf16[41,16,128]{2,1,0:T(8,128)(2,1)S(1)}, u32[]{:S(2)}, u32[]{:S(2)}) collective-permute-start(bf16[41,16,128]{2,1,0:T(8,128)(2,1)S(1)} %fusion.2.refs_4_), channel_id=1, source_target_pairs={{0,2},{1,3},{2,0},{3,1},{4,6},{5,7},{6,4},{7,5},{8,10},{9,11},{10,... | collective-permute-start | bytes 503816 | tf_op jit(solution)/shard_map/ppermute | solution.py:62
  13.0 5.9 %collective-permute-start.2 = (bf16[16,64,128]{2,1,0:T(8,128)(2,1)S(1)}, bf16[16,64,128]{2,1,0:T(8,128)(2,1)S(1)}, u32[]{:S(2)}, u32[]{:S(2)}) collective-permute-start(bf16[16,64,128]{2,1,0:T(8,128)(2,1)S(1)} %collective-permute-done.1.refs_2_), channel_id=1, source_target_pairs={{0,1},{1,0},{2,3},{3,2},{4,5},{5,4},{6,7},{7,6},{8,9},{9,8},{10,11... | collective-permute-start | bytes 786440 | tf_op jit(solution)/shard_map/ppermute | solution.py:62
  13.1 4.9 %collective-permute-start.5 = (bf16[41,16,128]{2,1,0:T(8,128)(2,1)S(1)}, bf16[41,16,128]{2,1,0:T(8,128)(2,1)S(1)}, u32[]{:S(2)}, u32[]{:S(2)}) collective-permute-start(bf16[41,16,128]{2,1,0:T(8,128)(2,1)S(1)} %fusion.2.refs_4_), channel_id=1, source_target_pairs={{0,1},{1,0},{2,3},{3,2},{4,5},{5,4},{6,7},{7,6},{8,9},{9,8},{10,11... | collective-permute-start | bytes 503816 | tf_op jit(solution)/shard_map/ppermute | solution.py:62
  17.5 1.4 %collective-permute-start.7 = (bf16[41,16,128]{2,1,0:T(8,128)(2,1)S(1)}, bf16[41,16,128]{2,1,0:T(8,128)(2,1)S(1)}, u32[]{:S(2)}, u32[]{:S(2)}) collective-permute-start(bf16[41,16,128]{2,1,0:T(8,128)(2,1)S(1)} %collective-permute-done.6.refs_6_), channel_id=1, source_target_pairs={{0,1},{1,0},{2,3},{3,2},{4,5},{5,4},{6,7},{7,6},{8,9},{9,8},{10,11... | collective-permute-start | bytes 503816 | tf_op jit(solution)/shard_map/ppermute | solution.py:62
  22.4 3.1 %collective-permute-start.10 = (f32[1,512]{1,0:T(1,128)S(1)}, f32[1,512]{1,0:T(1,128)S(1)}, u32[]{:S(2)}, u32[]{:S(2)}) collective-permute-start(f32[1,512]{1,0:T(1,128)S(1)} %get-tuple-element.29.refs_0_), channel_id=1, source_target_pairs={{0,3},{1,2},{2,1},{3,0},{4,7},{5,6},{6,5},{7,4},{8,11},{9,10},{10,... | collective-permute-start | bytes 6152 | tf_op jit(solution)/shard_map/ppermute | solution.py:62
  22.8 3.6 %collective-permute-start.9 = (f32[1,512]{1,0:T(1,128)S(1)}, f32[1,512]{1,0:T(1,128)S(1)}, u32[]{:S(2)}, u32[]{:S(2)}) collective-permute-start(f32[1,512]{1,0:T(1,128)S(1)} %get-tuple-element.29.refs_0_), channel_id=1, source_target_pairs={{0,2},{1,3},{2,0},{3,1},{4,6},{5,7},{6,4},{7,5},{8,10},{9,11},{10,... | collective-permute-start | bytes 6152 | tf_op jit(solution)/shard_map/ppermute | solution.py:62
  24.3 2.1 %collective-permute-start.8 = (f32[1,512]{1,0:T(1,128)S(1)}, f32[1,512]{1,0:T(1,128)S(1)}, u32[]{:S(2)}, u32[]{:S(2)}) collective-permute-start(f32[1,512]{1,0:T(1,128)S(1)} %get-tuple-element.29.refs_0_), channel_id=1, source_target_pairs={{0,1},{1,0},{2,3},{3,2},{4,5},{5,4},{6,7},{7,6},{8,9},{9,8},{10,11... | collective-permute-start | bytes 6152 | tf_op jit(solution)/shard_map/ppermute | solution.py:62
  26.4 25.0 %copy-start.1 = (bf16[4,128,128]{2,1,0:T(8,128)(2,1)S(1)}, bf16[4,128,128]{2,1,0:T(8,128)(2,1)}, u32[]{:S(2)}) copy-start(bf16[4,128,128]{2,1,0:T(8,128)(2,1)} %refs_7_.1) | copy-start | bytes 393220
  29.2 3.7 %collective-permute-start.11 = (bf16[96,512]{1,0:T(8,128)(2,1)S(1)}, bf16[96,512]{1,0:T(8,128)(2,1)S(1)}, u32[]{:S(2)}, u32[]{:S(2)}) collective-permute-start(bf16[96,512]{1,0:T(8,128)(2,1)S(1)} %get-tuple-element.40), channel_id=1, source_target_pairs={{0,1},{1,0},{2,3},{3,2},{4,5},{5,4},{6,7},{7,6},{8,9},{9,8},{10,11... | collective-permute-start | bytes 294920 | tf_op jit(solution)/shard_map/ppermute | solution.py:62
  29.3 5.9 %collective-permute-start.13 = (f32[224,128]{1,0:T(8,128)S(1)}, f32[224,128]{1,0:T(8,128)S(1)}, u32[]{:S(2)}, u32[]{:S(2)}) collective-permute-start(f32[224,128]{1,0:T(8,128)S(1)} %get-tuple-element.42), channel_id=1, source_target_pairs={{0,4},{4,0},{8,12},{12,8},{16,20},{20,16},{24,28},{28,24},{1,5},{5... | collective-permute-start | bytes 344072 | tf_op jit(solution)/shard_map/ppermute | solution.py:62
  31.4 8.3 %collective-permute-start.12 = (bf16[192,512]{1,0:T(8,128)(2,1)S(1)}, bf16[192,512]{1,0:T(8,128)(2,1)S(1)}, u32[]{:S(2)}, u32[]{:S(2)}) collective-permute-start(bf16[192,512]{1,0:T(8,128)(2,1)S(1)} %get-tuple-element.41), channel_id=1, source_target_pairs={{0,2},{1,3},{2,0},{3,1},{4,6},{5,7},{6,4},{7,5},{8,10},{9,11},{10,... | collective-permute-start | bytes 589832 | tf_op jit(solution)/shard_map/ppermute | solution.py:62
  35.1 6.5 %collective-permute-start.16 = (bf16[224,128]{1,0:T(8,128)(2,1)S(1)}, bf16[224,128]{1,0:T(8,128)(2,1)S(1)}, u32[]{:S(2)}, u32[]{:S(2)}) collective-permute-start(bf16[224,128]{1,0:T(8,128)(2,1)S(1)} %add_convert_fusion), channel_id=1, source_target_pairs={{0,24},{4,28},{8,16},{12,20},{16,8},{20,12},{24,0},{28,4},{1,25},{... | collective-permute-start | bytes 172040 | tf_op jit(solution)/shard_map/ppermute | solution.py:62
  39.1 5.1 %collective-permute-start.15 = (bf16[224,128]{1,0:T(8,128)(2,1)S(1)}, bf16[224,128]{1,0:T(8,128)(2,1)S(1)}, u32[]{:S(2)}, u32[]{:S(2)}) collective-permute-start(bf16[224,128]{1,0:T(8,128)(2,1)S(1)} %add_convert_fusion), channel_id=1, source_target_pairs={{0,16},{4,20},{8,24},{12,28},{16,0},{20,4},{24,8},{28,12},{1,17},{... | collective-permute-start | bytes 172040 | tf_op jit(solution)/shard_map/ppermute | solution.py:62
  39.1 5.1 %collective-permute-start.14 = (bf16[224,128]{1,0:T(8,128)(2,1)S(1)}, bf16[224,128]{1,0:T(8,128)(2,1)S(1)}, u32[]{:S(2)}, u32[]{:S(2)}) collective-permute-start(bf16[224,128]{1,0:T(8,128)(2,1)S(1)} %add_convert_fusion), channel_id=1, source_target_pairs={{0,8},{4,12},{8,0},{12,4},{16,24},{20,28},{24,16},{28,20},{1,9},{5... | collective-permute-start | bytes 172040 | tf_op jit(solution)/shard_map/ppermute | solution.py:62
  39.7 4.4 %collective-permute-start.17 = (bf16[192,512]{1,0:T(8,128)(2,1)S(1)}, bf16[192,512]{1,0:T(8,128)(2,1)S(1)}, u32[]{:S(2)}, u32[]{:S(2)}) collective-permute-start(bf16[192,512]{1,0:T(8,128)(2,1)S(1)} %collective-permute-done.12.refs_2_), channel_id=1, source_target_pairs={{0,1},{1,0},{2,3},{3,2},{4,5},{5,4},{6,7},{7,6},{8,9},{9,8},{10,11... | collective-permute-start | bytes 589832 | tf_op jit(solution)/shard_map/ppermute | solution.py:62
  44.2 4.9 %collective-permute-start.19 = (f32[224,128]{1,0:T(8,128)S(1)}, f32[224,128]{1,0:T(8,128)S(1)}, u32[]{:S(2)}, u32[]{:S(2)}) collective-permute-start(f32[224,128]{1,0:T(8,128)S(1)} %add_add_fusion.refs_0_), channel_id=1, source_target_pairs={{0,2},{1,3},{2,0},{3,1},{4,6},{5,7},{6,4},{7,5},{8,10},{9,11},{10,... | collective-permute-start | bytes 344072 | tf_op jit(solution)/shard_map/ppermute | solution.py:62
  45.8 3.8 %collective-permute-start.18 = (f32[224,128]{1,0:T(8,128)S(1)}, f32[224,128]{1,0:T(8,128)S(1)}, u32[]{:S(2)}, u32[]{:S(2)}) collective-permute-start(f32[224,128]{1,0:T(8,128)S(1)} %add_add_fusion.refs_0_), channel_id=1, source_target_pairs={{0,1},{1,0},{2,3},{3,2},{4,5},{5,4},{6,7},{7,6},{8,9},{9,8},{10,11... | collective-permute-start | bytes 344072 | tf_op jit(solution)/shard_map/ppermute | solution.py:62
  45.8 5.5 %collective-permute-start.21 = (bf16[4,16,512]{2,1,0:T(8,128)(2,1)S(1)}, bf16[4,16,512]{2,1,0:T(8,128)(2,1)S(1)}, u32[]{:S(2)}, u32[]{:S(2)}) collective-permute-start(bf16[4,16,512]{2,1,0:T(8,128)(2,1)S(1)} %pad_maximum_fusion.1), channel_id=1, source_target_pairs={{0,4},{1,5},{2,6},{3,7},{4,0},{5,1},{6,2},{7,3},{8,12},{9,13},{10,... | collective-permute-start | bytes 196616 | tf_op jit(solution)/shard_map/ppermute | solution.py:73
  47.1 4.2 %collective-permute-start.22 = (bf16[4,16,512]{2,1,0:T(8,128)(2,1)S(1)}, bf16[4,16,512]{2,1,0:T(8,128)(2,1)S(1)}, u32[]{:S(2)}, u32[]{:S(2)}) collective-permute-start(bf16[4,16,512]{2,1,0:T(8,128)(2,1)S(1)} %pad_maximum_fusion.2), channel_id=1, source_target_pairs={{0,1},{1,0},{2,3},{3,2},{4,8},{5,9},{6,10},{7,11},{8,4},{9,5},{10,... | collective-permute-start | bytes 196616 | tf_op jit(solution)/shard_map/ppermute | solution.py:73
  49.1 1.3 %collective-permute-start.20 = (f32[224,128]{1,0:T(8,128)S(1)}, f32[224,128]{1,0:T(8,128)S(1)}, u32[]{:S(2)}, u32[]{:S(2)}) collective-permute-start(f32[224,128]{1,0:T(8,128)S(1)} %collective-permute-done.19.refs_2_), channel_id=1, source_target_pairs={{0,1},{1,0},{2,3},{3,2},{4,5},{5,4},{6,7},{7,6},{8,9},{9,8},{10,11... | collective-permute-start | bytes 344072 | tf_op jit(solution)/shard_map/ppermute | solution.py:62
